TPU v7x, 32 devices: a whole 2x2x4 slice. The times are simulated.
32 devices in a mesh: dp: 16 (over z, y, x), mp: 2 (over core).
Axes of the slice: x: 2, y: 2, z: 4, core: 2. Of those that a mesh axis runs over, the one named last changes fastest.
Arguments:
- tokens: bfloat16 [2, 16, 512, 768], P(None, 'dp'), may hold values from -6 to 6
- pair_lengths: int32 [2, 16], P(None, 'dp'), may hold values from 128 to 512, as said below
- query_ids: int32 [2, 16], replicated, may hold values from 0 to 3, as said below
- distance_bucket: int32 [1023], replicated, may hold values from 0 to 31, as said below
- step_count: int32 [], replicated, may hold values from 1 to 20
- heads_in: float32 [768, 3, 768], P('dp', None, 'mp'), may hold values from -0.21650635 to 0.21650635
- heads_out: float32 [768, 768], P('dp', 'mp'), may hold values from -0.875 to 0.875
- hidden_in: float32 [768, 3072], P('dp', 'mp'), may hold values from -0.21875 to 0.21875
- hidden_out: float32 [768, 3072], P('dp', 'mp'), may hold values from -0.15625 to 0.15625
- gains: float32 [768, 3], P('dp'), may hold values from 0.3 to 2.5
- tied_rows: float32 [768, 2], P('dp'), may hold values from -6 to 6
- bias_table: float32 [32, 12], P(None, 'mp'), may hold values from -6 to 6
- first_heads_in: float32 [768, 3, 768], P('dp', None, 'mp'), may hold values from -5.722046e-06 to 5.722046e-06
- first_heads_out: float32 [768, 768], P('dp', 'mp'), may hold values from -5.722046e-06 to 5.722046e-06
- first_hidden_in: float32 [768, 3072], P('dp', 'mp'), may hold values from -5.722046e-06 to 5.722046e-06
- first_hidden_out: float32 [768, 3072], P('dp', 'mp'), may hold values from -5.722046e-06 to 5.722046e-06
- first_gains: float32 [768, 3], P('dp'), may hold values from -5.722046e-06 to 5.722046e-06
- first_tied: float32 [768, 2], P('dp'), may hold values from -5.722046e-06 to 5.722046e-06
- first_table: float32 [32, 12], P(None, 'mp'), may hold values from -5.722046e-06 to 5.722046e-06
- second_heads_in: float32 [768, 3, 768], P('dp', None, 'mp'), may hold values from 7.060041e-15 to 5.6480326e-14
- second_heads_out: float32 [768, 768], P('dp', 'mp'), may hold values from 7.060041e-15 to 5.6480326e-14
- second_hidden_in: float32 [768, 3072], P('dp', 'mp'), may hold values from 7.060041e-15 to 5.6480326e-14
- second_hidden_out: float32 [768, 3072], P('dp', 'mp'), may hold values from 7.060041e-15 to 5.6480326e-14
- second_gains: float32 [768, 3], P('dp'), may hold values from 7.060041e-15 to 5.6480326e-14
- second_tied: float32 [768, 2], P('dp'), may hold values from 7.060041e-15 to 5.6480326e-14
- second_table: float32 [32, 12], P(None, 'mp'), may hold values from 7.060041e-15 to 5.6480326e-14
Outputs:
- gradient_norm: float32 [], replicated
- token_gradient: float32 [2, 16, 512, 768], P(None, 'dp')
- next_heads_in: float32 [768, 3, 768], P('dp', None, 'mp')
- next_heads_out: float32 [768, 768], P('dp', 'mp')
- next_hidden_in: float32 [768, 3072], P('dp', 'mp')
- next_hidden_out: float32 [768, 3072], P('dp', 'mp')
- next_gains: float32 [768, 3], P('dp')
- next_tied: float32 [768, 2], P('dp')
- next_table: float32 [32, 12], P(None, 'mp')
- next_first_heads_in: float32 [768, 3, 768], P('dp', None, 'mp')
- next_first_heads_out: float32 [768, 768], P('dp', 'mp')
- next_first_hidden_in: float32 [768, 3072], P('dp', 'mp')
- next_first_hidden_out: float32 [768, 3072], P('dp', 'mp')
- next_first_gains: float32 [768, 3], P('dp')
- next_first_tied: float32 [768, 2], P('dp')
- next_first_table: float32 [32, 12], P(None, 'mp')
- next_second_heads_in: float32 [768, 3, 768], P('dp', None, 'mp')
- next_second_heads_out: float32 [768, 768], P('dp', 'mp')
- next_second_hidden_in: float32 [768, 3072], P('dp', 'mp')
- next_second_hidden_out: float32 [768, 3072], P('dp', 'mp')
- next_second_gains: float32 [768, 3], P('dp')
- next_second_tied: float32 [768, 2], P('dp')
- next_second_table: float32 [32, 12], P(None, 'mp')
Inputs may be any that keep to these rules, and one draw needn't show every extreme that they name: `pair_lengths`: pair 0 of each micro-batch uses all 512 positions of its slot. `query_ids`: every id names at least one pair of each micro-batch. `distance_bucket`: entry r + 511 is the bucket of key minus query r: buckets 16 to 31 are for r > 0, 0 to 15 for r <= 0; a magnitude below 8 is its own bucket (plus 16 for r > 0); larger magnitudes take buckets 8 to 15 (plus 16) that never fall as the magnitude grows, and the largest magnitude takes 15 (plus 16).
All inputs are finite; a program needn't handle non-finite values.
Results may differ from a plain program's by a relative error of at most 0.014.
Values may be sent and summed in bfloat16 or wider, within the bound.
No kernel may reach another device: no remote copies, remote signals or barrier semaphores. Data moves between devices by JAX's collectives and lax.ppermute only.
A program may use at most 320 MiB of HBM per device.

v0:
```python
import functools

import jax
import jax.numpy as jnp
from jax import lax
from jax.experimental import pallas as pl
from jax.experimental.pallas import tpu as pltpu
from jax.sharding import PartitionSpec as P

BUCKETS = 32
LOSS_SCALE = 1024
LANES = 128
ROWS = 256

norm_eps = 1e-06
clip_limit = 0.01
beta_first = 0.9
beta_second = 0.999
adam_eps = 1e-08
rate_matrix = 0.03
rate_vector = 0.25
decay_matrix = 0.1
masked_score = -1e30
gelu_slope = 0.7978845608028654
gelu_cubic = 0.044715
low_type = jnp.bfloat16
full_type = jnp.float32
core_swap = [(0, 1), (1, 0)]


def rms_scale(rows_in):
    return lax.rsqrt(jnp.mean(rows_in * rows_in, axis=-1, keepdims=True) + norm_eps)


def norm_input_grad(d_normed, gain_row, rows_in, norm_scale):
    weighted = d_normed * gain_row
    return norm_scale * weighted - rows_in * norm_scale**3 * jnp.mean(
        weighted * rows_in, axis=-1, keepdims=True
    )


def dot_nt(left, right):
    return lax.dot_general(left, right, (((1,), (1,)), ((), ())), preferred_element_type=full_type)


def dot_tn(left, right):
    return lax.dot_general(left, right, (((0,), (0,)), ((), ())), preferred_element_type=full_type)


def dot_nn(left, right):
    return lax.dot_general(left, right, (((1,), (0,)), ((), ())), preferred_element_type=full_type)


def call(
    kernel, name, out_shape, cost=(0, 0), vmem=16, deps=(), passing=(), in_specs=None,
    out_specs=None, input_output_aliases=None, **options
):
    single = not isinstance(out_shape, (list, tuple))
    out_shapes = [out_shape] if single else list(out_shape)
    outputs, extra = len(out_shapes), len(deps) + len(passing)

    def apply(*operands):
        inputs = len(operands)
        if not in_specs:
            options["grid"] = (1,)
        specs = in_specs or [whole(operand.shape) for operand in operands]
        targets = out_specs or [whole(shape.shape) for shape in out_shapes]
        targets = targets if isinstance(targets, (list, tuple)) else [targets]
        aliases = dict(input_output_aliases or {})
        for i in range(len(passing)):
            aliases[inputs + len(deps) + i] = outputs + i

        def run(*refs):
            own = inputs + extra
            kernel(*refs[:inputs], *refs[own : own + outputs], *refs[own + outputs + len(passing) :])

        results = pl.pallas_call(
            run,
            out_shape=[*out_shapes, *(shape_of(a.shape, a.dtype) for a in passing)],
            in_specs=[*specs, *[in_place()] * extra],
            out_specs=[*targets, *[in_place()] * len(passing)],
            input_output_aliases=aliases,
            compiler_params=pltpu.CompilerParams(vmem_limit_bytes=vmem * 1024 * 1024),
            cost_estimate=pl.CostEstimate(
                flops=int(cost[0] * 2e6), bytes_accessed=int(cost[1] * 1e3), transcendentals=0
            ),
            name=name,
            **options,
        )(*operands, *deps, *passing)
        return results[0] if single and not passing else results

    return apply


def in_place():
    return pl.BlockSpec(memory_space=pl.ANY)


def shape_of(shape, dtype):
    return jax.ShapeDtypeStruct(tuple(shape), dtype)


def whole(shape):
    return pl.BlockSpec(tuple(shape), lambda *_: (0,) * len(shape))


def on_scalars():
    return pl.BlockSpec(memory_space=pltpu.SMEM)


def row_blocks(shape, step=0):
    return pl.BlockSpec(tuple(shape), lambda i: (i,) + (0,) * (len(shape) - 1))


def column_blocks(shape, offset=0):
    return pl.BlockSpec(tuple(shape), lambda i: (0,) * (len(shape) - 1) + (i + offset,))


def fill_rows(target, pieces, columns=slice(None)):
    start = 0
    for piece in pieces:
        rows = piece.shape[0]
        target[start : start + rows, :] = piece[:, columns]
        start += rows


def spill_rows(value, pieces):
    start = 0
    for piece in pieces:
        rows = piece.shape[0]
        piece[...] = value[start : start + rows].astype(piece.dtype)
        start += rows


def swap(array, mask, size, label="exchange"):
    with jax.named_scope(f"{label}_across_{mask}"):
        return lax.ppermute(array, "dp", [(i, i ^ mask) for i in range(size)])


def other_core(array, label="other_core"):
    with jax.named_scope(label):
        return lax.ppermute(array, "mp", core_swap)


def stage_bits(size):
    if size == 16:
        return (4, 8, 2, 1)
    return tuple(1 << i for i in range(size.bit_length() - 1))


def block_masks(size):
    bits = stage_bits(size)
    return [sum(bit for i, bit in enumerate(bits) if k >> i & 1) for k in range(size)]


def piece_rows(size, width):
    if size != 16:
        return [width]
    return [width // 4] * 3 + [width // 8] * 2


def join_kernel(*refs):
    *part_refs, out_ref = refs
    start = 0
    for part in part_refs:
        rows = part.shape[0]
        out_ref[start : start + rows] = part[...]
        start += rows


def join(parts, **options):
    rows = sum(part.shape[0] for part in parts)
    return call(
        join_kernel, "join", shape_of((rows, *parts[0].shape[1:]), parts[0].dtype), **options
    )(*parts)


def step_kernel(parts, y_ref, x_ref, *refs):
    part_refs, (low_ref, high_ref, *line_refs) = refs[:parts], refs[parts:]
    low_ref[...] = y_ref[...]
    high_ref[...] = x_ref[...]
    if parts:
        join_kernel(*part_refs, *line_refs)


def gather_step(across_y, across_x, parts, **options):
    half = (across_y.shape[0] // 2, across_y.shape[1])
    shapes = [shape_of(half, across_y.dtype)] * 2
    if parts:
        shapes.append(shape_of((sum(p.shape[0] for p in parts), parts[0].shape[1]), parts[0].dtype))
    return call(
        functools.partial(step_kernel, len(parts)),
        "gather_step",
        shapes,
        grid=(1,),
        in_specs=[
            pl.BlockSpec(half, lambda i: (0, 0)),
            pl.BlockSpec(half, lambda i: (1, 0)),
            *(whole(part.shape) for part in parts),
        ],
        out_specs=[whole(shape.shape) for shape in shapes],
        **options,
    )(across_y, across_x, *parts)


def line_parts(part, size, label):
    return [part] + [swap(part, mask, size, label) for mask in (4, 8, 12)]


def side_parts(quarter, size, label):
    return [swap(quarter, mask, size, label) for mask in (2, 1)]


def corner_parts(low, high, size, label):
    return [swap(low, 1, size, label), swap(high, 2, size, label)]


def gather_doubling(part, size):
    for bit in stage_bits(size):
        part = jnp.concatenate([part, swap(part, bit, size)], axis=0)
    return part


def small_line(part, size, label):
    if size != 16:
        return part[None]
    return join(line_parts(part[None], size, label))


def small_plane(quarter, size, label):
    if size != 16:
        return [gather_doubling(quarter, size)]
    return [quarter] + [swap(quarter, mask, size, label) for mask in (2, 1, 3)]


def stacked(refs):
    return jnp.concatenate([ref[...] for ref in refs], axis=0)


def gather_small(part, size, label):
    return small_plane(small_line(part, size, label), size, label)


def plane_sum_kernel(y_ref, x_ref, low_ref, high_ref, y_out, x_out):
    half = low_ref.shape[0]
    y_out[:half] = (y_ref[:half].astype(full_type) + low_ref[...].astype(full_type)).astype(low_type)
    y_out[half:] = y_ref[half:]
    x_out[:half] = x_ref[:half]
    x_out[half:] = (x_ref[half:].astype(full_type) + high_ref[...].astype(full_type)).astype(low_type)


def line_sum_kernel(z_ref, y_ref, x_ref, own_ref, *out_refs):
    rows = own_ref.shape[0]
    for i in range(4):
        span = slice(i * rows, (i + 1) * rows)
        total = z_ref[span].astype(full_type) + y_ref[span].astype(full_type)
        total = total + x_ref[span].astype(full_type)
        target = own_ref if i == 0 else out_refs[i - 1]
        target[...] = total.astype(target.dtype)


class Scatter:
    def __init__(self, pieces, size, label):
        self.pieces, self.size, self.label, self.sources = pieces, size, label, ()
        if size == 16:
            *self.pieces, low, high = pieces
            self.came = [swap(low, 1, size, label), swap(high, 2, size, label)]

    def sides(self, deps=(), passing=()):
        if self.size != 16:
            return passing
        keep, to_y, to_x = self.pieces
        to_y, to_x, *passed = call(
            plane_sum_kernel,
            "plane_sum",
            [shape_of(to_y.shape, low_type)] * 2,
            deps=deps,
            passing=passing,
        )(to_y, to_x, *self.came)
        self.sources = (to_y, to_x)
        self.came = [swap(to_y, 2, self.size, self.label), swap(to_x, 1, self.size, self.label)]
        return passed

    def line(self, deps=(), passing=()):
        size, label = self.size, self.label
        if size != 16:
            grad = self.pieces[0]
            for bit in reversed(stage_bits(size)):
                half = grad.shape[0] // 2
                came = swap(grad[half:], bit, size, label)
                grad = (grad[:half].astype(full_type) + came.astype(full_type)).astype(low_type)
            return [grad.astype(full_type)], passing
        keep = self.pieces[0]
        part = (keep.shape[0] // 4, keep.shape[1])
        own, *others = call(
            line_sum_kernel,
            "line_sum",
            [shape_of(part, full_type)] + [shape_of(part, low_type)] * 3,
            deps=deps,
            passing=passing,
        )(keep, *self.came)
        came = [swap(other, mask, size, label) for other, mask in zip(others, (4, 8, 12))]
        return [own] + came, others[3:]


def pack_heads_kernel(in_ref, out_ref, gain_ref, tied_ref, a_ref):
    parts, rows, width = in_ref.shape
    for c in range(parts):
        a_ref[:, c * width : (c + 1) * width] = in_ref[c].astype(low_type)
    a_ref[:, parts * width : (parts + 1) * width] = out_ref[...].astype(low_type)
    gains, tied = gain_ref[...], tied_ref[...]
    vectors = few_rows([gains[i : i + 1] for i in range(3)] + [tied[i : i + 1] for i in range(2)], 16)
    pick = lax.broadcasted_iota(jnp.int32, (16, LANES), 0) == lax.broadcasted_iota(
        jnp.int32, (16, LANES), 1
    )
    extra = dot_tn(vectors.astype(low_type), jnp.where(pick, 1.0, 0.0).astype(low_type))
    a_ref[:, (parts + 1) * width :] = extra.astype(low_type)


def pack_hidden_kernel(up_ref, down_ref, b_ref, c_ref):
    b_ref[...] = up_ref[...].astype(low_type)
    c_ref[...] = down_ref[...].astype(low_type)


def order_kernel(x_ref, order_ref, out_ref):
    out_ref[...] = dot_nn(x_ref[...], order_ref[...]).astype(low_type)


def turn_kernel(x_ref, out_ref):
    out_ref[...] = x_ref[...].T


def head_lanes():
    lane = lax.broadcasted_iota(jnp.int32, (1, LANES), 1)
    return [lane < LANES // 2, lane >= LANES // 2]


def project_kernel(pieces, pairs, x_ref, *refs):
    weight_refs, (qkv_ref, normed_ref, vector_ref, w_ref) = refs[:pieces], refs[pieces:]
    parts = qkv_ref.shape[1]
    in_width = pairs * parts * LANES

    @pl.when(pl.program_id(0) == 0)
    def assemble():
        fill_rows(w_ref, weight_refs)
        pick = lax.broadcasted_iota(jnp.int32, (16, LANES), 0) == lax.broadcasted_iota(
            jnp.int32, (16, LANES), 1
        )
        vectors = dot_nt(jnp.where(pick, 1.0, 0.0).astype(low_type), w_ref[:, -LANES:])
        vector_ref[...] = vectors[:8]

    x = x_ref[...].astype(full_type)
    normed = (x * rms_scale(x) * vector_ref[0:1]).astype(low_type)
    normed_ref[...] = normed
    projected = dot_nn(normed, w_ref[:, :in_width]).astype(low_type)
    for c in range(parts):
        for p in range(pairs):
            start = (c * pairs + p) * LANES
            qkv_ref[p, c] = projected[:, start : start + LANES]


def project(rows_low, weights, pairs, deps):
    count, width = rows_low.shape
    parts = 3
    return call(
        functools.partial(project_kernel, len(weights), pairs),
        "projection",
        [
            shape_of((pairs, parts, count, LANES), low_type),
            shape_of((count, width), low_type),
            shape_of((8, width), full_type),
        ],
        deps=deps,
        grid=(count // ROWS,),
        in_specs=[row_blocks((ROWS, width)), *(whole(piece.shape) for piece in weights)],
        out_specs=[
            pl.BlockSpec((pairs, parts, ROWS, LANES), lambda i: (0, 0, i, 0)),
            row_blocks((ROWS, width)),
            whole((8, width)),
        ],
        scratch_shapes=[pltpu.VMEM((width, weights[0].shape[1]), low_type)],
    )(rows_low, *weights)


def attention_kernel(len_ref, line_ref, qkv_ref, *refs):
    att_ref, prob_ref, inv_ref, tile_ref = refs[-4:]
    micro, slot = prob_ref.shape[1], prob_ref.shape[3]
    blocks = slot // LANES
    lanes = head_lanes()
    for h in range(2):
        for d in range(2 * blocks - 1):
            piece = jnp.broadcast_to(
                line_ref[0, h : h + 1, d * LANES : (d + 2) * LANES], (LANES, 2 * LANES)
            )
            turned = pltpu.roll(piece, LANES + 1, 1, stride=1, stride_axis=0)
            tile_ref[h, d] = turned[:, :LANES]

    def micro_step(m, carry):
        start = pl.multiple_of(m * slot, slot)
        key_valid = lax.broadcasted_iota(jnp.int32, (1, slot), 1) < len_ref[m]
        keys = qkv_ref[0, 1, pl.ds(start, slot), :]
        values = qkv_ref[0, 2, pl.ds(start, slot), :]
        values = jnp.concatenate([values, jnp.ones_like(values)], axis=1)
        for r in range(slot // ROWS):
            rows = pl.ds(start + r * ROWS, ROWS)
            queries = qkv_ref[0, 0, rows, :]
            queries = jnp.concatenate(
                [queries * lanes[h].astype(low_type) for h in range(2)], axis=0
            )
            first = r * (ROWS // LANES)
            bias = jnp.concatenate(
                [
                    jnp.concatenate(
                        [tile_ref[h, j - first - i + blocks - 1] for j in range(blocks)], axis=1
                    )
                    for h in range(2)
                    for i in range(ROWS // LANES)
                ],
                axis=0,
            )
            scores = dot_nt(queries, keys)
            scores = jnp.where(key_valid, scores + bias, masked_score)
            terms = jnp.exp(scores - jnp.max(scores, axis=1, keepdims=True)).astype(low_type)
            for h in range(2):
                prob_ref[0, m, h, r * ROWS : (r + 1) * ROWS, :] = terms[h * ROWS : (h + 1) * ROWS]
            mixed = dot_nn(terms, values)
            inverse = 1.0 / mixed[:, LANES:]
            mixed = mixed[:, :LANES] * inverse
            att_ref[rows, :] = jnp.where(lanes[0], mixed[:ROWS], mixed[ROWS:]).astype(low_type)
            inv_ref[rows, :] = jnp.where(lanes[0], inverse[:ROWS], inverse[ROWS:])
        return carry

    lax.fori_loop(0, micro, micro_step, 0)


def attention(lengths, lines, qkv, pair, slot, before=(), deps=()):
    pairs, parts, count, _ = qkv.shape
    micro = count // slot
    spans = 2 * (slot // LANES) - 1
    column = pl.BlockSpec((count, LANES), lambda i: (0, pair))
    return call(
        attention_kernel,
        "attention_forward",
        [
            shape_of((count, pairs * LANES), low_type),
            shape_of((pairs, micro, 2, slot, slot), low_type),
            shape_of((count, pairs * LANES), full_type),
        ],
        deps=deps,
        grid=(1,),
        in_specs=[
            on_scalars(),
            pl.BlockSpec((1, 2, lines.shape[2]), lambda i: (pair, 0, 0)),
            pl.BlockSpec((1, parts, count, LANES), lambda i: (pair, 0, 0, 0)),
            *[in_place()] * len(before),
        ],
        out_specs=[
            column,
            pl.BlockSpec((1, micro, 2, slot, slot), lambda i: (pair, 0, 0, 0, 0)),
            column,
        ],
        input_output_aliases={3 + i: i for i in range(len(before))},
        scratch_shapes=[pltpu.VMEM((2, spans, LANES, LANES), full_type)],
    )(lengths, lines, qkv, *before)


def branch_kernel(att_ref, *refs):
    *weight_refs, out_ref, w_ref = refs

    @pl.when(pl.program_id(0) == 0)
    def assemble():
        fill_rows(w_ref, weight_refs)

    out_ref[...] = dot_nt(att_ref[...], w_ref[...]).astype(low_type)


def branch_rows(attended, weights, deps=()):
    count, head_width = attended.shape
    width = sum(piece.shape[0] for piece in weights)
    return call(
        branch_kernel,
        "branch",
        shape_of((count, width), low_type),
        deps=deps,
        grid=(count // (2 * ROWS),),
        in_specs=[
            row_blocks((2 * ROWS, head_width)),
            *(pl.BlockSpec((piece.shape[0], head_width), lambda i: (0, 3)) for piece in weights),
        ],
        out_specs=row_blocks((2 * ROWS, width)),
        scratch_shapes=[pltpu.VMEM((width, head_width), low_type)],
    )(attended, *weights)


def hidden_kernel(pieces, len_ref, x_ref, own_ref, came_ref, vector_ref, *refs):
    weight_refs, refs = refs[:pieces], refs[pieces:]
    normed_ref, slope_ref, act_ref, sum_ref, w_ref = refs
    m = pl.program_id(0)
    slot = x_ref.shape[0]

    @pl.when(m == 0)
    def assemble():
        fill_rows(w_ref, weight_refs)

    middle = middle_rows(x_ref, own_ref, came_ref)
    normed = (middle * rms_scale(middle) * vector_ref[1:2]).astype(low_type)
    valid = lax.broadcasted_iota(jnp.int32, (slot, 1), 0) < len_ref[m]
    normed_ref[...] = jnp.where(valid, normed, jnp.zeros_like(normed))
    counted = lax.broadcasted_iota(jnp.int32, (16, slot), 1) < len_ref[m]
    counted = jnp.where(counted, 1.0, 0.0).astype(low_type)
    sum_ref[0] = jnp.sum(jnp.where(valid, middle, 0.0), axis=0, keepdims=True)
    block = 3 * LANES

    def columns_step(n, carry):
        columns = pl.ds(pl.multiple_of(n * block, block), block)
        v = dot_nn(normed, w_ref[:, columns])
        square = v * v
        gate = jnp.tanh(v * (gelu_slope + (gelu_slope * gelu_cubic) * square))
        half = 0.5 + 0.5 * gate
        active = (v * half).astype(low_type)
        act_ref[0, :, columns] = dot_nn(counted, active)[0:1]
        inner = 0.5 * gelu_slope + (1.5 * gelu_slope * gelu_cubic) * square
        slope_ref[:, columns] = (half + v * (1.0 - gate * gate) * inner).astype(low_type)
        return carry

    lax.fori_loop(0, w_ref.shape[1] // block, columns_step, 0)


def middle_rows(x_ref, own_ref, came_ref):
    branch = own_ref[...].astype(full_type) + came_ref[...].astype(full_type)
    return x_ref[...].astype(full_type) + branch


def hidden(lengths, rows_low, own, came, vectors, weights, slot):
    count, width = rows_low.shape
    micro = count // slot
    inner = weights[0].shape[1]
    return call(
        functools.partial(hidden_kernel, len(weights)),
        "hidden_forward",
        [
            shape_of((count, width), low_type),
            shape_of((count, inner), low_type),
            shape_of((micro, 1, inner), full_type),
            shape_of((micro, 1, width), full_type),
        ],
        cost=(1200, 20000),
        grid=(micro,),
        in_specs=[
            on_scalars(),
            *[row_blocks((slot, width))] * 3,
            whole(vectors.shape),
            *(whole(piece.shape) for piece in weights),
        ],
        out_specs=[
            row_blocks((slot, width)),
            row_blocks((slot, inner)),
            row_blocks((1, 1, inner)),
            row_blocks((1, 1, width)),
        ],
        scratch_shapes=[pltpu.VMEM((width, inner), low_type)],
    )(lengths, rows_low, own, came, vectors, *weights)


def few_rows(rows, count):
    place = lax.broadcasted_iota(jnp.int32, (count, rows[0].shape[1]), 0)
    total = jnp.zeros(place.shape, full_type)
    for i, row in enumerate(rows):
        total = jnp.where(place == i, row, total)
    return total


def pool_kernel(act_ref, *refs):
    *weight_refs, out_ref, w_ref = refs
    fill_rows(w_ref, weight_refs)
    sums = [act_ref[m] for m in range(act_ref.shape[0])]
    highs = [row.astype(low_type).astype(full_type) for row in sums]
    rests = [row - high for row, high in zip(sums, highs)]
    down = dot_nt(few_rows(highs + rests, 16).astype(low_type), w_ref[...])
    micro = len(sums)
    out_ref[...] = few_rows([down[m : m + 1] + down[micro + m : micro + m + 1] for m in range(micro)], 8)


def margin_kernel(len_ref, own_ref, other_ref, sum_ref, vector_ref, margin_ref, pooled_ref):
    margins, vectors_pooled = [], []
    for m in range(sum_ref.shape[0]):
        total = own_ref[m : m + 1] + other_ref[m : m + 1] + sum_ref[m]
        pooled = (total / len_ref[m].astype(full_type)).astype(low_type).astype(full_type)
        final = pooled * rms_scale(pooled) * vector_ref[2:3]
        logits = [
            jnp.sum(final * vector_ref[i : i + 1], axis=1, keepdims=True) * pooled.shape[1] ** (-0.5)
            for i in (3, 4)
        ]
        margins.append(jnp.broadcast_to(logits[0] - logits[1], (1, LANES)))
        vectors_pooled.append(pooled)
    margin_ref[...] = few_rows(margins, 8)
    pooled_ref[...] = few_rows(vectors_pooled, 8)


def rank_kernel(
    margin_pieces, down_pieces, up_pieces, len_ref, same_ref, positive_ref, pooled_ref,
    vector_ref, sum_ref, slope_ref, *refs
):
    margin_refs, refs = refs[:margin_pieces], refs[margin_pieces:]
    down_refs, refs = refs[:down_pieces], refs[down_pieces:]
    up_refs, refs = refs[:up_pieces], refs[up_pieces:]
    line_ref, act_ref, small_ref, d_ref, down_ref, up_ref = refs
    m = pl.program_id(0)

    @pl.when(m == 0)
    def rank():
        fill_rows(down_ref, down_refs)
        fill_rows(up_ref, up_refs)
        margins, same = stacked(margin_refs), same_ref[...] > 0.5
        row_max = jnp.max(jnp.where(same, margins, masked_score), axis=0)
        total = jnp.sum(jnp.where(same, jnp.exp(margins - row_max[None]), 0.0), axis=0)
        chance = jnp.exp(margins[0] - row_max) / total
        d_margins = LOSS_SCALE * (chance - positive_ref[...])
        tied_gap = vector_ref[3:4] - vector_ref[4:5]
        gain = vector_ref[2:3]
        lines, tied = [], 0.0
        for i in range(2):
            pooled = pooled_ref[i : i + 1]
            scale = rms_scale(pooled)
            d_logit = d_margins[i : i + 1, 0:1] * pooled.shape[1] ** (-0.5)
            d_final = d_logit * tied_gap
            tied = tied + pooled * scale * d_logit
            d_pooled = norm_input_grad(d_final, gain, pooled, scale)
            lines.append(d_pooled / len_ref[i].astype(full_type))
        line_ref[...] = few_rows(lines, 8)
        width, parts = tied.shape[1], sum_ref.shape[2] // tied.shape[1]
        rows = [line.astype(low_type).astype(full_type) for line in lines]
        for i in range(2):
            sums = sum_ref[i]
            rows += [sums[:, part * width : (part + 1) * width] for part in range(parts)]
        small_ref[...] = few_rows([*rows, tied], 8)
        d_act = dot_nn(few_rows(lines, 16).astype(low_type), down_ref[...])
        act_ref[...] = d_act[:8]

    d_row = jnp.where(m == 0, act_ref[0:1], act_ref[1:2])
    d_hidden = (slope_ref[...].astype(full_type) * d_row).astype(low_type)
    d_normed = dot_nt(d_hidden, up_ref[...])
    valid = lax.broadcasted_iota(jnp.int32, (d_normed.shape[0], 1), 0) < len_ref[m]
    d_ref[...] = jnp.where(valid, d_normed, 0.0).astype(low_type)


def rank_back(lengths, margins, same, positive, pooled, vectors, act_sum, slope, down, up, slot, deps):
    count, inner = slope.shape
    width = pooled.shape[1]
    return call(
        functools.partial(rank_kernel, len(margins), len(down), len(up)),
        "rank_backward",
        [
            shape_of((8, width), full_type),
            shape_of((8, inner), full_type),
            shape_of((8, width), full_type),
            shape_of((count, width), low_type),
        ],
        cost=(1200, 20000),
        deps=deps,
        grid=(count // slot,),
        in_specs=[
            on_scalars(),
            *(whole(array.shape) for array in (same, positive, pooled, vectors, act_sum)),
            row_blocks((slot, inner)),
            *(whole(piece.shape) for piece in (*margins, *down, *up)),
        ],
        out_specs=[
            whole((8, width)),
            whole((8, inner)),
            whole((8, width)),
            row_blocks((slot, width)),
        ],
        scratch_shapes=[pltpu.VMEM((width, inner), low_type), pltpu.VMEM((width, inner), low_type)],
    )(lengths, same, positive, pooled, vectors, act_sum, slope, *margins, *down, *up)


def up_grad_kernel(slot, normed_ref, slope_ref, act_ref, *refs):
    *out_refs, turned_ref = refs

    @pl.when(pl.program_id(0) == 0)
    def turn():
        turned_ref[...] = normed_ref[...].T

    total = 0.0
    for m in range(normed_ref.shape[0] // slot):
        rows = slice(m * slot, (m + 1) * slot)
        d_hidden = (slope_ref[rows].astype(full_type) * act_ref[m : m + 1]).astype(low_type)
        total = total + dot_nn(turned_ref[:, rows], d_hidden)
    spill_rows(total, out_refs)


def up_grad(normed, slope, d_act, rows, slot):
    count, width = normed.shape
    inner = slope.shape[1]
    block = 4 * LANES
    return call(
        functools.partial(up_grad_kernel, slot),
        "hidden_in_gradient",
        [shape_of((r, inner), low_type) for r in rows],
        cost=(1200, 15000),
        grid=(inner // block,),
        in_specs=[
            whole(normed.shape),
            column_blocks((count, block)),
            column_blocks((8, block)),
        ],
        out_specs=[column_blocks((r, block)) for r in rows],
        scratch_shapes=[pltpu.VMEM((width, count), low_type)],
    )(normed, slope, d_act)


def middle_kernel(
    pieces, len_ref, x_ref, branch_ref, other_ref, own_ref, came_ref, vector_ref, line_ref,
    att_ref, inv_ref, *refs
):
    weight_refs, refs = refs[:pieces], refs[pieces:]
    d_ref, d_att_ref, total_ref, w_ref = refs
    m = pl.program_id(0)

    @pl.when(m == 0)
    def assemble():
        fill_rows(w_ref, weight_refs)
        total_ref[...] = jnp.zeros_like(total_ref)

    middle = middle_rows(x_ref, branch_ref, other_ref)
    own = own_ref[...].astype(full_type)
    scale = rms_scale(middle)
    valid = lax.broadcasted_iota(jnp.int32, (middle.shape[0], 1), 0) < len_ref[m]
    line = jnp.where(m == 0, line_ref[0:1], line_ref[1:2])
    d_middle = jnp.where(valid, line, 0.0) + norm_input_grad(
        own + came_ref[...].astype(full_type), vector_ref[1:2], middle, scale
    )
    d_ref[...] = d_middle
    d_low = d_middle.astype(low_type)
    d_att_ref[...] = (dot_nn(d_low, w_ref[...]) * inv_ref[...]).astype(low_type)
    total_ref[...] += dot_tn(d_low, att_ref[...])


def middle_back(
    lengths, rows_low, branch, other, own, came, vectors, lines, attended, inverse, weights, slot
):
    count, width = rows_low.shape
    head_width = attended.shape[1]
    return call(
        functools.partial(middle_kernel, len(weights)),
        "middle_backward",
        [
            shape_of((count, width), full_type),
            shape_of((count, head_width), low_type),
            shape_of((width, head_width), full_type),
        ],
        cost=(600, 15000),
        grid=(count // slot,),
        in_specs=[
            on_scalars(),
            *[row_blocks((slot, width))] * 5,
            whole(vectors.shape),
            whole(lines.shape),
            row_blocks((slot, head_width)),
            row_blocks((slot, head_width)),
            *(
                pl.BlockSpec((piece.shape[0], head_width), lambda i: (0, 3)) for piece in weights
            ),
        ],
        out_specs=[
            row_blocks((slot, width)),
            row_blocks((slot, head_width)),
            whole((width, head_width)),
        ],
        scratch_shapes=[pltpu.VMEM((width, head_width), low_type)],
    )(
        lengths, rows_low, branch, other, own, came, vectors, lines, attended, inverse, *weights
    )


def attention_back_kernel(
    befores, grads, tables, own, prob_ref, qkv_ref, d_ref, att_ref, turned_ref, hot_ref, *refs
):
    table_refs, refs = refs[:tables], refs[tables:]
    grad_refs, refs = refs[:grads], refs[grads:]
    d_out_ref, table_ref, *out_refs, tile_ref, dk_ref, dv_ref = refs[befores:]
    step = pl.program_id(0)

    if grads:

        @pl.when(step > 0)
        def projection():
            spill_rows(grad_refs[0][...], out_refs)

    @pl.when(step == 0)
    def heads():
        pair_back(
            prob_ref, qkv_ref, d_ref, att_ref, turned_ref, hot_ref, d_out_ref, table_ref, out_refs,
            tile_ref, dk_ref, dv_ref
        )
        if tables:
            lines = [ref[0, h : h + 1] for ref in (*table_refs, table_ref) for h in range(2)]
            width = turned_ref.shape[0]
            place = lax.broadcasted_iota(jnp.int32, (width, 16), 0) % own
            pick = place == lax.broadcasted_iota(jnp.int32, (width, 16), 1)
            pick = jnp.where(pick, 1.0, 0.0).astype(low_type)
            spread = dot_nn(pick, few_rows(lines, 16).astype(low_type))
            spill_rows(spread, [ref.at[:, 3 * LANES :] for ref in out_refs])


def pair_back(
    prob_ref, qkv_ref, d_ref, att_ref, turned_ref, hot_ref, d_out_ref, table_ref, out_refs,
    tile_ref, dk_ref, dv_ref
):
    micro, slot = prob_ref.shape[1], prob_ref.shape[3]
    blocks = slot // LANES
    spans = 2 * blocks - 1
    lanes = head_lanes()

    tile_ref[...] = jnp.zeros_like(tile_ref)

    def micro_step(m, carry):
        start = pl.multiple_of(m * slot, slot)
        everything = pl.ds(start, slot)
        keys, values = qkv_ref[0, 1, everything, :], qkv_ref[0, 2, everything, :]
        for r in range(slot // ROWS):
            rows = pl.ds(start + r * ROWS, ROWS)
            queries = qkv_ref[0, 0, rows, :]
            queries = jnp.concatenate(
                [queries * lanes[h].astype(low_type) for h in range(2)], axis=0
            )
            d_att = d_ref[rows, :]
            product = d_att.astype(full_type) * att_ref[rows, :].astype(full_type)
            row_dot = jnp.concatenate(
                [
                    jnp.sum(jnp.where(lanes[h], product, 0.0), axis=1, keepdims=True)
                    for h in range(2)
                ],
                axis=0,
            )
            d_att = jnp.concatenate([d_att * lanes[h].astype(low_type) for h in range(2)], axis=0)
            span = slice(r * ROWS, (r + 1) * ROWS)
            probs = jnp.concatenate([prob_ref[0, m, h, span, :] for h in range(2)], axis=0)
            d_scores = probs.astype(full_type) * (dot_nt(d_att, values) - row_dot)
            d_low = d_scores.astype(low_type)
            for h in range(2):
                for i in range(ROWS // LANES):
                    for j in range(blocks):
                        top = h * ROWS + i * LANES
                        tile_ref[h, j - r * (ROWS // LANES) - i + blocks - 1] += d_scores[
                            top : top + LANES, j * LANES : (j + 1) * LANES
                        ]
            d_queries = dot_nn(d_low, keys)
            d_out_ref[0, 0, rows, :] = jnp.where(
                lanes[0], d_queries[:ROWS], d_queries[ROWS:]
            ).astype(low_type)
            d_keys, d_values = dot_tn(d_low, queries), dot_tn(probs, d_att)
            dk_ref[...] = d_keys if r == 0 else dk_ref[...] + d_keys
            dv_ref[...] = d_values if r == 0 else dv_ref[...] + d_values
        d_out_ref[0, 1, everything, :] = dk_ref[...].astype(low_type)
        d_out_ref[0, 2, everything, :] = dv_ref[...].astype(low_type)
        return carry

    lax.fori_loop(0, micro, micro_step, 0)
    d_project = jnp.concatenate([d_out_ref[0, c] for c in range(3)], axis=1)
    spill_rows(dot_nn(turned_ref[...], d_project), [ref.at[:, : 3 * LANES] for ref in out_refs])
    flip = (
        lax.broadcasted_iota(jnp.int32, (LANES, LANES), 0)
        + lax.broadcasted_iota(jnp.int32, (LANES, LANES), 1)
        == LANES - 1
    )
    flip = jnp.where(flip, 1.0, 0.0).astype(low_type)
    table = jnp.zeros((16, LANES), full_type)
    for d in range(spans):
        highs, rests = [], []
        for h in range(2):
            tile = tile_ref[h, d]
            high = tile.astype(low_type)
            rest = (tile - high.astype(full_type)).astype(low_type)
            flipped = dot_nn(flip, high) + dot_nn(flip, rest)
            wide = jnp.concatenate([flipped, jnp.zeros_like(flipped)], axis=1)
            turned = pltpu.roll(wide, 0, 1, stride=1, stride_axis=0)
            line = jnp.sum(turned, axis=0, keepdims=True)
            highs.append(line.astype(low_type).astype(full_type))
            rests.append(line - highs[-1])
        table = table + dot_nn(few_rows(highs + rests, 16).astype(low_type), hot_ref[d])
    table_ref[0] = few_rows([table[h : h + 1] + table[2 + h : 3 + h] for h in range(2)], 8)


def attention_back(
    probs, qkv, d_attended, attended, turned, hot, rows, pair, slot, own,
    grad_out=None, tables=(), before=(), deps=()
):
    width, count = turned.shape
    micro = count // slot
    pairs = qkv.shape[0]
    spans = 2 * (slot // LANES) - 1
    lead = lambda shape: pl.BlockSpec(shape, lambda i: (pair,) + (0,) * (len(shape) - 1))
    column = pl.BlockSpec((count, LANES), lambda i: (0, pair))
    if tables:
        steps, extra, extra_specs = 1, tables, [whole(table.shape) for table in tables]
        gradients = [shape_of((r, 4 * LANES), low_type) for r in rows]
        gradient_specs = [whole((r, 4 * LANES)) for r in rows]
    else:
        steps = 1 if grad_out is None else 2
        extra = () if grad_out is None else (grad_out,)
        extra_specs = [whole(array.shape) for array in extra]
        gradients = [shape_of((r, pairs * 3 * LANES), low_type) for r in rows]
        gradient_specs = [pl.BlockSpec((r, 3 * LANES), lambda i: (0, i + pair)) for r in rows]
    first = 6 + len(extra)
    return call(
        functools.partial(
            attention_back_kernel, len(before), 0 if grad_out is None else 1, len(tables), own
        ),
        "attention_backward",
        [
            shape_of((pairs, 3, count, LANES), low_type),
            shape_of((1, 8, LANES), full_type),
            *gradients,
        ],
        deps=deps,
        grid=(steps,),
        in_specs=[
            lead((1, micro, 2, slot, slot)),
            lead((1, 3, count, LANES)),
            column,
            column,
            whole(turned.shape),
            whole(hot.shape),
            *extra_specs,
            *[in_place()] * len(before),
        ],
        out_specs=[lead((1, 3, count, LANES)), whole((1, 8, LANES)), *gradient_specs],
        input_output_aliases={first + i: i if i == 0 else i + 1 for i in range(len(before))},
        scratch_shapes=[
            pltpu.VMEM((2, spans, LANES, LANES), full_type),
            pltpu.VMEM((slot, LANES), full_type),
            pltpu.VMEM((slot, LANES), full_type),
        ],
    )(probs, qkv, d_attended, attended, turned, hot, *extra, *before)


def normed_back_kernel(d_ref, *refs):
    *weight_refs, out_ref, w_ref = refs
    pairs, parts = d_ref.shape[0], d_ref.shape[1]

    @pl.when(pl.program_id(0) == 0)
    def assemble():
        fill_rows(w_ref, weight_refs, slice(0, w_ref.shape[1]))

    blocks = [d_ref[p, c] for c in range(parts) for p in range(pairs)]
    d_normed = dot_nt(jnp.concatenate(blocks, axis=1), w_ref[...])
    out_ref[...] = d_normed.astype(low_type)


def normed_back(d_project, weights, deps):
    pairs, parts, count, _ = d_project.shape
    width = sum(piece.shape[0] for piece in weights)
    return call(
        normed_back_kernel,
        "normed_backward",
        shape_of((count, width), low_type),
        cost=(900, 15000),
        deps=deps,
        grid=(count // ROWS,),
        in_specs=[
            pl.BlockSpec((pairs, parts, ROWS, LANES), lambda i: (0, 0, i, 0)),
            *(whole(piece.shape) for piece in weights),
        ],
        out_specs=row_blocks((ROWS, width)),
        scratch_shapes=[pltpu.VMEM((width, pairs * parts * LANES), low_type)],
    )(d_project, *weights)


def token_kernel(d_ref, own_ref, came_ref, x_ref, vector_ref, order_ref, out_ref):
    x = x_ref[...].astype(full_type)
    d_normed = own_ref[...].astype(full_type) + came_ref[...].astype(full_type)
    grad = d_ref[...] + norm_input_grad(d_normed, vector_ref[0:1], x, rms_scale(x))
    high = grad.astype(low_type)
    rest = (grad - high.astype(full_type)).astype(low_type)
    order = order_ref[...]
    out_ref[...] = dot_nt(high, order) + dot_nt(rest, order)


def token_back(d_middle, own, came, rows_low, vectors, order, deps):
    count, width = rows_low.shape
    return call(
        token_kernel,
        "token_gradient",
        shape_of((count, width), full_type),
        cost=(1200, 15000),
        deps=deps,
        grid=(count // ROWS,),
        in_specs=[row_blocks((ROWS, width))] * 4 + [whole(vectors.shape), whole(order.shape)],
        out_specs=row_blocks((ROWS, width)),
    )(d_middle, own, came, rows_low, vectors, order)


def total_kernel(smalls, counts, micro, pairs, *refs):
    small_refs, refs = refs[:smalls], refs[smalls:]
    groups = []
    for count in counts:
        groups.append(refs[:count])
        refs = refs[count:]
    in_ref, up_ref, gain_ref, tied_ref, down_ref, line_ref, *out_refs = refs
    size, width = sum(ref.shape[0] for ref in small_refs), small_refs[0].shape[2]
    row_of = lambda row: jnp.concatenate([ref[:, row, :] for ref in small_refs], axis=0)
    own = down_ref.shape[0]
    inverse = 1.0 / LOSS_SCALE
    add_up = lambda values: jnp.sum(values, axis=0, keepdims=True).sum(axis=1, keepdims=True)
    squares, sums = 0.0, []
    for group, out_ref in zip(groups, out_refs):
        total = sum(ref[...].astype(full_type) for ref in group) * inverse
        total, rest = total[:, : out_ref.shape[1]], total[:, out_ref.shape[1] :]
        out_ref[...] = total
        sums.append((total, rest))
        squares = squares + add_up(total * total)
    table = sums[1][1]

    block = lax.broadcasted_iota(jnp.int32, (size, width), 1) // own
    mine = block == lax.broadcasted_iota(jnp.int32, (size, width), 0)
    fold = lax.broadcasted_iota(jnp.int32, (width, LANES), 0) % own == lax.broadcasted_iota(
        jnp.int32, (width, LANES), 1
    )
    fold = jnp.where(fold, 1.0, 0.0).astype(low_type)
    pick = lambda row: jnp.where(mine, row_of(row), 0.0)
    down = 0.0
    parts = down_ref.shape[1] // width
    for m in range(micro):
        lines = dot_nn(pick(m).astype(low_type), fold).astype(low_type)
        acts = [row_of(micro + m * parts + i) for i in range(parts)]
        acts = jnp.concatenate(acts, axis=1)
        high = acts.astype(low_type)
        rest = (acts - high.astype(full_type)).astype(low_type)
        down = down + dot_tn(lines, high) + dot_tn(lines, rest)
    down = down[:own] * inverse
    down_ref[...] = down
    squares = squares + add_up(down * down)

    rest = jnp.sum(pick(micro + micro * parts), axis=0, keepdims=True) * inverse
    rest = jnp.broadcast_to(rest, (16, width))
    ranked = 0.0
    for _ in range(3):
        high = rest.astype(low_type)
        ranked = ranked + dot_nn(high, fold)
        rest = rest - high.astype(full_type)
    ranked = ranked[0:1, :own]
    rounded = lambda ref, i: ref[i : i + 1].astype(low_type).astype(full_type)
    tied_gap = rounded(tied_ref, 0) - rounded(tied_ref, 1)

    def through(products):
        ones = jnp.ones((16, products.shape[1]), low_type)
        high = products.astype(low_type)
        rest = (products - high.astype(full_type)).astype(low_type)
        return (dot_nt(ones, high) + dot_nt(ones, rest))[0:1]

    weighed = lambda ref, total: ref.astype(low_type).astype(full_type) * total
    first = 0.0
    for p in range(pairs):
        source = sums[0][0] if p < pairs - 1 else sums[1][0]
        offset = p * 3 * LANES if p < pairs - 1 else 0
        for c in range(3):
            columns = slice(offset + c * LANES, offset + (c + 1) * LANES)
            first = first + weighed(in_ref[c, :, p * LANES : (p + 1) * LANES], source[:, columns])
    rows = [
        through(first) / rounded(gain_ref, 0),
        through(weighed(up_ref[...], sums[2][0])) / rounded(gain_ref, 1),
        tied_gap * ranked,
        rounded(gain_ref, 2) * ranked,
    ]
    place = lax.broadcasted_iota(jnp.int32, (8, own), 0)
    extra = jnp.zeros((8, own), full_type)
    for i, row in enumerate(rows):
        extra = jnp.where(place == i, row, extra)
    line_ref[...] = jnp.zeros_like(line_ref)
    line_ref[:8, :own] = extra
    line_ref[8:16] = jnp.broadcast_to(squares, (8, LANES))
    line_ref[16 : 16 + 2 * pairs] = table[: 2 * pairs]


def totals(small_all, grads, heads_in, hidden_in, gains, tied_rows, widths, micro, deps):
    counts = tuple(len(group) for group in grads)
    flat = [array for group in grads for array in group]
    own, inner = hidden_in.shape
    down, line, *sums = call(
        functools.partial(
            total_kernel, len(small_all), counts, micro, heads_in.shape[2] // LANES
        ),
        "gradient_totals",
        [
            shape_of((own, inner), full_type),
            shape_of((24, LANES), full_type),
            *(shape_of((own, width), full_type) for width in widths),
        ],
        cost=(100, 10000),
        deps=deps,
    )(*small_all, *flat, heads_in, hidden_in, gains, tied_rows)
    return down, line, sums


def adam(weight, first_old, second, grad, factor, rate, decay, step_ref):
    clipped = grad * factor
    next_first = beta_first * first_old + (1.0 - beta_first) * clipped
    next_second = beta_second * second + (1.0 - beta_second) * clipped * clipped
    first_hat = next_first * step_ref[0]
    second_hat = next_second * step_ref[1]
    next_weight = weight - rate * (first_hat / (jnp.sqrt(second_hat) + adam_eps) + decay * weight)
    return next_weight, next_first, next_second


def square_kernel(heads, own_ref, other_ref, out_ref, extra_ref):
    place = lax.broadcasted_iota(jnp.int32, (8, LANES), 0)
    extra = own_ref[:8] + jnp.where(place < 2, other_ref[:8], 0.0)
    extra_ref[...] = extra
    counted = jnp.where(place == 3, 2.0, 1.0) * extra * extra
    add_up = lambda values: jnp.sum(values, axis=0, keepdims=True).sum(axis=1, keepdims=True)
    squares = own_ref[8:16] + other_ref[8:16] + add_up(counted)
    out_ref[:8] = squares
    tables = own_ref[16:24] * own_ref[16:24] + other_ref[16:24] * other_ref[16:24]
    out_ref[8:16] = own_ref[16:24]
    out_ref[16:24] = jnp.broadcast_to(add_up(tables), (8, LANES))


def update_kernel(squares, groups, pick_ref, step_ref, extra_ref, *refs):
    square_refs, refs = refs[:squares], refs[squares:]
    grad_refs, refs = refs[:groups], refs[groups:]
    state_refs, refs = refs[:21], refs[21:]
    norm_ref, *out_refs = refs
    tiles = stacked(square_refs)
    device = lax.broadcasted_iota(jnp.int32, (tiles.shape[0], 1, 1), 0)
    tables = jnp.sum(jnp.where(device == pick_ref[0], tiles[:, 8:24], 0.0), axis=0)
    norm = jnp.sqrt(jnp.sum(tiles[:, 0:8], axis=0)[0:1, 0:1] + tables[8:9, 0:1])
    norm_ref[...] = norm
    factor = jnp.minimum(1.0, clip_limit / (norm + 1e-06))
    weights, firsts, seconds = state_refs[:7], state_refs[7:14], state_refs[14:]
    next_weights, next_firsts, next_seconds = out_refs[:7], out_refs[7:14], out_refs[14:]

    def step(index, where, grad, rate, decay):
        results = adam(
            weights[index][where], firsts[index][where], seconds[index][where], grad, factor,
            rate, decay, step_ref,
        )
        for target, result in zip((next_weights, next_firsts, next_seconds), results):
            target[index][where] = result

    everything = (slice(None), slice(None))
    early_ref, late_ref, up_ref, down_ref = grad_refs
    part = pl.program_id(0)
    pairs = weights[0].shape[2] // LANES
    for p in range(pairs):
        source, offset = (early_ref, p * 3) if p < pairs - 1 else (late_ref, 0)
        columns = pl.ds(pl.multiple_of((offset + part) * LANES, LANES), LANES)
        where = (0, slice(None), slice(p * LANES, (p + 1) * LANES))
        step(0, where, source[:, columns], rate_matrix, decay_matrix)
    columns = pl.ds(pl.multiple_of(((pairs - 1) * 3 + part) * LANES, LANES), LANES)
    step(1, everything, early_ref[:, columns], rate_matrix, decay_matrix)
    step(2, everything, up_ref[...], rate_matrix, decay_matrix)
    step(3, everything, down_ref[...], rate_matrix, decay_matrix)

    @pl.when(part == 0)
    def small():
        rows = weights[4].shape[1]
        extra = extra_ref[...]
        step(4, everything, extra[0:3, :rows], rate_vector, 0.0)
        tied = extra[3:4, :rows]
        step(5, everything, jnp.concatenate([tied, -tied], axis=0), rate_vector, 0.0)
        step(6, everything, tables[: 2 * pairs, :BUCKETS], rate_vector, 0.0)


def update(pick, corrections, extra, squares, grads, states):
    parts = states[0].shape[0]
    thirds = lambda array: column_blocks((array.shape[0], array.shape[1] // parts))
    state_specs = []
    for _ in range(3):
        one = states[len(state_specs) : len(state_specs) + 7]
        state_specs += [pl.BlockSpec((1, *one[0].shape[1:]), lambda i: (i, 0, 0))]
        state_specs += [thirds(array) for array in one[1:4]]
        state_specs += [whole(array.shape) for array in one[4:]]
    return call(
        functools.partial(update_kernel, len(squares), len(grads)),
        "update",
        [shape_of((1, 1), full_type)] + [shape_of(s.shape, full_type) for s in states],
        cost=(0, 6000),
        grid=(parts,),
        in_specs=[
            on_scalars(),
            on_scalars(),
            whole(extra.shape),
            *(whole(array.shape) for array in squares),
            *(whole(array.shape) for array in grads[:2]),
            *(thirds(array) for array in grads[2:]),
            *state_specs,
        ],
        out_specs=[whole((1, 1)), *state_specs],
    )(pick, corrections, extra, *squares, *grads, *states)


def body(
    tokens,
    pair_lengths,
    query_ids,
    distance_bucket,
    step_count,
    heads_in,
    heads_out,
    hidden_in,
    hidden_out,
    gains,
    tied_rows,
    bias_table,
    first_heads_in,
    first_heads_out,
    first_hidden_in,
    first_hidden_out,
    first_gains,
    first_tied,
    first_table,
    second_heads_in,
    second_heads_out,
    second_hidden_in,
    second_hidden_out,
    second_gains,
    second_tied,
    second_table,
):
    size = lax.axis_size("dp")
    me = lax.axis_index("dp")
    core = lax.axis_index("mp")
    micro, _, slot, width = tokens.shape
    count = micro * slot
    own, local_heads = heads_in.shape[0], bias_table.shape[1]
    head_width = heads_in.shape[2]
    inner = hidden_in.shape[1]
    pairs = local_heads // 2
    spans = 2 * (slot // LANES) - 1
    turn_matrix = lambda array: jnp.transpose(array, (1, 0, 2))
    heads_in, first_heads_in, second_heads_in = (
        turn_matrix(array) for array in (heads_in, first_heads_in, second_heads_in)
    )
    gains, tied_rows, bias_table = gains.T, tied_rows.T, bias_table.T
    first_gains, first_tied, first_table = first_gains.T, first_tied.T, first_table.T
    second_gains, second_tied, second_table = second_gains.T, second_tied.T, second_table.T

    packed_heads = call(
        pack_heads_kernel, "pack_heads", shape_of((own, 4 * head_width + LANES), low_type)
    )(heads_in, heads_out, gains, tied_rows)
    packed_up, packed_down = call(
        pack_hidden_kernel, "pack_hidden", [shape_of((own, inner), low_type)] * 2
    )(hidden_in, hidden_out)
    pair_ids = jnp.bitwise_xor(me, jnp.array(block_masks(size), jnp.int32))
    place = (pair_ids[:, None] * own + jnp.arange(own, dtype=jnp.int32)[None, :]).reshape(width)
    order = (jnp.arange(width, dtype=jnp.int32)[:, None] == place[None, :]).astype(low_type)
    lengths = pair_lengths.reshape(micro)
    queries = query_ids[:, pair_ids]
    same_query = queries == queries[:, :1]
    earlier = jnp.any(same_query & (pair_ids < me)[None, :], axis=1)
    to_tile = lambda rows_m: jnp.broadcast_to(
        jnp.concatenate(
            [rows_m, jnp.zeros(rows_m.shape[:-1] + (8 - micro,), full_type)], axis=-1
        )[..., None],
        rows_m.shape[:-1] + (8, LANES),
    )
    same_tile = to_tile(same_query.astype(full_type).T)
    positive_tile = to_tile(jnp.where(earlier, 0.0, 1.0))

    bucket_line = jnp.concatenate([distance_bucket, jnp.full((1,), -1, jnp.int32)])
    bucket_hot = (
        bucket_line[:, None] == jnp.arange(LANES, dtype=jnp.int32)[None, :]
    ).astype(low_type)
    lines = dot_nt(bias_table.astype(low_type), bucket_hot[:, :BUCKETS])
    lines = lines.reshape(pairs, 2, 2 * slot)
    hot_spans = jnp.stack([bucket_hot[d * LANES : (d + 2) * LANES] for d in range(spans)])

    rows_low = call(
        order_kernel,
        "order_tokens",
        shape_of((count, width), low_type),
        cost=(600, 5000),
        grid=(count // ROWS,),
        in_specs=[row_blocks((ROWS, width)), whole((width, width))],
        out_specs=row_blocks((ROWS, width)),
    )(tokens.reshape(count, width), order)
    if size != 16:
        weight_heads, weight_up, weight_down = (
            [gather_doubling(part, size)] for part in (packed_heads, packed_up, packed_down)
        )
        qkv, normed_first, vectors = project(rows_low, weight_heads, pairs, ())
    else:
        heads_line, packed_up = join(line_parts(packed_heads, size, "heads"), passing=(packed_up,))
        heads_sides = side_parts(heads_line, size, "heads")
        up_line_parts = line_parts(packed_up, size, "up")
        low, high = gather_step(*heads_sides, [], deps=(rows_low, *up_line_parts[1:]))
        heads_corner = corner_parts(low, high, size, "heads_corner")
        up_line, packed_down = join(up_line_parts, deps=heads_corner, passing=(packed_down,))
        up_sides = side_parts(up_line, size, "up")
        down_parts = line_parts(packed_down, size, "down")
        weight_heads = [heads_line, *heads_sides, *heads_corner]
        qkv, normed_first, vectors = project(
            rows_low, weight_heads, pairs, (same_tile, positive_tile)
        )
    filled = ()
    for pair in range(pairs):
        filled = attention(lengths, lines, qkv, pair, slot, before=filled)
        if pair == 0 and size == 16:
            low, high, down_line = gather_step(*up_sides, down_parts, deps=(filled[0],))
            up_corner = corner_parts(low, high, size, "up_corner")
            down_sides = side_parts(down_line, size, "down")
            weight_up = [up_line, *up_sides, *up_corner]
    turned_first = call(turn_kernel, "turn", shape_of((width, count), low_type))(normed_first)
    attended, probs, inverse = filled
    branch = branch_rows(
        attended, weight_heads, (*down_sides, *up_corner, turned_first) if size == 16 else ()
    )
    if size == 16:
        low, high = gather_step(*down_sides, [], deps=(branch,))
        down_corner = corner_parts(low, high, size, "down_corner")
        weight_down = [down_line, *down_sides, *down_corner]
    branch_came = other_core(branch, "branch_other_core")
    normed_second, slope, act_sum, middle_sum = hidden(
        lengths, rows_low, branch, branch_came, vectors, weight_up, slot
    )
    down = call(
        pool_kernel,
        "pool",
        shape_of((8, width), full_type),
        cost=(20, 5000),
        scratch_shapes=[pltpu.VMEM((width, inner), low_type)],
    )(act_sum, *weight_down)
    margin_tile, pooled = call(
        margin_kernel,
        "margin",
        [shape_of((8, LANES), full_type), shape_of((8, width), full_type)],
        grid=(1,),
        in_specs=[on_scalars(), *[whole(down.shape)] * 2, whole(middle_sum.shape), whole(vectors.shape)],
    )(lengths, down, other_core(down, "pooled_part_other_core"), middle_sum, vectors)
    margins = gather_small(margin_tile, size, "margins")

    d_line, d_act, small, d_normed_second = rank_back(
        lengths, margins, same_tile, positive_tile, pooled, vectors, act_sum,
        slope, weight_down, weight_up, slot, (turned_first,),
    )
    d_normed_second_came = other_core(d_normed_second, "second_gradient_other_core")
    up_sum = Scatter(
        up_grad(normed_second, slope, d_act, piece_rows(size, width), slot), size, "up_gradient"
    )
    d_middle, d_attended, g_out = middle_back(
        lengths, rows_low, branch, branch_came, d_normed_second, d_normed_second_came, vectors,
        d_line, attended, inverse, weight_heads, slot,
    )
    up_sum.sides(deps=(d_attended,))
    filled, tables = (), []
    for pair in range(pairs - 1):
        d_project, table, *g_early = attention_back(
            probs, qkv, d_attended, attended, turned_first, hot_spans, piece_rows(size, width),
            pair, slot, own, grad_out=g_out if pair == pairs - 2 else None, before=filled,
        )
        filled = (d_project, *g_early)
        tables.append(table)
    up_parts, _ = up_sum.line(deps=(d_project,))
    early_sum = Scatter(g_early, size, "early_gradient")
    d_project, table, *g_late = attention_back(
        probs, qkv, d_attended, attended, turned_first, hot_spans, piece_rows(size, width),
        pairs - 1, slot, own, tables=tuple(tables), before=(d_project,), deps=(up_parts[0],),
    )
    late_sum = Scatter(g_late, size, "late_gradient")
    early_sum.sides(deps=(table,))
    d_normed_first = normed_back(d_project, weight_heads, (*early_sum.sources, *up_parts[1:]))
    d_normed_first, small = late_sum.sides(passing=(d_normed_first, small))
    small = small_line(small, size, "small_sums")
    early_parts, _ = early_sum.line(deps=late_sum.sources)
    token_gradient = token_back(
        d_middle, d_normed_first, other_core(d_normed_first, "first_gradient_other_core"), rows_low,
        vectors, order, (early_parts[0],),
    )
    late_parts, (small,) = late_sum.line(deps=(token_gradient,), passing=(small,))
    small_all = small_plane(small, size, "small_sums")

    g_down, line, grad_sums = totals(
        small_all, [early_parts, late_parts, up_parts], heads_in, hidden_in, gains, tied_rows,
        (head_width * 3, 3 * LANES, inner), micro, (),
    )
    square_tile, extra = call(
        functools.partial(square_kernel, local_heads),
        "squares",
        [shape_of((24, LANES), full_type), shape_of((8, LANES), full_type)],
    )(line, other_core(line, "totals_other_core"))
    squares_all = gather_small(square_tile, size, "squares")
    step_float = step_count.astype(full_type)
    corrections = jnp.stack(
        [1.0 / (1.0 - beta_first**step_float), 1.0 / (1.0 - beta_second**step_float)]
    )
    grads = [*grad_sums, g_down]
    weights = (heads_in, heads_out, hidden_in, hidden_out, gains, tied_rows, bias_table)
    firsts = (
        first_heads_in,
        first_heads_out,
        first_hidden_in,
        first_hidden_out,
        first_gains,
        first_tied,
        first_table,
    )
    seconds = (
        second_heads_in,
        second_heads_out,
        second_hidden_in,
        second_hidden_out,
        second_gains,
        second_tied,
        second_table,
    )
    states = (*weights, *firsts, *seconds)
    first_place = jnp.sum(jnp.where(pair_ids == 0, jnp.arange(size, dtype=jnp.int32), 0)).reshape(1)
    norm, *results = update(first_place, corrections, extra, squares_all, grads, states)
    for index in (0, 7, 14):
        results[index] = turn_matrix(results[index])
        for other in (4, 5, 6):
            results[index + other] = results[index + other].T
    return (norm.reshape(()), token_gradient.reshape(tokens.shape), *results)


def solution(mesh):
    in_specs = (
        P(None, "dp", None, None),
        P(None, "dp"),
        P(),
        P(),
        P(),
        P("dp", None, "mp"),
        P("dp", "mp"),
        P("dp", "mp"),
        P("dp", "mp"),
        P("dp", None),
        P("dp", None),
        P(None, "mp"),
        P("dp", None, "mp"),
        P("dp", "mp"),
        P("dp", "mp"),
        P("dp", "mp"),
        P("dp", None),
        P("dp", None),
        P(None, "mp"),
        P("dp", None, "mp"),
        P("dp", "mp"),
        P("dp", "mp"),
        P("dp", "mp"),
        P("dp", None),
        P("dp", None),
        P(None, "mp"),
    )
    out_specs = (
        P(),
        P(None, "dp", None, None),
        P("dp", None, "mp"),
        P("dp", "mp"),
        P("dp", "mp"),
        P("dp", "mp"),
        P("dp", None),
        P("dp", None),
        P(None, "mp"),
        P("dp", None, "mp"),
        P("dp", "mp"),
        P("dp", "mp"),
        P("dp", "mp"),
        P("dp", None),
        P("dp", None),
        P(None, "mp"),
        P("dp", None, "mp"),
        P("dp", "mp"),
        P("dp", "mp"),
        P("dp", "mp"),
        P("dp", None),
        P("dp", None),
        P(None, "mp"),
    )
    return jax.shard_map(body, mesh=mesh, in_specs=in_specs, out_specs=out_specs, check_vma=False)
```

profile of v0, /device:TPU:0, one launch (start us, length us, event | category | flops | bytes accessed | tf_op | source)
XLA Modules:
  0.0 246.4 jit_solution(12597834409243628103)
XLA Ops:
  4.0 3.0 %collective-permute-start = (bf16[48,1664]{1,0:T(8,128)(2,1)S(1)}, bf16[48,1664]{1,0:T(8,128)(2,1)S(1)}, u32[]{:S(2)}, u32[]{:S(2)}) collective-permute-start(bf16[48,1664]{1,0:T(8,128)(2,1)S(1)} %pack_heads.1.refs_0_), channel_id=1, source_target_pairs={{0,8},{2,10},{4,12},{6,14},{8,0},{10,2},{12,4},{14,6},{16,24},{18,... | collective-permute-start | bytes 479240 | tf_op jit(solution)/shard_map/heads_across_4/ppermute | solution.py:137
  7.1 2.6 %collective-permute-start.1 = (bf16[48,1664]{1,0:T(8,128)(2,1)S(1)}, bf16[48,1664]{1,0:T(8,128)(2,1)S(1)}, u32[]{:S(2)}, u32[]{:S(2)}) collective-permute-start(bf16[48,1664]{1,0:T(8,128)(2,1)S(1)} %pack_heads.1.refs_0_), channel_id=1, source_target_pairs={{0,16},{2,18},{4,20},{6,22},{8,24},{10,26},{12,28},{14,30},{16,0},... | collective-permute-start | bytes 479240 | tf_op jit(solution)/shard_map/heads_across_8/ppermute | solution.py:137
  15.1 6.8 %collective-permute-done.1.refs_2_ = bf16[48,1664]{1,0:T(8,128)(2,1)S(1)} collective-permute-done((bf16[48,1664]{1,0:T(8,128)(2,1)S(1)}, bf16[48,1664]{1,0:T(8,128)(2,1)S(1)}, u32[]{:S(2)}, u32[]{:S(2)}) %collective-permute-start.1) | collective-permute-done | bytes 159776 | tf_op jit(solution)/shard_map/heads_across_8/ppermute | solution.py:137
  21.9 1.6 collective-permute-start.3
  23.5 1.5 collective-permute-start.4
  25.5 2.6 %collective-permute-start.5 = (bf16[48,1536]{1,0:T(8,128)(2,1)}, bf16[48,1536]{1,0:T(8,128)(2,1)S(1)}, u32[]{:S(2)}, u32[]{:S(2)}) collective-permute-start(bf16[48,1536]{1,0:T(8,128)(2,1)} %get-tuple-element.139.refs_0_), channel_id=1, source_target_pairs={{0,8},{2,10},{4,12},{6,14},{8,0},{10,2},{12,4},{14,6},{16,24},{18,... | collective-permute-start | bytes 442376 | tf_op jit(solution)/shard_map/up_across_4/ppermute | solution.py:137
  29.2 1.4 collective-permute-start.7
  30.6 1.4 copy-done.41
  32.0 1.9 order_tokens.1.refs_2_.refs_0_.refs_1_.refs_3_
  34.0 6.7 %collective-permute-done.6.refs_4_.refs_2_ = bf16[48,1536]{1,0:T(8,128)(2,1)S(1)} collective-permute-done((bf16[48,1536]{1,0:T(8,128)(2,1)}, bf16[48,1536]{1,0:T(8,128)(2,1)S(1)}, u32[]{:S(2)}, u32[]{:S(2)}) %collective-permute-start.6) | collective-permute-done | bytes 147488 | tf_op jit(solution)/shard_map/up_across_8/ppermute | solution.py:137
  42.9 5.0 %collective-permute-done.8.refs_4_.refs_13_ = bf16[96,1664]{1,0:T(8,128)(2,1)S(1)} collective-permute-done((bf16[96,1664]{1,0:T(8,128)(2,1)S(1)}, bf16[96,1664]{1,0:T(8,128)(2,1)S(1)}, u32[]{:S(2)}, u32[]{:S(2)}) %collective-permute-start.8) | collective-permute-done | bytes 319520 | tf_op jit(solution)/shard_map/heads_corner_across_1/ppermute | solution.py:137
  48.7 1.9 join.6
  51.8 1.5 collective-permute-start.11
  53.6 2.5 %collective-permute-start.12 = (bf16[48,1536]{1,0:T(8,128)(2,1)}, bf16[48,1536]{1,0:T(8,128)(2,1)}, u32[]{:S(2)}, u32[]{:S(2)}) collective-permute-start(bf16[48,1536]{1,0:T(8,128)(2,1)} %get-tuple-element.153.refs_2_), channel_id=1, source_target_pairs={{0,8},{2,10},{4,12},{6,14},{8,0},{10,2},{12,4},{14,6},{16,24},{18,... | collective-permute-start | bytes 442376 | tf_op jit(solution)/shard_map/down_across_4/ppermute | solution.py:137
  56.2 1.9 collective-permute-start.13
  58.0 1.4 collective-permute-start.14
  61.6 3.6 %projection.1 = (bf16[3,3,1024,128]{3,2,1,0:T(8,128)(2,1)S(1)}, bf16[1024,768]{1,0:T(8,128)(2,1)S(1)}, f32[8,768]{1,0:T(8,128)S(1)}) custom-call(bf16[1024,768]{1,0:T(8,128)(2,1)S(1)} %order_tokens.1.refs_2_.refs_0_.refs_1_.refs_3_, bf16[192,1664]{1,0:T(8,128)(2,1)S(1)} %get-tuple-element.138.refs_1_.refs_10_, ...), custom_call_target="tpu_custom_call" | custom-call | tf_op jit(solution)/shard_map/projection/pallas_call | solution.py:77
  65.2 3.5 %attention_forward.3 = (bf16[1024,384]{1,0:T(8,128)(2,1)S(1)}, bf16[3,2,2,512,512]{4,3,2,1,0:T(8,128)(2,1)S(1)}, f32[1024,384]{1,0:T(8,128)S(1)}) custom-call(s32[2]{0:T(128)S(1)} %bitcast.98, f32[3,2,1024]{2,1,0:T(2,128)S(1)} %reshape.86.refs_1_, bf16[3,3,1024,128]{3,2,1,0:T(8,128)(2,1)S(1)} %get-tuple-element.142.refs_2_.refs_1_), custom_call_target="tpu_custom_call" | custom-call | tf_op jit(solution)/shard_map/attention_forward/pallas_call | solution.py:77
  70.1 1.6 collective-permute-start.15
  72.2 1.5 collective-permute-start.17
  74.7 3.5 %attention_forward.4 = (bf16[1024,384]{1,0:T(8,128)(2,1)S(1)}, bf16[3,2,2,512,512]{4,3,2,1,0:T(8,128)(2,1)S(1)}, f32[1024,384]{1,0:T(8,128)S(1)}) custom-call(s32[2]{0:T(128)S(1)} %bitcast.99, f32[3,2,1024]{2,1,0:T(2,128)S(1)} %reshape.86.refs_1_, ...), custom_call_target="tpu_custom_call", output_to_operand_aliasing={{0}: (3, {}), {1}: (4, {}), {2}: (5, {})} | custom-call | tf_op jit(solution)/shard_map/attention_forward/pallas_call | solution.py:77
  78.2 3.5 %attention_forward.5 = (bf16[1024,384]{1,0:T(8,128)(2,1)S(1)}, bf16[3,2,2,512,512]{4,3,2,1,0:T(8,128)(2,1)S(1)}, f32[1024,384]{1,0:T(8,128)S(1)}) custom-call(s32[2]{0:T(128)S(1)} %bitcast.100, f32[3,2,1024]{2,1,0:T(2,128)S(1)} %reshape.86.refs_1_, ...), custom_call_target="tpu_custom_call", output_to_operand_aliasing={{0}: (3, {}), {1}: (4, {}), {2}: (5, {})} | custom-call | tf_op jit(solution)/shard_map/attention_forward/pallas_call | solution.py:77
  81.8 8.0 %collective-permute-done.17.refs_8_.refs_19_ = bf16[96,1536]{1,0:T(8,128)(2,1)S(1)} collective-permute-done((bf16[96,1536]{1,0:T(8,128)(2,1)S(1)}, bf16[96,1536]{1,0:T(8,128)(2,1)S(1)}, u32[]{:S(2)}, u32[]{:S(2)}) %collective-permute-start.17) | collective-permute-done | bytes 294944 | tf_op jit(solution)/shard_map/up_corner_across_1/ppermute | solution.py:137
  92.5 2.2 collective-permute-done.19.refs_3_
  94.7 10.8 %hidden_forward.1 = (bf16[1024,768]{1,0:T(8,128)(2,1)S(1)}, bf16[1024,1536]{1,0:T(8,128)(2,1)S(1)}, f32[2,1,1536]{2,1,0:T(1,128)S(1)}, f32[2,1,768]{2,1,0:T(1,128)S(1)}) custom-call(s32[2]{0:T(128)S(1)} %bitcast.101, bf16[1024,768]{1,0:T(8,128)(2,1)S(1)} %order_tokens.1.refs_2_.refs_0_.refs_1_.refs_3_, bf16[1024,768]{1,0:T(8,128)(2,1)S(1)} %branch.1.refs_2_, ...), custom_call_target="tpu_custom_call" | custom-call | flops 2400000000 | bytes 20000000 | tf_op jit(solution)/shard_map/hidden_forward/pallas_call | solution.py:77
  108.2 3.4 %collective-permute-start.23 = (f32[1,8,128]{2,1,0:T(8,128)S(1)}, f32[1,8,128]{2,1,0:T(8,128)S(1)}, u32[]{:S(2)}, u32[]{:S(2)}) collective-permute-start(f32[1,8,128]{2,1,0:T(8,128)S(1)} %bitcast.115), channel_id=1, source_target_pairs={{0,8},{2,10},{4,12},{6,14},{8,0},{10,2},{12,4},{14,6},{16,24},{18,... | collective-permute-start | bytes 12296 | tf_op jit(solution)/shard_map/margins_across_4/ppermute | solution.py:137
  111.6 2.0 collective-permute-start.24
  116.1 2.9 %collective-permute-done.25.refs_3_ = f32[1,8,128]{2,1,0:T(8,128)S(1)} collective-permute-done((f32[1,8,128]{2,1,0:T(8,128)S(1)}, f32[1,8,128]{2,1,0:T(8,128)S(1)}, u32[]{:S(2)}, u32[]{:S(2)}) %collective-permute-start.25) | collective-permute-done | bytes 4128 | tf_op jit(solution)/shard_map/margins_across_12/ppermute | solution.py:137
  120.0 2.4 collective-permute-start.28
  123.2 1.5 collective-permute-done.28.refs_10_
  124.7 5.0 %rank_backward.1 = (f32[8,768]{1,0:T(8,128)S(1)}, f32[8,1536]{1,0:T(8,128)S(1)}, f32[8,768]{1,0:T(8,128)S(1)}, bf16[1024,768]{1,0:T(8,128)(2,1)S(1)}) custom-call(s32[2]{0:T(128)S(1)} %bitcast.103, f32[16,8,128]{2,1,0:T(8,128)S(1)} %broadcast_in_dim.22.refs_6_.refs_1_, f32[8,128]{1,0:T(8,128)S(1)} %broadcast_in_dim.45.refs_7_.refs_2_, ...), custom_call_target="tpu_custom_call" | custom-call | flops 2400000000 | bytes 20000000 | tf_op jit(solution)/shard_map/rank_backward/pallas_call | solution.py:77
  129.8 3.9 %hidden_in_gradient.1 = (bf16[192,1536]{1,0:T(8,128)(2,1)S(1)}, bf16[192,1536]{1,0:T(8,128)(2,1)S(1)}, bf16[192,1536]{1,0:T(8,128)(2,1)S(1)}, bf16[96,1536]{1,0:T(8,128)(2,1)S(1)}, bf16[96,1536]{1,0:T(8,128)(2,1)S(1)}) custom-call(bf16[1024,768]{1,0:T(8,128)(2,1)S(1)} %get-tuple-element.180.refs_0_, ...), custom_call_target="tpu_custom_call" | custom-call | flops 2400000000 | bytes 15000000 | tf_op jit(solution)/shard_map/hidden_in_gradient/pallas_call | solution.py:77
  133.7 1.5 collective-permute-start.30
  135.3 1.5 collective-permute-start.31
  136.8 4.5 %middle_backward.1 = (f32[1024,768]{1,0:T(8,128)S(1)}, bf16[1024,384]{1,0:T(8,128)(2,1)S(1)}, f32[768,384]{1,0:T(8,128)S(1)}) custom-call(s32[2]{0:T(128)S(1)} %bitcast.104, bf16[1024,768]{1,0:T(8,128)(2,1)S(1)} %order_tokens.1.refs_2_.refs_0_.refs_1_.refs_3_, bf16[1024,768]{1,0:T(8,128)(2,1)S(1)} %branch.1.refs_2_, ...), custom_call_target="tpu_custom_call" | custom-call | flops 1200000000 | bytes 15000000 | tf_op jit(solution)/shard_map/middle_backward/pallas_call | solution.py:77
  141.3 1.9 collective-permute-done.30.refs_2_
  144.5 1.6 collective-permute-start.32
  146.7 6.1 %attention_backward.3 = (bf16[3,3,1024,128]{3,2,1,0:T(8,128)(2,1)S(1)}, f32[1,8,128]{2,1,0:T(8,128)S(1)}, bf16[192,1152]{1,0:T(8,128)(2,1)S(1)}, bf16[192,1152]{...) custom-call(bf16[3,2,2,512,512]{4,3,2,1,0:T(8,128)(2,1)S(1)} %get-tu, ...), custom_call_target="tpu_custom_call" | custom-call | tf_op jit(solution)/shard_map/attention_backward/pallas_call | solution.py:77
  152.8 6.5 %attention_backward.4 = (bf16[3,3,1024,128]{3,2,1,0:T(8,128)(2,1)S(1)}, f32[1,8,128]{2,1,0:T(8,128)S(1)}, bf16[192,1152]{1,0:T(8,128)(2,1)S(1)}, bf16[192,1152]{...) custom-call(bf16[3,2,2,512,512]{4,3,2,1,0:T(8,128)(2,1)S(1)} %get-tu, ...), custom_call_target="tpu_custom_call", output_to_operand_aliasing={{0}: (7, {}), {2}: (8, {}), {3}: (9, {}), {4}: (10, {}), {5... | custom-call | tf_op jit(solution)/shard_map/attention_backward/pallas_call | solution.py:77
  159.3 1.5 collective-permute-start.36
  161.7 1.8 collective-permute-start.39
  163.5 2.5 collective-permute-start.40
  166.0 6.2 %attention_backward.5 = (bf16[3,3,1024,128]{3,2,1,0:T(8,128)(2,1)S(1)}, f32[1,8,128]{2,1,0:T(8,128)S(1)}, bf16[192,512]{1,0:T(8,128)(2,1)S(1)}, bf16[192,512]{1,...) custom-call(bf16[3,2,2,512,512]{4,3,2,1,0:T(8,128)(2,1)S(1)} %get-tu, ...), custom_call_target="tpu_custom_call", output_to_operand_aliasing={{0}: (8, {})} | custom-call | tf_op jit(solution)/shard_map/attention_backward/pallas_call | solution.py:77
  172.9 1.5 collective-permute-start.35
  174.6 3.2 %normed_backward.1.refs_4_ = bf16[1024,768]{1,0:T(8,128)(2,1)S(1)} custom-call(bf16[3,3,1024,128]{3,2,1,0:T(8,128)(2,1)S(1)} %get-tuple-element.195.refs_0_, bf16[192,1664]{1,0:T(8,128)(2,1)S(1)} %get-tuple-element.138.refs_1_.refs_10_, bf16[192,1664]{1,0:T(8,128)(2,1)S(1)} %collective-permute-done.3.refs_0_.refs_2_.refs_11_, ...), custom_call_target="tpu_custom_call" | custom-call | flops 1800000000 | bytes 15000000 | tf_op jit(solution)/shard_map/normed_backward/pallas_call | solution.py:77
  178.0 1.6 collective-permute-start.44
  180.7 1.6 collective-permute-start.46
  182.6 1.9 collective-permute-done.46.refs_1_
  187.5 2.7 %collective-permute-done.48.refs_3_ = f32[1,8,768]{2,1,0:T(8,128)S(1)} collective-permute-done((f32[1,8,768]{2,1,0:T(8,128)S(1)}, f32[1,8,768]{2,1,0:T(8,128)S(1)}, u32[]{:S(2)}, u32[]{:S(2)}) %collective-permute-start.48) | collective-permute-done | bytes 24608 | tf_op jit(solution)/shard_map/small_sums_across_12/ppermute | solution.py:137
  191.1 1.4 collective-permute-done.45.refs_2_
  192.7 2.2 collective-permute-start.52
  194.9 2.4 collective-permute-start.54
  197.3 5.5 %token_gradient.1.refs_3_ = f32[1024,768]{1,0:T(8,128)} custom-call(f32[1024,768]{1,0:T(8,128)S(1)} %get-tuple-element.209.refs_0_, bf16[1024,768]{1,0:T(8,128)(2,1)S(1)} %get-tuple-element.210.refs_1_, bf16[1024,768]{1,0:T(8,128)(2,1)S(1)} %collective-permute-done.43.refs_2_, bf16[1024,768]{1,0:T(8,128)(2,1)S(1)} %order_tokens.1.refs_2_.refs_0_.refs_1_.refs_3_, ...), custom_call_target="tpu_custom_call" | custom-call | flops 2400000000 | bytes 15000000 | tf_op jit(solution)/shard_map/token_gradient/pallas_call | solution.py:77
  202.8 1.9 copy-done
  207.1 2.4 collective-permute-start.51
  210.4 2.4 collective-permute-start.57
  212.9 2.2 collective-permute-done.56.refs_10_
  216.4 1.6 gradient_totals.1
  219.9 3.0 %collective-permute-start.60 = (f32[1,24,128]{2,1,0:T(8,128)S(1)}, f32[1,24,128]{2,1,0:T(8,128)}, u32[]{:S(2)}, u32[]{:S(2)}) collective-permute-start(f32[1,24,128]{2,1,0:T(8,128)S(1)} %bitcast.106), channel_id=1, source_target_pairs={{0,16},{2,18},{4,20},{6,22},{8,24},{10,26},{12,28},{14,30},{16,0},... | collective-permute-start | bytes 36872 | tf_op jit(solution)/shard_map/squares_across_8/ppermute | solution.py:137
  222.9 1.4 collective-permute-start.61
  225.1 3.4 %collective-permute-done.61.refs_3_ = f32[1,24,128]{2,1,0:T(8,128)} collective-permute-done((f32[1,24,128]{2,1,0:T(8,128)S(1)}, f32[1,24,128]{2,1,0:T(8,128)}, u32[]{:S(2)}, u32[]{:S(2)}) %collective-permute-start.61) | collective-permute-done | bytes 12320 | tf_op jit(solution)/shard_map/squares_across_12/ppermute | solution.py:137
  231.0 1.7 collective-permute-start.64
  233.8 2.2 collective-permute-done.64.refs_6_
  242.3 4.0 %update.1 = (f32[1,1]{1,0:T(1,128)}, f32[3,48,384]{2,1,0:T(8,128)}, f32[48,384]{1,0:T(8,128)}, f32[48,1536]{1,0:T(8,128)}, f32[48,1536]{1,0:T(8,128)}, /*index=5...) custom-call(s32[1]{0:T(128)} %bitcast.refs_0_, ...), custom_call_target="tpu_custom_call" | custom-call | bytes 6000000 | tf_op jit(solution)/shard_map/update/pallas_call | solution.py:77
  (220 shorter events, 55.4 us)
Async XLA Ops:
  4.0 11.0 %collective-permute-start = (bf16[48,1664]{1,0:T(8,128)(2,1)S(1)}, bf16[48,1664]{1,0:T(8,128)(2,1)S(1)}, u32[]{:S(2)}, u32[]{:S(2)}) collective-permute-start(bf16[48,1664]{1,0:T(8,128)(2,1)S(1)} %pack_heads.1.refs_0_), channel_id=1, source_target_pairs={{0,8},{2,10},{4,12},{6,14},{8,0},{10,2},{12,4},{14,6},{16,24},{18,... | collective-permute-start | bytes 479240 | tf_op jit(solution)/shard_map/heads_across_4/ppermute | solution.py:137
  7.1 14.8 %collective-permute-start.1 = (bf16[48,1664]{1,0:T(8,128)(2,1)S(1)}, bf16[48,1664]{1,0:T(8,128)(2,1)S(1)}, u32[]{:S(2)}, u32[]{:S(2)}) collective-permute-start(bf16[48,1664]{1,0:T(8,128)(2,1)S(1)} %pack_heads.1.refs_0_), channel_id=1, source_target_pairs={{0,16},{2,18},{4,20},{6,22},{8,24},{10,26},{12,28},{14,30},{16,0},... | collective-permute-start | bytes 479240 | tf_op jit(solution)/shard_map/heads_across_8/ppermute | solution.py:137
  9.7 12.2 %collective-permute-start.2 = (bf16[48,1664]{1,0:T(8,128)(2,1)S(1)}, bf16[48,1664]{1,0:T(8,128)(2,1)S(1)}, u32[]{:S(2)}, u32[]{:S(2)}) collective-permute-start(bf16[48,1664]{1,0:T(8,128)(2,1)S(1)} %pack_heads.1.refs_0_), channel_id=1, source_target_pairs={{0,24},{2,26},{4,28},{6,30},{8,16},{10,18},{12,20},{14,22},{16,8},... | collective-permute-start | bytes 479240 | tf_op jit(solution)/shard_map/heads_across_12/ppermute | solution.py:137
  21.9 18.8 %collective-permute-start.3 = (bf16[192,1664]{1,0:T(8,128)(2,1)S(1)}, bf16[192,1664]{1,0:T(8,128)(2,1)S(1)}, u32[]{:S(2)}, u32[]{:S(2)}) collective-permute-start(bf16[192,1664]{1,0:T(8,128)(2,1)S(1)} %get-tuple-element.138.refs_1_.refs_10_), channel_id=1, source_target_pairs={{0,4},{2,6},{4,0},{6,2},{8,12},{10,14},{12,8},{14,10},{16,20},{18,... | collective-permute-start | bytes 1916936 | tf_op jit(solution)/shard_map/heads_across_2/ppermute | solution.py:137
  23.5 17.2 %collective-permute-start.4 = (bf16[192,1664]{1,0:T(8,128)(2,1)S(1)}, bf16[192,1664]{1,0:T(8,128)(2,1)S(1)}, u32[]{:S(2)}, u32[]{:S(2)}) collective-permute-start(bf16[192,1664]{1,0:T(8,128)(2,1)S(1)} %get-tuple-element.138.refs_1_.refs_10_), channel_id=1, source_target_pairs={{0,2},{2,0},{4,6},{6,4},{8,10},{10,8},{12,14},{14,12},{16,18},{18,... | collective-permute-start | bytes 1916936 | tf_op jit(solution)/shard_map/heads_across_1/ppermute | solution.py:137
  25.5 8.5 %collective-permute-start.5 = (bf16[48,1536]{1,0:T(8,128)(2,1)}, bf16[48,1536]{1,0:T(8,128)(2,1)S(1)}, u32[]{:S(2)}, u32[]{:S(2)}) collective-permute-start(bf16[48,1536]{1,0:T(8,128)(2,1)} %get-tuple-element.139.refs_0_), channel_id=1, source_target_pairs={{0,8},{2,10},{4,12},{6,14},{8,0},{10,2},{12,4},{14,6},{16,24},{18,... | collective-permute-start | bytes 442376 | tf_op jit(solution)/shard_map/up_across_4/ppermute | solution.py:137
  28.1 12.6 %collective-permute-start.6 = (bf16[48,1536]{1,0:T(8,128)(2,1)}, bf16[48,1536]{1,0:T(8,128)(2,1)S(1)}, u32[]{:S(2)}, u32[]{:S(2)}) collective-permute-start(bf16[48,1536]{1,0:T(8,128)(2,1)} %get-tuple-element.139.refs_0_), channel_id=1, source_target_pairs={{0,16},{2,18},{4,20},{6,22},{8,24},{10,26},{12,28},{14,30},{16,0},... | collective-permute-start | bytes 442376 | tf_op jit(solution)/shard_map/up_across_8/ppermute | solution.py:137
  29.2 11.5 %collective-permute-start.7 = (bf16[48,1536]{1,0:T(8,128)(2,1)}, bf16[48,1536]{1,0:T(8,128)(2,1)S(1)}, u32[]{:S(2)}, u32[]{:S(2)}) collective-permute-start(bf16[48,1536]{1,0:T(8,128)(2,1)} %get-tuple-element.139.refs_0_), channel_id=1, source_target_pairs={{0,24},{2,26},{4,28},{6,30},{8,16},{10,18},{12,20},{14,22},{16,8},... | collective-permute-start | bytes 442376 | tf_op jit(solution)/shard_map/up_across_12/ppermute | solution.py:137
  40.8 7.1 %collective-permute-start.8 = (bf16[96,1664]{1,0:T(8,128)(2,1)S(1)}, bf16[96,1664]{1,0:T(8,128)(2,1)S(1)}, u32[]{:S(2)}, u32[]{:S(2)}) collective-permute-start(bf16[96,1664]{1,0:T(8,128)(2,1)S(1)} %get-tuple-element.140), channel_id=1, source_target_pairs={{0,2},{2,0},{4,6},{6,4},{8,10},{10,8},{12,14},{14,12},{16,18},{18,... | collective-permute-start | bytes 958472 | tf_op jit(solution)/shard_map/heads_corner_across_1/ppermute | solution.py:137
  41.4 7.3 %collective-permute-start.9 = (bf16[96,1664]{1,0:T(8,128)(2,1)S(1)}, bf16[96,1664]{1,0:T(8,128)(2,1)S(1)}, u32[]{:S(2)}, u32[]{:S(2)}) collective-permute-start(bf16[96,1664]{1,0:T(8,128)(2,1)S(1)} %get-tuple-element.141), channel_id=1, source_target_pairs={{0,4},{2,6},{4,0},{6,2},{8,12},{10,14},{12,8},{14,10},{16,20},{18,... | collective-permute-start | bytes 958472 | tf_op jit(solution)/shard_map/heads_corner_across_2/ppermute | solution.py:137
  51.3 17.4 %collective-permute-start.10 = (bf16[192,1536]{1,0:T(8,128)(2,1)}, bf16[192,1536]{1,0:T(8,128)(2,1)}, u32[]{:S(2)}, u32[]{:S(2)}) collective-permute-start(bf16[192,1536]{1,0:T(8,128)(2,1)} %get-tuple-element.152.refs_5_.refs_16_), channel_id=1, source_target_pairs={{0,4},{2,6},{4,0},{6,2},{8,12},{10,14},{12,8},{14,10},{16,20},{18,... | collective-permute-start | bytes 1769480 | tf_op jit(solution)/shard_map/up_across_2/ppermute | solution.py:137
  51.8 16.9 %collective-permute-start.11 = (bf16[192,1536]{1,0:T(8,128)(2,1)}, bf16[192,1536]{1,0:T(8,128)(2,1)}, u32[]{:S(2)}, u32[]{:S(2)}) collective-permute-start(bf16[192,1536]{1,0:T(8,128)(2,1)} %get-tuple-element.152.refs_5_.refs_16_), channel_id=1, source_target_pairs={{0,2},{2,0},{4,6},{6,4},{8,10},{10,8},{12,14},{14,12},{16,18},{18,... | collective-permute-start | bytes 1769480 | tf_op jit(solution)/shard_map/up_across_1/ppermute | solution.py:137
  53.6 15.1 %collective-permute-start.12 = (bf16[48,1536]{1,0:T(8,128)(2,1)}, bf16[48,1536]{1,0:T(8,128)(2,1)}, u32[]{:S(2)}, u32[]{:S(2)}) collective-permute-start(bf16[48,1536]{1,0:T(8,128)(2,1)} %get-tuple-element.153.refs_2_), channel_id=1, source_target_pairs={{0,8},{2,10},{4,12},{6,14},{8,0},{10,2},{12,4},{14,6},{16,24},{18,... | collective-permute-start | bytes 442376 | tf_op jit(solution)/shard_map/down_across_4/ppermute | solution.py:137
  56.2 12.6 %collective-permute-start.13 = (bf16[48,1536]{1,0:T(8,128)(2,1)}, bf16[48,1536]{1,0:T(8,128)(2,1)}, u32[]{:S(2)}, u32[]{:S(2)}) collective-permute-start(bf16[48,1536]{1,0:T(8,128)(2,1)} %get-tuple-element.153.refs_2_), channel_id=1, source_target_pairs={{0,16},{2,18},{4,20},{6,22},{8,24},{10,26},{12,28},{14,30},{16,0},... | collective-permute-start | bytes 442376 | tf_op jit(solution)/shard_map/down_across_8/ppermute | solution.py:137
  58.0 10.7 %collective-permute-start.14 = (bf16[48,1536]{1,0:T(8,128)(2,1)}, bf16[48,1536]{1,0:T(8,128)(2,1)}, u32[]{:S(2)}, u32[]{:S(2)}) collective-permute-start(bf16[48,1536]{1,0:T(8,128)(2,1)} %get-tuple-element.153.refs_2_), channel_id=1, source_target_pairs={{0,24},{2,26},{4,28},{6,30},{8,16},{10,18},{12,20},{14,22},{16,8},... | collective-permute-start | bytes 442376 | tf_op jit(solution)/shard_map/down_across_12/ppermute | solution.py:137
  70.1 19.7 %collective-permute-start.15 = (bf16[192,1536]{1,0:T(8,128)(2,1)S(1)}, bf16[192,1536]{1,0:T(8,128)(2,1)S(1)}, u32[]{:S(2)}, u32[]{:S(2)}) collective-permute-start(bf16[192,1536]{1,0:T(8,128)(2,1)S(1)} %get-tuple-element.154.refs_1_.refs_11_), channel_id=1, source_target_pairs={{0,4},{2,6},{4,0},{6,2},{8,12},{10,14},{12,8},{14,10},{16,20},{18,... | collective-permute-start | bytes 1769480 | tf_op jit(solution)/shard_map/down_across_2/ppermute | solution.py:137
  71.7 18.1 %collective-permute-start.16 = (bf16[192,1536]{1,0:T(8,128)(2,1)S(1)}, bf16[192,1536]{1,0:T(8,128)(2,1)S(1)}, u32[]{:S(2)}, u32[]{:S(2)}) collective-permute-start(bf16[192,1536]{1,0:T(8,128)(2,1)S(1)} %get-tuple-element.154.refs_1_.refs_11_), channel_id=1, source_target_pairs={{0,2},{2,0},{4,6},{6,4},{8,10},{10,8},{12,14},{14,12},{16,18},{18,... | collective-permute-start | bytes 1769480 | tf_op jit(solution)/shard_map/down_across_1/ppermute | solution.py:137
  72.2 17.6 %collective-permute-start.17 = (bf16[96,1536]{1,0:T(8,128)(2,1)S(1)}, bf16[96,1536]{1,0:T(8,128)(2,1)S(1)}, u32[]{:S(2)}, u32[]{:S(2)}) collective-permute-start(bf16[96,1536]{1,0:T(8,128)(2,1)S(1)} %get-tuple-element.155), channel_id=1, source_target_pairs={{0,2},{2,0},{4,6},{6,4},{8,10},{10,8},{12,14},{14,12},{16,18},{18,... | collective-permute-start | bytes 884744 | tf_op jit(solution)/shard_map/up_corner_across_1/ppermute | solution.py:137
  73.7 16.1 %collective-permute-start.18 = (bf16[96,1536]{1,0:T(8,128)(2,1)S(1)}, bf16[96,1536]{1,0:T(8,128)(2,1)S(1)}, u32[]{:S(2)}, u32[]{:S(2)}) collective-permute-start(bf16[96,1536]{1,0:T(8,128)(2,1)S(1)} %get-tuple-element.156), channel_id=1, source_target_pairs={{0,4},{2,6},{4,0},{6,2},{8,12},{10,14},{12,8},{14,10},{16,20},{18,... | collective-permute-start | bytes 884744 | tf_op jit(solution)/shard_map/up_corner_across_2/ppermute | solution.py:137
  91.2 3.5 %collective-permute-start.19 = (bf16[1024,768]{1,0:T(8,128)(2,1)S(1)}, bf16[1024,768]{1,0:T(8,128)(2,1)S(1)}, u32[]{:S(2)}, u32[]{:S(2)}) collective-permute-start(bf16[1024,768]{1,0:T(8,128)(2,1)S(1)} %branch.1.refs_2_), channel_id=1, source_target_pairs={{0,1},{1,0},{2,3},{3,2},{4,5},{5,4},{6,7},{7,6},{8,9},{9,8},{10,11... | collective-permute-start | bytes 4718600 | tf_op jit(solution)/shard_map/branch_other_core/ppermute | solution.py:142
  91.3 14.2 %collective-permute-start.20 = (bf16[96,1536]{1,0:T(8,128)(2,1)S(1)}, bf16[96,1536]{1,0:T(8,128)(2,1)S(1)}, u32[]{:S(2)}, u32[]{:S(2)}) collective-permute-start(bf16[96,1536]{1,0:T(8,128)(2,1)S(1)} %get-tuple-element.160), channel_id=1, source_target_pairs={{0,2},{2,0},{4,6},{6,4},{8,10},{10,8},{12,14},{14,12},{16,18},{18,... | collective-permute-start | bytes 884744 | tf_op jit(solution)/shard_map/down_corner_across_1/ppermute | solution.py:137
  91.9 13.6 %collective-permute-start.21 = (bf16[96,1536]{1,0:T(8,128)(2,1)S(1)}, bf16[96,1536]{1,0:T(8,128)(2,1)S(1)}, u32[]{:S(2)}, u32[]{:S(2)}) collective-permute-start(bf16[96,1536]{1,0:T(8,128)(2,1)S(1)} %get-tuple-element.161), channel_id=1, source_target_pairs={{0,4},{2,6},{4,0},{6,2},{8,12},{10,14},{12,8},{14,10},{16,20},{18,... | collective-permute-start | bytes 884744 | tf_op jit(solution)/shard_map/down_corner_across_2/ppermute | solution.py:137
  106.2 1.2 collective-permute-start.22
  108.2 6.8 %collective-permute-start.23 = (f32[1,8,128]{2,1,0:T(8,128)S(1)}, f32[1,8,128]{2,1,0:T(8,128)S(1)}, u32[]{:S(2)}, u32[]{:S(2)}) collective-permute-start(f32[1,8,128]{2,1,0:T(8,128)S(1)} %bitcast.115), channel_id=1, source_target_pairs={{0,8},{2,10},{4,12},{6,14},{8,0},{10,2},{12,4},{14,6},{16,24},{18,... | collective-permute-start | bytes 12296 | tf_op jit(solution)/shard_map/margins_across_4/ppermute | solution.py:137
  111.6 4.5 %collective-permute-start.24 = (f32[1,8,128]{2,1,0:T(8,128)S(1)}, f32[1,8,128]{2,1,0:T(8,128)S(1)}, u32[]{:S(2)}, u32[]{:S(2)}) collective-permute-start(f32[1,8,128]{2,1,0:T(8,128)S(1)} %bitcast.116), channel_id=1, source_target_pairs={{0,16},{2,18},{4,20},{6,22},{8,24},{10,26},{12,28},{14,30},{16,0},... | collective-permute-start | bytes 12296 | tf_op jit(solution)/shard_map/margins_across_8/ppermute | solution.py:137
  113.6 5.4 %collective-permute-start.25 = (f32[1,8,128]{2,1,0:T(8,128)S(1)}, f32[1,8,128]{2,1,0:T(8,128)S(1)}, u32[]{:S(2)}, u32[]{:S(2)}) collective-permute-start(f32[1,8,128]{2,1,0:T(8,128)S(1)} %bitcast.117), channel_id=1, source_target_pairs={{0,24},{2,26},{4,28},{6,30},{8,16},{10,18},{12,20},{14,22},{16,8},... | collective-permute-start | bytes 12296 | tf_op jit(solution)/shard_map/margins_across_12/ppermute | solution.py:137
  119.0 3.7 %collective-permute-start.26 = (f32[4,8,128]{2,1,0:T(8,128)S(1)}, f32[4,8,128]{2,1,0:T(8,128)S(1)}, u32[]{:S(2)}, u32[]{:S(2)}) collective-permute-start(f32[4,8,128]{2,1,0:T(8,128)S(1)} %join.7.refs_7_), channel_id=1, source_target_pairs={{0,4},{2,6},{4,0},{6,2},{8,12},{10,14},{12,8},{14,10},{16,20},{18,... | collective-permute-start | bytes 49160 | tf_op jit(solution)/shard_map/margins_across_2/ppermute | solution.py:137
  119.5 3.7 %collective-permute-start.27 = (f32[4,8,128]{2,1,0:T(8,128)S(1)}, f32[4,8,128]{2,1,0:T(8,128)S(1)}, u32[]{:S(2)}, u32[]{:S(2)}) collective-permute-start(f32[4,8,128]{2,1,0:T(8,128)S(1)} %join.7.refs_7_), channel_id=1, source_target_pairs={{0,2},{2,0},{4,6},{6,4},{8,10},{10,8},{12,14},{14,12},{16,18},{18,... | collective-permute-start | bytes 49160 | tf_op jit(solution)/shard_map/margins_across_1/ppermute | solution.py:137
  120.0 4.6 %collective-permute-start.28 = (f32[4,8,128]{2,1,0:T(8,128)S(1)}, f32[4,8,128]{2,1,0:T(8,128)S(1)}, u32[]{:S(2)}, u32[]{:S(2)}) collective-permute-start(f32[4,8,128]{2,1,0:T(8,128)S(1)} %join.7.refs_7_), channel_id=1, source_target_pairs={{0,6},{2,4},{4,2},{6,0},{8,14},{10,12},{12,10},{14,8},{16,22},{18,... | collective-permute-start | bytes 49160 | tf_op jit(solution)/shard_map/margins_across_3/ppermute | solution.py:137
  129.7 7.1 %collective-permute-start.29 = (bf16[1024,768]{1,0:T(8,128)(2,1)S(1)}, bf16[1024,768]{1,0:T(8,128)(2,1)S(1)}, u32[]{:S(2)}, u32[]{:S(2)}) collective-permute-start(bf16[1024,768]{1,0:T(8,128)(2,1)S(1)} %get-tuple-element.166.refs_4_), channel_id=1, source_target_pairs={{0,1},{1,0},{2,3},{3,2},{4,5},{5,4},{6,7},{7,6},{8,9},{9,8},{10,11... | collective-permute-start | bytes 4718600 | tf_op jit(solution)/shard_map/second_gradient_other_core/ppermute | solution.py:142
  133.7 9.5 %collective-permute-start.30 = (bf16[96,1536]{1,0:T(8,128)(2,1)S(1)}, bf16[96,1536]{1,0:T(8,128)(2,1)S(1)}, u32[]{:S(2)}, u32[]{:S(2)}) collective-permute-start(bf16[96,1536]{1,0:T(8,128)(2,1)S(1)} %get-tuple-element.185), channel_id=1, source_target_pairs={{0,2},{2,0},{4,6},{6,4},{8,10},{10,8},{12,14},{14,12},{16,18},{18,... | collective-permute-start | bytes 884744 | tf_op jit(solution)/shard_map/up_gradient_across_1/ppermute | solution.py:137
  135.3 9.1 %collective-permute-start.31 = (bf16[96,1536]{1,0:T(8,128)(2,1)S(1)}, bf16[96,1536]{1,0:T(8,128)(2,1)S(1)}, u32[]{:S(2)}, u32[]{:S(2)}) collective-permute-start(bf16[96,1536]{1,0:T(8,128)(2,1)S(1)} %get-tuple-element.186), channel_id=1, source_target_pairs={{0,4},{2,6},{4,0},{6,2},{8,12},{10,14},{12,8},{14,10},{16,20},{18,... | collective-permute-start | bytes 884744 | tf_op jit(solution)/shard_map/up_gradient_across_2/ppermute | solution.py:137
  144.5 16.8 %collective-permute-start.32 = (bf16[192,1536]{1,0:T(8,128)(2,1)S(1)}, bf16[192,1536]{1,0:T(8,128)(2,1)S(1)}, u32[]{:S(2)}, u32[]{:S(2)}) collective-permute-start(bf16[192,1536]{1,0:T(8,128)(2,1)S(1)} %get-tuple-element.187), channel_id=1, source_target_pairs={{0,4},{2,6},{4,0},{6,2},{8,12},{10,14},{12,8},{14,10},{16,20},{18,... | collective-permute-start | bytes 1769480 | tf_op jit(solution)/shard_map/up_gradient_across_2/ppermute | solution.py:137
  146.1 15.2 %collective-permute-start.33 = (bf16[192,1536]{1,0:T(8,128)(2,1)S(1)}, bf16[192,1536]{1,0:T(8,128)(2,1)S(1)}, u32[]{:S(2)}, u32[]{:S(2)}) collective-permute-start(bf16[192,1536]{1,0:T(8,128)(2,1)S(1)} %get-tuple-element.188), channel_id=1, source_target_pairs={{0,2},{2,0},{4,6},{6,4},{8,10},{10,8},{12,14},{14,12},{16,18},{18,... | collective-permute-start | bytes 1769480 | tf_op jit(solution)/shard_map/up_gradient_across_1/ppermute | solution.py:137
  159.3 13.0 %collective-permute-start.36 = (bf16[96,1152]{1,0:T(8,128)(2,1)S(1)}, bf16[96,1152]{1,0:T(8,128)(2,1)S(1)}, u32[]{:S(2)}, u32[]{:S(2)}) collective-permute-start(bf16[96,1152]{1,0:T(8,128)(2,1)S(1)} %get-tuple-element.198), channel_id=1, source_target_pairs={{0,2},{2,0},{4,6},{6,4},{8,10},{10,8},{12,14},{14,12},{16,18},{18,... | collective-permute-start | bytes 663560 | tf_op jit(solution)/shard_map/early_gradient_across_1/ppermute | solution.py:137
  160.8 12.1 %collective-permute-start.37 = (bf16[96,1152]{1,0:T(8,128)(2,1)S(1)}, bf16[96,1152]{1,0:T(8,128)(2,1)S(1)}, u32[]{:S(2)}, u32[]{:S(2)}) collective-permute-start(bf16[96,1152]{1,0:T(8,128)(2,1)S(1)} %get-tuple-element.199), channel_id=1, source_target_pairs={{0,4},{2,6},{4,0},{6,2},{8,12},{10,14},{12,8},{14,10},{16,20},{18,... | collective-permute-start | bytes 663560 | tf_op jit(solution)/shard_map/early_gradient_across_2/ppermute | solution.py:137
  161.5 13.0 %collective-permute-start.38 = (bf16[48,1536]{1,0:T(8,128)(2,1)S(1)}, bf16[48,1536]{1,0:T(8,128)(2,1)S(1)}, u32[]{:S(2)}, u32[]{:S(2)}) collective-permute-start(bf16[48,1536]{1,0:T(8,128)(2,1)S(1)} %get-tuple-element.203), channel_id=1, source_target_pairs={{0,8},{2,10},{4,12},{6,14},{8,0},{10,2},{12,4},{14,6},{16,24},{18,... | collective-permute-start | bytes 442376 | tf_op jit(solution)/shard_map/up_gradient_across_4/ppermute | solution.py:137
  161.7 12.8 %collective-permute-start.39 = (bf16[48,1536]{1,0:T(8,128)(2,1)S(1)}, bf16[48,1536]{1,0:T(8,128)(2,1)S(1)}, u32[]{:S(2)}, u32[]{:S(2)}) collective-permute-start(bf16[48,1536]{1,0:T(8,128)(2,1)S(1)} %get-tuple-element.204), channel_id=1, source_target_pairs={{0,16},{2,18},{4,20},{6,22},{8,24},{10,26},{12,28},{14,30},{16,0},... | collective-permute-start | bytes 442376 | tf_op jit(solution)/shard_map/up_gradient_across_8/ppermute | solution.py:137
  163.5 11.0 %collective-permute-start.40 = (bf16[48,1536]{1,0:T(8,128)(2,1)S(1)}, bf16[48,1536]{1,0:T(8,128)(2,1)S(1)}, u32[]{:S(2)}, u32[]{:S(2)}) collective-permute-start(bf16[48,1536]{1,0:T(8,128)(2,1)S(1)} %get-tuple-element.205), channel_id=1, source_target_pairs={{0,24},{2,26},{4,28},{6,30},{8,16},{10,18},{12,20},{14,22},{16,8},... | collective-permute-start | bytes 442376 | tf_op jit(solution)/shard_map/up_gradient_across_12/ppermute | solution.py:137
  172.2 5.5 %collective-permute-start.34 = (bf16[96,512]{1,0:T(8,128)(2,1)S(1)}, bf16[96,512]{1,0:T(8,128)(2,1)S(1)}, u32[]{:S(2)}, u32[]{:S(2)}) collective-permute-start(bf16[96,512]{1,0:T(8,128)(2,1)S(1)} %get-tuple-element.193), channel_id=1, source_target_pairs={{0,2},{2,0},{4,6},{6,4},{8,10},{10,8},{12,14},{14,12},{16,18},{18,... | collective-permute-start | bytes 294920 | tf_op jit(solution)/shard_map/late_gradient_across_1/ppermute | solution.py:137
  172.9 4.9 %collective-permute-start.35 = (bf16[96,512]{1,0:T(8,128)(2,1)S(1)}, bf16[96,512]{1,0:T(8,128)(2,1)S(1)}, u32[]{:S(2)}, u32[]{:S(2)}) collective-permute-start(bf16[96,512]{1,0:T(8,128)(2,1)S(1)} %get-tuple-element.194), channel_id=1, source_target_pairs={{0,4},{2,6},{4,0},{6,2},{8,12},{10,14},{12,8},{14,10},{16,20},{18,... | collective-permute-start | bytes 294920 | tf_op jit(solution)/shard_map/late_gradient_across_2/ppermute | solution.py:137
  177.9 17.0 %collective-permute-start.43 = (bf16[1024,768]{1,0:T(8,128)(2,1)S(1)}, bf16[1024,768]{1,0:T(8,128)(2,1)S(1)}, u32[]{:S(2)}, u32[]{:S(2)}) collective-permute-start(bf16[1024,768]{1,0:T(8,128)(2,1)S(1)} %get-tuple-element.210.refs_1_), channel_id=1, source_target_pairs={{0,1},{1,0},{2,3},{3,2},{4,5},{5,4},{6,7},{7,6},{8,9},{9,8},{10,11... | collective-permute-start | bytes 4718600 | tf_op jit(solution)/shard_map/first_gradient_other_core/ppermute | solution.py:142
  178.0 13.2 %collective-permute-start.44 = (bf16[192,1152]{1,0:T(8,128)(2,1)S(1)}, bf16[192,1152]{1,0:T(8,128)(2,1)S(1)}, u32[]{:S(2)}, u32[]{:S(2)}) collective-permute-start(bf16[192,1152]{1,0:T(8,128)(2,1)S(1)} %get-tuple-element.201.refs_6_), channel_id=1, source_target_pairs={{0,4},{2,6},{4,0},{6,2},{8,12},{10,14},{12,8},{14,10},{16,20},{18,... | collective-permute-start | bytes 1327112 | tf_op jit(solution)/shard_map/early_gradient_across_2/ppermute | solution.py:137
  179.5 13.0 %collective-permute-start.45 = (bf16[192,1152]{1,0:T(8,128)(2,1)S(1)}, bf16[192,1152]{1,0:T(8,128)(2,1)S(1)}, u32[]{:S(2)}, u32[]{:S(2)}) collective-permute-start(bf16[192,1152]{1,0:T(8,128)(2,1)S(1)} %get-tuple-element.202.refs_7_), channel_id=1, source_target_pairs={{0,2},{2,0},{4,6},{6,4},{8,10},{10,8},{12,14},{14,12},{16,18},{18,... | collective-permute-start | bytes 1327112 | tf_op jit(solution)/shard_map/early_gradient_across_1/ppermute | solution.py:137
  180.7 3.8 %collective-permute-start.46 = (f32[1,8,768]{2,1,0:T(8,128)S(1)}, f32[1,8,768]{2,1,0:T(8,128)S(1)}, u32[]{:S(2)}, u32[]{:S(2)}) collective-permute-start(f32[1,8,768]{2,1,0:T(8,128)S(1)} %bitcast.91), channel_id=1, source_target_pairs={{0,8},{2,10},{4,12},{6,14},{8,0},{10,2},{12,4},{14,6},{16,24},{18,... | collective-permute-start | bytes 73736 | tf_op jit(solution)/shard_map/small_sums_across_4/ppermute | solution.py:137
  182.3 4.9 %collective-permute-start.47 = (f32[1,8,768]{2,1,0:T(8,128)S(1)}, f32[1,8,768]{2,1,0:T(8,128)S(1)}, u32[]{:S(2)}, u32[]{:S(2)}) collective-permute-start(f32[1,8,768]{2,1,0:T(8,128)S(1)} %bitcast.92), channel_id=1, source_target_pairs={{0,16},{2,18},{4,20},{6,22},{8,24},{10,26},{12,28},{14,30},{16,0},... | collective-permute-start | bytes 73736 | tf_op jit(solution)/shard_map/small_sums_across_8/ppermute | solution.py:137
  184.5 5.6 %collective-permute-start.48 = (f32[1,8,768]{2,1,0:T(8,128)S(1)}, f32[1,8,768]{2,1,0:T(8,128)S(1)}, u32[]{:S(2)}, u32[]{:S(2)}) collective-permute-start(f32[1,8,768]{2,1,0:T(8,128)S(1)} %bitcast.93), channel_id=1, source_target_pairs={{0,24},{2,26},{4,28},{6,30},{8,16},{10,18},{12,20},{14,22},{16,8},... | collective-permute-start | bytes 73736 | tf_op jit(solution)/shard_map/small_sums_across_12/ppermute | solution.py:137
  187.1 15.7 %collective-permute-start.41 = (bf16[192,512]{1,0:T(8,128)(2,1)S(1)}, bf16[192,512]{1,0:T(8,128)(2,1)S(1)}, u32[]{:S(2)}, u32[]{:S(2)}) collective-permute-start(bf16[192,512]{1,0:T(8,128)(2,1)S(1)} %get-tuple-element.207.refs_3_), channel_id=1, source_target_pairs={{0,4},{2,6},{4,0},{6,2},{8,12},{10,14},{12,8},{14,10},{16,20},{18,... | collective-permute-start | bytes 589832 | tf_op jit(solution)/shard_map/late_gradient_across_2/ppermute | solution.py:137
  190.1 12.7 %collective-permute-start.42 = (bf16[192,512]{1,0:T(8,128)(2,1)S(1)}, bf16[192,512]{1,0:T(8,128)(2,1)S(1)}, u32[]{:S(2)}, u32[]{:S(2)}) collective-permute-start(bf16[192,512]{1,0:T(8,128)(2,1)S(1)} %get-tuple-element.208.refs_4_), channel_id=1, source_target_pairs={{0,2},{2,0},{4,6},{6,4},{8,10},{10,8},{12,14},{14,12},{16,18},{18,... | collective-permute-start | bytes 589832 | tf_op jit(solution)/shard_map/late_gradient_across_1/ppermute | solution.py:137
  192.7 13.8 %collective-permute-start.52 = (bf16[48,1152]{1,0:T(8,128)(2,1)S(1)}, bf16[48,1152]{1,0:T(8,128)(2,1)S(1)}, u32[]{:S(2)}, u32[]{:S(2)}) collective-permute-start(bf16[48,1152]{1,0:T(8,128)(2,1)S(1)} %get-tuple-element.215), channel_id=1, source_target_pairs={{0,8},{2,10},{4,12},{6,14},{8,0},{10,2},{12,4},{14,6},{16,24},{18,... | collective-permute-start | bytes 331784 | tf_op jit(solution)/shard_map/early_gradient_across_4/ppermute | solution.py:137
  194.9 12.2 %collective-permute-start.53 = (bf16[48,1152]{1,0:T(8,128)(2,1)S(1)}, bf16[48,1152]{1,0:T(8,128)(2,1)S(1)}, u32[]{:S(2)}, u32[]{:S(2)}) collective-permute-start(bf16[48,1152]{1,0:T(8,128)(2,1)S(1)} %get-tuple-element.216), channel_id=1, source_target_pairs={{0,16},{2,18},{4,20},{6,22},{8,24},{10,26},{12,28},{14,30},{16,0},... | collective-permute-start | bytes 331784 | tf_op jit(solution)/shard_map/early_gradient_across_8/ppermute | solution.py:137
  194.9 14.6 %collective-permute-start.54 = (bf16[48,1152]{1,0:T(8,128)(2,1)S(1)}, bf16[48,1152]{1,0:T(8,128)(2,1)S(1)}, u32[]{:S(2)}, u32[]{:S(2)}) collective-permute-start(bf16[48,1152]{1,0:T(8,128)(2,1)S(1)} %get-tuple-element.217), channel_id=1, source_target_pairs={{0,24},{2,26},{4,28},{6,30},{8,16},{10,18},{12,20},{14,22},{16,8},... | collective-permute-start | bytes 331784 | tf_op jit(solution)/shard_map/early_gradient_across_12/ppermute | solution.py:137
  204.9 5.5 %collective-permute-start.55 = (bf16[48,512]{1,0:T(8,128)(2,1)S(1)}, bf16[48,512]{1,0:T(8,128)(2,1)S(1)}, u32[]{:S(2)}, u32[]{:S(2)}) collective-permute-start(bf16[48,512]{1,0:T(8,128)(2,1)S(1)} %get-tuple-element.219), channel_id=1, source_target_pairs={{0,8},{2,10},{4,12},{6,14},{8,0},{10,2},{12,4},{14,6},{16,24},{18,... | collective-permute-start | bytes 147464 | tf_op jit(solution)/shard_map/late_gradient_across_4/ppermute | solution.py:137
  206.0 10.3 %collective-permute-start.49 = (f32[4,8,768]{2,1,0:T(8,128)S(1)}, f32[4,8,768]{2,1,0:T(8,128)S(1)}, u32[]{:S(2)}, u32[]{:S(2)}) collective-permute-start(f32[4,8,768]{2,1,0:T(8,128)S(1)} %get-tuple-element.214.refs_0_), channel_id=1, source_target_pairs={{0,4},{2,6},{4,0},{6,2},{8,12},{10,14},{12,8},{14,10},{16,20},{18,... | collective-permute-start | bytes 294920 | tf_op jit(solution)/shard_map/small_sums_across_2/ppermute | solution.py:137
  206.5 9.8 %collective-permute-start.50 = (f32[4,8,768]{2,1,0:T(8,128)S(1)}, f32[4,8,768]{2,1,0:T(8,128)S(1)}, u32[]{:S(2)}, u32[]{:S(2)}) collective-permute-start(f32[4,8,768]{2,1,0:T(8,128)S(1)} %get-tuple-element.214.refs_0_), channel_id=1, source_target_pairs={{0,2},{2,0},{4,6},{6,4},{8,10},{10,8},{12,14},{14,12},{16,18},{18,... | collective-permute-start | bytes 294920 | tf_op jit(solution)/shard_map/small_sums_across_1/ppermute | solution.py:137
  207.1 9.2 %collective-permute-start.51 = (f32[4,8,768]{2,1,0:T(8,128)S(1)}, f32[4,8,768]{2,1,0:T(8,128)S(1)}, u32[]{:S(2)}, u32[]{:S(2)}) collective-permute-start(f32[4,8,768]{2,1,0:T(8,128)S(1)} %get-tuple-element.214.refs_0_), channel_id=1, source_target_pairs={{0,6},{2,4},{4,2},{6,0},{8,14},{10,12},{12,10},{14,8},{16,22},{18,... | collective-permute-start | bytes 294920 | tf_op jit(solution)/shard_map/small_sums_across_3/ppermute | solution.py:137
  209.5 5.5 %collective-permute-start.56 = (bf16[48,512]{1,0:T(8,128)(2,1)S(1)}, bf16[48,512]{1,0:T(8,128)(2,1)S(1)}, u32[]{:S(2)}, u32[]{:S(2)}) collective-permute-start(bf16[48,512]{1,0:T(8,128)(2,1)S(1)} %get-tuple-element.220), channel_id=1, source_target_pairs={{0,16},{2,18},{4,20},{6,22},{8,24},{10,26},{12,28},{14,30},{16,0},... | collective-permute-start | bytes 147464 | tf_op jit(solution)/shard_map/late_gradient_across_8/ppermute | solution.py:137
  210.4 5.9 %collective-permute-start.57 = (bf16[48,512]{1,0:T(8,128)(2,1)S(1)}, bf16[48,512]{1,0:T(8,128)(2,1)S(1)}, u32[]{:S(2)}, u32[]{:S(2)}) collective-permute-start(bf16[48,512]{1,0:T(8,128)(2,1)S(1)} %get-tuple-element.221), channel_id=1, source_target_pairs={{0,24},{2,26},{4,28},{6,30},{8,16},{10,18},{12,20},{14,22},{16,8},... | collective-permute-start | bytes 147464 | tf_op jit(solution)/shard_map/late_gradient_across_12/ppermute | solution.py:137
  219.9 5.2 %collective-permute-start.59 = (f32[1,24,128]{2,1,0:T(8,128)S(1)}, f32[1,24,128]{2,1,0:T(8,128)}, u32[]{:S(2)}, u32[]{:S(2)}) collective-permute-start(f32[1,24,128]{2,1,0:T(8,128)S(1)} %bitcast.105), channel_id=1, source_target_pairs={{0,8},{2,10},{4,12},{6,14},{8,0},{10,2},{12,4},{14,6},{16,24},{18,... | collective-permute-start | bytes 36872 | tf_op jit(solution)/shard_map/squares_across_4/ppermute | solution.py:137
  219.9 5.2 %collective-permute-start.60 = (f32[1,24,128]{2,1,0:T(8,128)S(1)}, f32[1,24,128]{2,1,0:T(8,128)}, u32[]{:S(2)}, u32[]{:S(2)}) collective-permute-start(f32[1,24,128]{2,1,0:T(8,128)S(1)} %bitcast.106), channel_id=1, source_target_pairs={{0,16},{2,18},{4,20},{6,22},{8,24},{10,26},{12,28},{14,30},{16,0},... | collective-permute-start | bytes 36872 | tf_op jit(solution)/shard_map/squares_across_8/ppermute | solution.py:137
  222.9 5.6 %collective-permute-start.61 = (f32[1,24,128]{2,1,0:T(8,128)S(1)}, f32[1,24,128]{2,1,0:T(8,128)}, u32[]{:S(2)}, u32[]{:S(2)}) collective-permute-start(f32[1,24,128]{2,1,0:T(8,128)S(1)} %bitcast.107), channel_id=1, source_target_pairs={{0,24},{2,26},{4,28},{6,30},{8,16},{10,18},{12,20},{14,22},{16,8},... | collective-permute-start | bytes 36872 | tf_op jit(solution)/shard_map/squares_across_12/ppermute | solution.py:137
  229.2 4.3 %collective-permute-start.62 = (f32[4,24,128]{2,1,0:T(8,128)S(1)}, f32[4,24,128]{2,1,0:T(8,128)S(1)}, u32[]{:S(2)}, u32[]{:S(2)}) collective-permute-start(f32[4,24,128]{2,1,0:T(8,128)S(1)} %join.9.refs_3_), channel_id=1, source_target_pairs={{0,4},{2,6},{4,0},{6,2},{8,12},{10,14},{12,8},{14,10},{16,20},{18,... | collective-permute-start | bytes 147464 | tf_op jit(solution)/shard_map/squares_across_2/ppermute | solution.py:137
  229.7 4.1 %collective-permute-start.63 = (f32[4,24,128]{2,1,0:T(8,128)S(1)}, f32[4,24,128]{2,1,0:T(8,128)S(1)}, u32[]{:S(2)}, u32[]{:S(2)}) collective-permute-start(f32[4,24,128]{2,1,0:T(8,128)S(1)} %join.9.refs_3_), channel_id=1, source_target_pairs={{0,2},{2,0},{4,6},{6,4},{8,10},{10,8},{12,14},{14,12},{16,18},{18,... | collective-permute-start | bytes 147464 | tf_op jit(solution)/shard_map/squares_across_1/ppermute | solution.py:137
  231.0 5.0 %collective-permute-start.64 = (f32[4,24,128]{2,1,0:T(8,128)S(1)}, f32[4,24,128]{2,1,0:T(8,128)S(1)}, u32[]{:S(2)}, u32[]{:S(2)}) collective-permute-start(f32[4,24,128]{2,1,0:T(8,128)S(1)} %join.9.refs_3_), channel_id=1, source_target_pairs={{0,6},{2,4},{4,2},{6,0},{8,14},{10,12},{12,10},{14,8},{16,22},{18,... | collective-permute-start | bytes 147464 | tf_op jit(solution)/shard_map/squares_across_3/ppermute | solution.py:137
  (46 other events, 490.1 us)
where the time goes:
time: 247 us; the launch traced here: 246 us
  Pallas kernels  82.6 us (33%)
  starting transfers between devices  80.2 us (32%)
  waiting for transfers between devices  58.4 us (24%)
  local copies, waits for them, and re-layouts  19.6 us (8%)
  other arithmetic  3 us (1%)
    pallas_call x37, Pallas kernels, apply(): pl.pallas_call(run, out_shape=[*out_shapes, *(shape_of(a.shape, a.dtype)...  82.6 us
    ppermute x60, starting transfers between devices, swap(): return lax.ppermute(array, 'dp', [(i, i ^ mask) for i in range(size)])  79.8 us
    ppermute x60, waiting for transfers between devices, swap(): return lax.ppermute(array, 'dp', [(i, i ^ mask) for i in range(size)])  54 us
    unnamed x97, local copies, waits for them, and re-layouts  18.7 us
  transfers between devices with their start and end apart: 65, of which 25 were waited for; matrix products, arithmetic and copies ran while one was open for 2% of the time, Pallas kernels for 26%

commit v1 on v0

--- a/solution.py
+++ b/solution.py
@@ -61,9 +61,9 @@
 
     def apply(*operands):
         inputs = len(operands)
-        if not in_specs:
+        if in_specs is None:
             options["grid"] = (1,)
-        specs = in_specs or [whole(operand.shape) for operand in operands]
+        specs = [whole(operand.shape) for operand in operands] if in_specs is None else in_specs
         targets = out_specs or [whole(shape.shape) for shape in out_shapes]
         targets = targets if isinstance(targets, (list, tuple)) else [targets]
         aliases = dict(input_output_aliases or {})
@@ -137,6 +137,10 @@
         return lax.ppermute(array, "dp", [(i, i ^ mask) for i in range(size)])
 
 
+def tie(arrays, deps):
+    return call(lambda: None, "tie", [], deps=deps, passing=arrays, in_specs=[], grid=(1,))()
+
+
 def other_core(array, label="other_core"):
     with jax.named_scope(label):
         return lax.ppermute(array, "mp", core_swap)
@@ -144,7 +148,7 @@
 
 def stage_bits(size):
     if size == 16:
-        return (4, 8, 2, 1)
+        return (8, 4, 2, 1)
     return tuple(1 << i for i in range(size.bit_length() - 1))
 
 
@@ -175,36 +179,38 @@
     )(*parts)
 
 
-def step_kernel(parts, y_ref, x_ref, *refs):
-    part_refs, (low_ref, high_ref, *line_refs) = refs[:parts], refs[parts:]
+def step_kernel(groups, y_ref, x_ref, *refs):
+    part_refs, (low_ref, high_ref, *joined_refs) = refs[: sum(groups)], refs[sum(groups) :]
     low_ref[...] = y_ref[...]
     high_ref[...] = x_ref[...]
-    if parts:
-        join_kernel(*part_refs, *line_refs)
-
-
-def gather_step(across_y, across_x, parts, **options):
+    for group, joined_ref in zip(groups, joined_refs):
+        join_kernel(*part_refs[:group], joined_ref)
+        part_refs = part_refs[group:]
+
+
+def gather_step(across_y, across_x, *groups, **options):
     half = (across_y.shape[0] // 2, across_y.shape[1])
     shapes = [shape_of(half, across_y.dtype)] * 2
-    if parts:
+    for parts in groups:
         shapes.append(shape_of((sum(p.shape[0] for p in parts), parts[0].shape[1]), parts[0].dtype))
+    flat = [part for parts in groups for part in parts]
     return call(
-        functools.partial(step_kernel, len(parts)),
+        functools.partial(step_kernel, tuple(len(parts) for parts in groups)),
         "gather_step",
         shapes,
         grid=(1,),
         in_specs=[
             pl.BlockSpec(half, lambda i: (0, 0)),
             pl.BlockSpec(half, lambda i: (1, 0)),
-            *(whole(part.shape) for part in parts),
+            *(whole(part.shape) for part in flat),
         ],
         out_specs=[whole(shape.shape) for shape in shapes],
         **options,
-    )(across_y, across_x, *parts)
+    )(across_y, across_x, *flat)
 
 
 def line_parts(part, size, label):
-    return [part] + [swap(part, mask, size, label) for mask in (4, 8, 12)]
+    return [part] + [swap(part, mask, size, label) for mask in (8, 4, 12)]
 
 
 def side_parts(quarter, size, label):
@@ -235,6 +241,10 @@
 
 def stacked(refs):
     return jnp.concatenate([ref[...] for ref in refs], axis=0)
+
+
+def stacked_row(refs, row):
+    return jnp.concatenate([ref[:, row, :] for ref in refs], axis=0)
 
 
 def gather_small(part, size, label):
@@ -249,19 +259,22 @@
     x_out[half:] = (x_ref[half:].astype(full_type) + high_ref[...].astype(full_type)).astype(low_type)
 
 
-def line_sum_kernel(z_ref, y_ref, x_ref, own_ref, *out_refs):
-    rows = own_ref.shape[0]
-    for i in range(4):
+def line_sum_kernel(*refs):
+    count = sum(ref.shape[0] == refs[0].shape[0] for ref in refs)
+    add_refs, out_refs = refs[:count], refs[count:]
+    rows = out_refs[0].shape[0]
+    for i, out_ref in enumerate(out_refs):
         span = slice(i * rows, (i + 1) * rows)
-        total = z_ref[span].astype(full_type) + y_ref[span].astype(full_type)
-        total = total + x_ref[span].astype(full_type)
-        target = own_ref if i == 0 else out_refs[i - 1]
-        target[...] = total.astype(target.dtype)
+        total = add_refs[0][span].astype(full_type)
+        for ref in add_refs[1:]:
+            total = total + ref[span].astype(full_type)
+        out_ref[...] = total.astype(out_ref.dtype)
 
 
 class Scatter:
     def __init__(self, pieces, size, label):
-        self.pieces, self.size, self.label, self.sources = pieces, size, label, ()
+        self.pieces, self.size, self.label = pieces, size, label
+        self.sources, self.came = (), ()
         if size == 16:
             *self.pieces, low, high = pieces
             self.came = [swap(low, 1, size, label), swap(high, 2, size, label)]
@@ -280,6 +293,33 @@
         self.sources = (to_y, to_x)
         self.came = [swap(to_y, 2, self.size, self.label), swap(to_x, 1, self.size, self.label)]
         return passed
+
+    def near(self, deps=()):
+        if self.size != 16:
+            return
+        keep = self.pieces[0]
+        half = (keep.shape[0] // 2, keep.shape[1])
+        kept, sent = call(
+            line_sum_kernel,
+            "line_sum",
+            [shape_of(half, full_type), shape_of(half, low_type)],
+            deps=deps,
+        )(keep, *self.came)
+        self.sources, self.came, self.pieces = (sent,), [swap(sent, 4, self.size, self.label)], [kept]
+
+    def far(self, deps=()):
+        if self.size != 16:
+            return self.line(deps)[0]
+        kept = self.pieces[0]
+        half = (kept.shape[0] // 2, kept.shape[1])
+        own, sent = call(
+            line_sum_kernel,
+            "line_sum",
+            [shape_of(half, full_type), shape_of(half, low_type)],
+            deps=deps,
+        )(kept, *self.came)
+        self.sources = (sent,)
+        return [own, swap(sent, 8, self.size, self.label)]
 
     def line(self, deps=(), passing=()):
         size, label = self.size, self.label
@@ -299,7 +339,7 @@
             deps=deps,
             passing=passing,
         )(keep, *self.came)
-        came = [swap(other, mask, size, label) for other, mask in zip(others, (4, 8, 12))]
+        came = [swap(other, mask, size, label) for other, mask in zip(others, (8, 4, 12))]
         return [own] + came, others[3:]
 
 
@@ -581,59 +621,67 @@
     out_ref[...] = few_rows([down[m : m + 1] + down[micro + m : micro + m + 1] for m in range(micro)], 8)
 
 
-def margin_kernel(len_ref, own_ref, other_ref, sum_ref, vector_ref, margin_ref, pooled_ref):
-    margins, vectors_pooled = [], []
+def margin_kernel(len_ref, own_ref, other_ref, sum_ref, act_ref, vector_ref, send_ref):
+    margins, rows = [], []
     for m in range(sum_ref.shape[0]):
+        length = len_ref[m].astype(full_type)
         total = own_ref[m : m + 1] + other_ref[m : m + 1] + sum_ref[m]
-        pooled = (total / len_ref[m].astype(full_type)).astype(low_type).astype(full_type)
+        pooled = (total / length).astype(low_type).astype(full_type)
         final = pooled * rms_scale(pooled) * vector_ref[2:3]
         logits = [
             jnp.sum(final * vector_ref[i : i + 1], axis=1, keepdims=True) * pooled.shape[1] ** (-0.5)
             for i in (3, 4)
         ]
-        margins.append(jnp.broadcast_to(logits[0] - logits[1], (1, LANES)))
-        vectors_pooled.append(pooled)
-    margin_ref[...] = few_rows(margins, 8)
-    pooled_ref[...] = few_rows(vectors_pooled, 8)
+        lane = lax.broadcasted_iota(jnp.int32, pooled.shape, 1)
+        margins.append(jnp.where(lane < LANES, logits[0] - logits[1], length))
+        rows.append(pooled)
+    width = rows[0].shape[1]
+    for m in range(sum_ref.shape[0]):
+        sums = act_ref[m]
+        rows += [sums[:, i * width : (i + 1) * width] for i in range(sums.shape[1] // width)]
+    send_ref[...] = few_rows(rows + margins, 8)
+
+
+def ranking(margins, same, positive):
+    place = lax.broadcasted_iota(jnp.int32, margins.shape, 0)
+    lane = lax.broadcasted_iota(jnp.int32, margins.shape, 1)
+    others = jnp.sum(jnp.where(place == lane, margins, 0.0), axis=0, keepdims=True)
+    row_max = jnp.max(jnp.where(same, others, masked_score), axis=1, keepdims=True)
+    terms = jnp.where(same, jnp.exp(jnp.where(same, others - row_max, 0.0)), 0.0)
+    chance = jnp.exp(margins - row_max) / jnp.sum(terms, axis=1, keepdims=True)
+    return LOSS_SCALE * (chance - positive)
+
+
+def pooled_grad(pooled, d_margin, vector_ref):
+    scale = rms_scale(pooled)
+    d_logit = d_margin * pooled.shape[1] ** (-0.5)
+    d_final = d_logit * (vector_ref[3:4] - vector_ref[4:5])
+    return norm_input_grad(d_final, vector_ref[2:3], pooled, scale)
 
 
 def rank_kernel(
-    margin_pieces, down_pieces, up_pieces, len_ref, same_ref, positive_ref, pooled_ref,
-    vector_ref, sum_ref, slope_ref, *refs
+    small_pieces, down_pieces, up_pieces, len_ref, same_ref, positive_ref, vector_ref, slope_ref,
+    *refs
 ):
-    margin_refs, refs = refs[:margin_pieces], refs[margin_pieces:]
+    small_refs, refs = refs[:small_pieces], refs[small_pieces:]
     down_refs, refs = refs[:down_pieces], refs[down_pieces:]
     up_refs, refs = refs[:up_pieces], refs[up_pieces:]
-    line_ref, act_ref, small_ref, d_ref, down_ref, up_ref = refs
+    line_ref, act_ref, rank_ref, d_ref, down_ref, up_ref = refs
     m = pl.program_id(0)
 
     @pl.when(m == 0)
     def rank():
         fill_rows(down_ref, down_refs)
         fill_rows(up_ref, up_refs)
-        margins, same = stacked(margin_refs), same_ref[...] > 0.5
-        row_max = jnp.max(jnp.where(same, margins, masked_score), axis=0)
-        total = jnp.sum(jnp.where(same, jnp.exp(margins - row_max[None]), 0.0), axis=0)
-        chance = jnp.exp(margins[0] - row_max) / total
-        d_margins = LOSS_SCALE * (chance - positive_ref[...])
-        tied_gap = vector_ref[3:4] - vector_ref[4:5]
-        gain = vector_ref[2:3]
-        lines, tied = [], 0.0
+        lines = []
         for i in range(2):
-            pooled = pooled_ref[i : i + 1]
-            scale = rms_scale(pooled)
-            d_logit = d_margins[i : i + 1, 0:1] * pooled.shape[1] ** (-0.5)
-            d_final = d_logit * tied_gap
-            tied = tied + pooled * scale * d_logit
-            d_pooled = norm_input_grad(d_final, gain, pooled, scale)
+            margins = stacked_row(small_refs, 6 + i)[:, :LANES]
+            d_margins = ranking(margins, same_ref[i] > 0.5, positive_ref[i])
+            rank_ref[i] = d_margins
+            pooled = small_refs[0][0, i : i + 1, :]
+            d_pooled = pooled_grad(pooled, d_margins[0:1, 0:1], vector_ref)
             lines.append(d_pooled / len_ref[i].astype(full_type))
         line_ref[...] = few_rows(lines, 8)
-        width, parts = tied.shape[1], sum_ref.shape[2] // tied.shape[1]
-        rows = [line.astype(low_type).astype(full_type) for line in lines]
-        for i in range(2):
-            sums = sum_ref[i]
-            rows += [sums[:, part * width : (part + 1) * width] for part in range(parts)]
-        small_ref[...] = few_rows([*rows, tied], 8)
         d_act = dot_nn(few_rows(lines, 16).astype(low_type), down_ref[...])
         act_ref[...] = d_act[:8]
 
@@ -644,16 +692,16 @@
     d_ref[...] = jnp.where(valid, d_normed, 0.0).astype(low_type)
 
 
-def rank_back(lengths, margins, same, positive, pooled, vectors, act_sum, slope, down, up, slot, deps):
+def rank_back(lengths, same, positive, vectors, slope, small_all, down, up, slot, deps):
     count, inner = slope.shape
-    width = pooled.shape[1]
+    width = vectors.shape[1]
     return call(
-        functools.partial(rank_kernel, len(margins), len(down), len(up)),
+        functools.partial(rank_kernel, len(small_all), len(down), len(up)),
         "rank_backward",
         [
             shape_of((8, width), full_type),
             shape_of((8, inner), full_type),
-            shape_of((8, width), full_type),
+            shape_of(positive.shape, full_type),
             shape_of((count, width), low_type),
         ],
         cost=(1200, 20000),
@@ -661,18 +709,18 @@
         grid=(count // slot,),
         in_specs=[
             on_scalars(),
-            *(whole(array.shape) for array in (same, positive, pooled, vectors, act_sum)),
+            *(whole(array.shape) for array in (same, positive, vectors)),
             row_blocks((slot, inner)),
-            *(whole(piece.shape) for piece in (*margins, *down, *up)),
+            *(whole(piece.shape) for piece in (*small_all, *down, *up)),
         ],
         out_specs=[
             whole((8, width)),
             whole((8, inner)),
-            whole((8, width)),
+            whole(positive.shape),
             row_blocks((slot, width)),
         ],
         scratch_shapes=[pltpu.VMEM((width, inner), low_type), pltpu.VMEM((width, inner), low_type)],
-    )(lengths, same, positive, pooled, vectors, act_sum, slope, *margins, *down, *up)
+    )(lengths, same, positive, vectors, slope, *small_all, *down, *up)
 
 
 def up_grad_kernel(slot, normed_ref, slope_ref, act_ref, *refs):
@@ -968,7 +1016,7 @@
     )(d_project, *weights)
 
 
-def token_kernel(d_ref, own_ref, came_ref, x_ref, vector_ref, order_ref, out_ref):
+def token_kernel(d_ref, own_ref, came_ref, x_ref, vector_ref, order_ref, out_ref, done_ref):
     x = x_ref[...].astype(full_type)
     d_normed = own_ref[...].astype(full_type) + came_ref[...].astype(full_type)
     grad = d_ref[...] + norm_input_grad(d_normed, vector_ref[0:1], x, rms_scale(x))
@@ -976,6 +1024,7 @@
     rest = (grad - high.astype(full_type)).astype(low_type)
     order = order_ref[...]
     out_ref[...] = dot_nt(high, order) + dot_nt(rest, order)
+    done_ref[...] = jnp.zeros_like(done_ref)
 
 
 def token_back(d_middle, own, came, rows_low, vectors, order, deps):
@@ -983,12 +1032,12 @@
     return call(
         token_kernel,
         "token_gradient",
-        shape_of((count, width), full_type),
+        [shape_of((count, width), full_type), shape_of((8, LANES), full_type)],
         cost=(1200, 15000),
         deps=deps,
         grid=(count // ROWS,),
         in_specs=[row_blocks((ROWS, width))] * 4 + [whole(vectors.shape), whole(order.shape)],
-        out_specs=row_blocks((ROWS, width)),
+        out_specs=[row_blocks((ROWS, width)), whole((8, LANES))],
     )(d_middle, own, came, rows_low, vectors, order)
 
 
@@ -998,9 +1047,9 @@
     for count in counts:
         groups.append(refs[:count])
         refs = refs[count:]
-    in_ref, up_ref, gain_ref, tied_ref, down_ref, line_ref, *out_refs = refs
+    rank_ref, vector_ref, in_ref, up_ref, gain_ref, tied_ref, down_ref, line_ref, *out_refs = refs
     size, width = sum(ref.shape[0] for ref in small_refs), small_refs[0].shape[2]
-    row_of = lambda row: jnp.concatenate([ref[:, row, :] for ref in small_refs], axis=0)
+    row_of = lambda row: stacked_row(small_refs, row)
     own = down_ref.shape[0]
     inverse = 1.0 / LOSS_SCALE
     add_up = lambda values: jnp.sum(values, axis=0, keepdims=True).sum(axis=1, keepdims=True)
@@ -1019,11 +1068,22 @@
         jnp.int32, (width, LANES), 1
     )
     fold = jnp.where(fold, 1.0, 0.0).astype(low_type)
-    pick = lambda row: jnp.where(mine, row_of(row), 0.0)
-    down = 0.0
+    down, ranked = 0.0, 0.0
+    lane = lax.broadcasted_iota(jnp.int32, (1, LANES), 1)
+    own_factor = (vector_ref[3:4, :LANES] - vector_ref[4:5, :LANES]) * vector_ref[2:3, :LANES]
+    own_factor = jnp.where(lane < own, own_factor, 0.0)
     parts = down_ref.shape[1] // width
     for m in range(micro):
-        lines = dot_nn(pick(m).astype(low_type), fold).astype(low_type)
+        pooled = row_of(m)
+        scale = rms_scale(pooled)
+        lengths = row_of(micro + micro * parts + m)
+        margins, lengths = lengths[:, 0:1], lengths[:, LANES : LANES + 1]
+        d_logit = rank_ref[m][:, 0:1] * width ** (-0.5)
+        mean = d_logit * margins * (width**0.5 / width) / scale
+        mine_low = dot_nn(jnp.where(mine, pooled, 0.0).astype(low_type), fold)
+        ranked = ranked + jnp.sum(mine_low * scale * d_logit, axis=0, keepdims=True)
+        d_pooled = scale * d_logit * own_factor - mine_low * scale**3 * mean
+        lines = (d_pooled / lengths).astype(low_type)
         acts = [row_of(micro + m * parts + i) for i in range(parts)]
         acts = jnp.concatenate(acts, axis=1)
         high = acts.astype(low_type)
@@ -1033,14 +1093,7 @@
     down_ref[...] = down
     squares = squares + add_up(down * down)
 
-    rest = jnp.sum(pick(micro + micro * parts), axis=0, keepdims=True) * inverse
-    rest = jnp.broadcast_to(rest, (16, width))
-    ranked = 0.0
-    for _ in range(3):
-        high = rest.astype(low_type)
-        ranked = ranked + dot_nn(high, fold)
-        rest = rest - high.astype(full_type)
-    ranked = ranked[0:1, :own]
+    ranked = ranked[:, :own] * inverse
     rounded = lambda ref, i: ref[i : i + 1].astype(low_type).astype(full_type)
     tied_gap = rounded(tied_ref, 0) - rounded(tied_ref, 1)
 
@@ -1074,7 +1127,9 @@
     line_ref[16 : 16 + 2 * pairs] = table[: 2 * pairs]
 
 
-def totals(small_all, grads, heads_in, hidden_in, gains, tied_rows, widths, micro, deps):
+def totals(
+    small_all, ranks, vectors, grads, heads_in, hidden_in, gains, tied_rows, widths, micro, deps
+):
     counts = tuple(len(group) for group in grads)
     flat = [array for group in grads for array in group]
     own, inner = hidden_in.shape
@@ -1090,7 +1145,7 @@
         ],
         cost=(100, 10000),
         deps=deps,
-    )(*small_all, *flat, heads_in, hidden_in, gains, tied_rows)
+    )(*small_all, *flat, ranks, vectors, heads_in, hidden_in, gains, tied_rows)
     return down, line, sums
 
 
@@ -1141,53 +1196,37 @@
 
     everything = (slice(None), slice(None))
     early_ref, late_ref, up_ref, down_ref = grad_refs
-    part = pl.program_id(0)
     pairs = weights[0].shape[2] // LANES
     for p in range(pairs):
         source, offset = (early_ref, p * 3) if p < pairs - 1 else (late_ref, 0)
-        columns = pl.ds(pl.multiple_of((offset + part) * LANES, LANES), LANES)
-        where = (0, slice(None), slice(p * LANES, (p + 1) * LANES))
-        step(0, where, source[:, columns], rate_matrix, decay_matrix)
-    columns = pl.ds(pl.multiple_of(((pairs - 1) * 3 + part) * LANES, LANES), LANES)
-    step(1, everything, early_ref[:, columns], rate_matrix, decay_matrix)
+        for c in range(3):
+            columns = slice((offset + c) * LANES, (offset + c + 1) * LANES)
+            where = (c, slice(None), slice(p * LANES, (p + 1) * LANES))
+            step(0, where, source[:, columns], rate_matrix, decay_matrix)
+    step(1, everything, early_ref[:, (pairs - 1) * 3 * LANES :], rate_matrix, decay_matrix)
     step(2, everything, up_ref[...], rate_matrix, decay_matrix)
     step(3, everything, down_ref[...], rate_matrix, decay_matrix)
-
-    @pl.when(part == 0)
-    def small():
-        rows = weights[4].shape[1]
-        extra = extra_ref[...]
-        step(4, everything, extra[0:3, :rows], rate_vector, 0.0)
-        tied = extra[3:4, :rows]
-        step(5, everything, jnp.concatenate([tied, -tied], axis=0), rate_vector, 0.0)
-        step(6, everything, tables[: 2 * pairs, :BUCKETS], rate_vector, 0.0)
+    rows = weights[4].shape[1]
+    extra = extra_ref[...]
+    step(4, everything, extra[0:3, :rows], rate_vector, 0.0)
+    tied = extra[3:4, :rows]
+    step(5, everything, jnp.concatenate([tied, -tied], axis=0), rate_vector, 0.0)
+    step(6, everything, tables[: 2 * pairs, :BUCKETS], rate_vector, 0.0)
 
 
 def update(pick, corrections, extra, squares, grads, states):
-    parts = states[0].shape[0]
-    thirds = lambda array: column_blocks((array.shape[0], array.shape[1] // parts))
-    state_specs = []
-    for _ in range(3):
-        one = states[len(state_specs) : len(state_specs) + 7]
-        state_specs += [pl.BlockSpec((1, *one[0].shape[1:]), lambda i: (i, 0, 0))]
-        state_specs += [thirds(array) for array in one[1:4]]
-        state_specs += [whole(array.shape) for array in one[4:]]
     return call(
         functools.partial(update_kernel, len(squares), len(grads)),
         "update",
         [shape_of((1, 1), full_type)] + [shape_of(s.shape, full_type) for s in states],
         cost=(0, 6000),
-        grid=(parts,),
+        vmem=56,
+        grid=(1,),
         in_specs=[
             on_scalars(),
             on_scalars(),
-            whole(extra.shape),
-            *(whole(array.shape) for array in squares),
-            *(whole(array.shape) for array in grads[:2]),
-            *(thirds(array) for array in grads[2:]),
-            *state_specs,
-        ],
-        out_specs=[whole((1, 1)), *state_specs],
+            *(whole(array.shape) for array in (extra, *squares, *grads, *states)),
+        ],
     )(pick, corrections, extra, *squares, *grads, *states)
 
 
@@ -1238,7 +1277,7 @@
     second_gains, second_tied, second_table = second_gains.T, second_tied.T, second_table.T
 
     packed_heads = call(
-        pack_heads_kernel, "pack_heads", shape_of((own, 4 * head_width + LANES), low_type)
+        pack_heads_kernel, "pack_heads", shape_of((own, 4 * head_width + LANES), low_type), vmem=56
     )(heads_in, heads_out, gains, tied_rows)
     packed_up, packed_down = call(
         pack_hidden_kernel, "pack_hidden", [shape_of((own, inner), low_type)] * 2
@@ -1248,16 +1287,12 @@
     order = (jnp.arange(width, dtype=jnp.int32)[:, None] == place[None, :]).astype(low_type)
     lengths = pair_lengths.reshape(micro)
     queries = query_ids[:, pair_ids]
-    same_query = queries == queries[:, :1]
-    earlier = jnp.any(same_query & (pair_ids < me)[None, :], axis=1)
-    to_tile = lambda rows_m: jnp.broadcast_to(
-        jnp.concatenate(
-            [rows_m, jnp.zeros(rows_m.shape[:-1] + (8 - micro,), full_type)], axis=-1
-        )[..., None],
-        rows_m.shape[:-1] + (8, LANES),
-    )
-    same_tile = to_tile(same_query.astype(full_type).T)
-    positive_tile = to_tile(jnp.where(earlier, 0.0, 1.0))
+    same_query = queries[:, :, None] == queries[:, None, :]
+    padded = jnp.pad(queries, ((0, 0), (0, LANES - size)), constant_values=-1)
+    same_tile = (queries[:, :, None] == padded[:, None, :]).astype(full_type)
+    earlier = same_query & (pair_ids[None, :] < pair_ids[:, None])[None]
+    positive_tile = jnp.where(jnp.any(earlier, axis=2), 0.0, 1.0)[:, :, None]
+    positive_tile = jnp.broadcast_to(positive_tile, (micro, size, LANES))
 
     bucket_line = jnp.concatenate([distance_bucket, jnp.full((1,), -1, jnp.int32)])
     bucket_hot = (
@@ -1266,6 +1301,12 @@
     lines = dot_nt(bias_table.astype(low_type), bucket_hot[:, :BUCKETS])
     lines = lines.reshape(pairs, 2, 2 * slot)
     hot_spans = jnp.stack([bucket_hot[d * LANES : (d + 2) * LANES] for d in range(spans)])
+
+    step_float = step_count.astype(full_type)
+    corrections = jnp.stack(
+        [1.0 / (1.0 - beta_first**step_float), 1.0 / (1.0 - beta_second**step_float)]
+    )
+    first_place = jnp.sum(jnp.where(pair_ids == 0, jnp.arange(size, dtype=jnp.int32), 0)).reshape(1)
 
     rows_low = call(
         order_kernel,
@@ -1280,35 +1321,42 @@
         weight_heads, weight_up, weight_down = (
             [gather_doubling(part, size)] for part in (packed_heads, packed_up, packed_down)
         )
-        qkv, normed_first, vectors = project(rows_low, weight_heads, pairs, ())
+        qkv, normed_first, vectors = project(rows_low, weight_heads, pairs, (same_tile, positive_tile, corrections))
     else:
-        heads_line, packed_up = join(line_parts(packed_heads, size, "heads"), passing=(packed_up,))
+        heads_line, packed_up, packed_down = join(
+            line_parts(packed_heads, size, "heads"), passing=(packed_up, packed_down)
+        )
         heads_sides = side_parts(heads_line, size, "heads")
-        up_line_parts = line_parts(packed_up, size, "up")
-        low, high = gather_step(*heads_sides, [], deps=(rows_low, *up_line_parts[1:]))
+        up_pair = join([packed_up, swap(packed_up, 8, size, "up")], deps=(rows_low,))
+        up_near = swap(up_pair, 4, size, "up")
+        low, high, packed_down = gather_step(*heads_sides, deps=(up_pair,), passing=(packed_down,))
+        down_far = swap(packed_down, 8, size, "down")
         heads_corner = corner_parts(low, high, size, "heads_corner")
-        up_line, packed_down = join(up_line_parts, deps=heads_corner, passing=(packed_down,))
+        up_line = join([up_pair, up_near], deps=(low,))
+        down_pair = join([packed_down, down_far], deps=(up_line,))
+        down_near = swap(down_pair, 4, size, "down")
         up_sides = side_parts(up_line, size, "up")
-        down_parts = line_parts(packed_down, size, "down")
         weight_heads = [heads_line, *heads_sides, *heads_corner]
         qkv, normed_first, vectors = project(
-            rows_low, weight_heads, pairs, (same_tile, positive_tile)
+            rows_low, weight_heads, pairs, (same_tile, positive_tile, down_pair, corrections, first_place)
         )
     filled = ()
     for pair in range(pairs):
         filled = attention(lengths, lines, qkv, pair, slot, before=filled)
         if pair == 0 and size == 16:
-            low, high, down_line = gather_step(*up_sides, down_parts, deps=(filled[0],))
+            down_line = join([down_pair, down_near], deps=(filled[0],))
+            down_sides = side_parts(down_line, size, "down")
+        if pair == 1 and size == 16:
+            low, high = gather_step(*up_sides, deps=(filled[0],))
             up_corner = corner_parts(low, high, size, "up_corner")
-            down_sides = side_parts(down_line, size, "down")
             weight_up = [up_line, *up_sides, *up_corner]
     turned_first = call(turn_kernel, "turn", shape_of((width, count), low_type))(normed_first)
     attended, probs, inverse = filled
     branch = branch_rows(
-        attended, weight_heads, (*down_sides, *up_corner, turned_first) if size == 16 else ()
+        attended, weight_heads, (*down_sides, turned_first) if size == 16 else ()
     )
     if size == 16:
-        low, high = gather_step(*down_sides, [], deps=(branch,))
+        low, high = gather_step(*down_sides, deps=(branch,))
         down_corner = corner_parts(low, high, size, "down_corner")
         weight_down = [down_line, *down_sides, *down_corner]
     branch_came = other_core(branch, "branch_other_core")
@@ -1322,18 +1370,22 @@
         cost=(20, 5000),
         scratch_shapes=[pltpu.VMEM((width, inner), low_type)],
     )(act_sum, *weight_down)
-    margin_tile, pooled = call(
+    small = call(
         margin_kernel,
         "margin",
-        [shape_of((8, LANES), full_type), shape_of((8, width), full_type)],
+        shape_of((8, width), full_type),
         grid=(1,),
-        in_specs=[on_scalars(), *[whole(down.shape)] * 2, whole(middle_sum.shape), whole(vectors.shape)],
-    )(lengths, down, other_core(down, "pooled_part_other_core"), middle_sum, vectors)
-    margins = gather_small(margin_tile, size, "margins")
-
-    d_line, d_act, small, d_normed_second = rank_back(
-        lengths, margins, same_tile, positive_tile, pooled, vectors, act_sum,
-        slope, weight_down, weight_up, slot, (turned_first,),
+        in_specs=[
+            on_scalars(),
+            *(whole(array.shape) for array in (down, down, middle_sum, act_sum, vectors)),
+        ],
+        out_specs=whole((8, width)),
+    )(lengths, down, other_core(down, "pooled_part_other_core"), middle_sum, act_sum, vectors)
+    small_all = gather_small(small, size, "small_sums")
+
+    d_line, d_act, ranks, d_normed_second = rank_back(
+        lengths, same_tile, positive_tile, vectors, slope, small_all, weight_down, weight_up, slot,
+        (turned_first,),
     )
     d_normed_second_came = other_core(d_normed_second, "second_gradient_other_core")
     up_sum = Scatter(
@@ -1352,27 +1404,27 @@
         )
         filled = (d_project, *g_early)
         tables.append(table)
-    up_parts, _ = up_sum.line(deps=(d_project,))
+    up_sum.near(deps=(d_project,))
     early_sum = Scatter(g_early, size, "early_gradient")
     d_project, table, *g_late = attention_back(
         probs, qkv, d_attended, attended, turned_first, hot_spans, piece_rows(size, width),
-        pairs - 1, slot, own, tables=tuple(tables), before=(d_project,), deps=(up_parts[0],),
+        pairs - 1, slot, own, tables=tuple(tables), before=(d_project,), deps=up_sum.sources,
     )
     late_sum = Scatter(g_late, size, "late_gradient")
     early_sum.sides(deps=(table,))
-    d_normed_first = normed_back(d_project, weight_heads, (*early_sum.sources, *up_parts[1:]))
-    d_normed_first, small = late_sum.sides(passing=(d_normed_first, small))
-    small = small_line(small, size, "small_sums")
-    early_parts, _ = early_sum.line(deps=late_sum.sources)
-    token_gradient = token_back(
+    up_parts = up_sum.far(deps=(table, *early_sum.sources))
+    d_normed_first = normed_back(d_project, weight_heads, (up_parts[0],))
+    (d_normed_first,) = late_sum.sides(deps=(*early_sum.came, *up_parts[1:]), passing=(d_normed_first,))
+    early_sum.near(deps=late_sum.sources)
+    token_gradient, token_done = token_back(
         d_middle, d_normed_first, other_core(d_normed_first, "first_gradient_other_core"), rows_low,
-        vectors, order, (early_parts[0],),
-    )
-    late_parts, (small,) = late_sum.line(deps=(token_gradient,), passing=(small,))
-    small_all = small_plane(small, size, "small_sums")
+        vectors, order, early_sum.sources,
+    )
+    early_parts = early_sum.far(deps=(token_done,))
+    late_parts, _ = late_sum.line(deps=(early_parts[0],))
 
     g_down, line, grad_sums = totals(
-        small_all, [early_parts, late_parts, up_parts], heads_in, hidden_in, gains, tied_rows,
+        small_all, ranks, vectors, [early_parts, late_parts, up_parts], heads_in, hidden_in, gains, tied_rows,
         (head_width * 3, 3 * LANES, inner), micro, (),
     )
     square_tile, extra = call(
@@ -1381,10 +1433,6 @@
         [shape_of((24, LANES), full_type), shape_of((8, LANES), full_type)],
     )(line, other_core(line, "totals_other_core"))
     squares_all = gather_small(square_tile, size, "squares")
-    step_float = step_count.astype(full_type)
-    corrections = jnp.stack(
-        [1.0 / (1.0 - beta_first**step_float), 1.0 / (1.0 - beta_second**step_float)]
-    )
     grads = [*grad_sums, g_down]
     weights = (heads_in, heads_out, hidden_in, hidden_out, gains, tied_rows, bias_table)
     firsts = (
@@ -1406,7 +1454,6 @@
         second_table,
     )
     states = (*weights, *firsts, *seconds)
-    first_place = jnp.sum(jnp.where(pair_ids == 0, jnp.arange(size, dtype=jnp.int32), 0)).reshape(1)
     norm, *results = update(first_place, corrections, extra, squares_all, grads, states)
     for index in (0, 7, 14):
         results[index] = turn_matrix(results[index])

time: 247 us -> 220 us (0.89)
  local copies, waits for them, and re-layouts: 19.6 us -> 8.6 us
  starting transfers between devices: 80.2 us -> 69.3 us
  waiting for transfers between devices: 58.4 us -> 55.3 us
  Pallas kernels: 82.6 us -> 79.9 us
    unnamed x97 -> x49, local copies, waits for them, and re-layouts: 18.7 us -> 7.78 us
    ppermute x60 -> x50, starting transfers between devices: 79.8 us -> 69.1 us  [swap(): return lax.ppermute(array, 'dp', [(i, i ^ mask) for i in range(size)])]
    pallas_call x37 -> x41, Pallas kernels: 82.6 us -> 79.9 us  [apply(): pl.pallas_call(run, out_shape=[*out_shapes, *(shape_of(a.shape, a.dtype)...]
    ppermute x60 -> x50, waiting for transfers between devices: 54 us -> 52.9 us  [swap(): return lax.ppermute(array, 'dp', [(i, i ^ mask) for i in range(size)])]
  transfers between devices with their start and end apart: 65 -> 55, of which waited for: 25 -> 28; matrix products, arithmetic and copies ran while one was open for 2% -> 3% of each run, Pallas kernels for 26% -> 29%
where the time goes in v1:
time: 220 us
  Pallas kernels  79.9 us (36%)
  starting transfers between devices  69.3 us (32%)
  waiting for transfers between devices  55.3 us (25%)
  local copies, waits for them, and re-layouts  8.6 us (4%)
  other arithmetic  3.88 us (2%)
    pallas_call x41, Pallas kernels, apply(): pl.pallas_call(run, out_shape=[*out_shapes, *(shape_of(a.shape, a.dtype)...  79.9 us
    ppermute x50, starting transfers between devices, swap(): return lax.ppermute(array, 'dp', [(i, i ^ mask) for i in range(size)])  69.1 us
    ppermute x50, waiting for transfers between devices, swap(): return lax.ppermute(array, 'dp', [(i, i ^ mask) for i in range(size)])  52.9 us
    unnamed x49, local copies, waits for them, and re-layouts  7.78 us
  transfers between devices with their start and end apart: 55, of which 28 were waited for; matrix products, arithmetic and copies ran while one was open for 3% of the time, Pallas kernels for 29%

profile of v1, /device:TPU:0, one launch (start us, length us, event | category | flops | bytes accessed | tf_op | source)
XLA Modules:
  0.0 220.0 jit_solution(11940873489624469172)
XLA Ops:
  0.7 1.8 pack_heads.1.refs_0_
  2.5 4.0 %collective-permute-start = (bf16[48,1664]{1,0:T(8,128)(2,1)}, bf16[48,1664]{1,0:T(8,128)(2,1)S(1)}, u32[]{:S(2)}, u32[]{:S(2)}) collective-permute-start(bf16[48,1664]{1,0:T(8,128)(2,1)} %pack_heads.1.refs_0_), channel_id=1, source_target_pairs={{0,16},{2,18},{4,20},{6,22},{8,24},{10,26},{12,28},{14,30},{16,0},... | collective-permute-start | bytes 479240 | tf_op jit(solution)/shard_map/heads_across_8/ppermute | solution.py:137
  6.5 1.6 collective-permute-start.1
  11.7 1.3 broadcast_xor_fusion
  14.0 1.9 collective-permute-done.refs_1_
  15.9 3.0 %collective-permute-done.2.refs_3_ = bf16[48,1664]{1,0:T(8,128)(2,1)S(1)} collective-permute-done((bf16[48,1664]{1,0:T(8,128)(2,1)}, bf16[48,1664]{1,0:T(8,128)(2,1)S(1)}, u32[]{:S(2)}, u32[]{:S(2)}) %collective-permute-start.2) | collective-permute-done | bytes 159776 | tf_op jit(solution)/shard_map/heads_across_12/ppermute | solution.py:137
  19.9 1.6 collective-permute-start.3
  21.4 1.5 collective-permute-start.4
  23.5 4.9 %collective-permute-start.5 = (bf16[48,1536]{1,0:T(8,128)(2,1)S(1)}, bf16[48,1536]{1,0:T(8,128)(2,1)}, u32[]{:S(2)}, u32[]{:S(2)}) collective-permute-start(bf16[48,1536]{1,0:T(8,128)(2,1)S(1)} %get-tuple-element.137.refs_0_), channel_id=1, source_target_pairs={{0,16},{2,18},{4,20},{6,22},{8,24},{10,26},{12,28},{14,30},{16,0},... | collective-permute-start | bytes 442376 | tf_op jit(solution)/shard_map/up_across_8/ppermute | solution.py:137
  30.0 1.4 copy-done.15
  31.4 1.9 order_tokens.1.refs_2_.refs_0_.refs_1_.refs_3_
  33.4 1.8 collective-permute-done.5.refs_1_
  36.5 6.0 %collective-permute-start.8 = (bf16[48,1536]{1,0:T(8,128)(2,1)S(1)}, bf16[48,1536]{1,0:T(8,128)(2,1)S(1)}, u32[]{:S(2)}, u32[]{:S(2)}) collective-permute-start(bf16[48,1536]{1,0:T(8,128)(2,1)S(1)} %get-tuple-element.141.refs_0_), channel_id=1, source_target_pairs={{0,16},{2,18},{4,20},{6,22},{8,24},{10,26},{12,28},{14,30},{16,0},... | collective-permute-start | bytes 442376 | tf_op jit(solution)/shard_map/down_across_8/ppermute | solution.py:137
  42.4 1.5 collective-permute-start.6
  44.4 2.0 collective-permute-done.9.refs_1_
  46.5 2.0 collective-permute-done.8.refs_1_
  49.3 1.5 collective-permute-start.15
  50.8 2.2 collective-permute-done.7.refs_5_.refs_14_
  53.1 4.2 %projection.1 = (bf16[3,3,1024,128]{3,2,1,0:T(8,128)(2,1)S(1)}, bf16[1024,768]{1,0:T(8,128)(2,1)S(1)}, f32[8,768]{1,0:T(8,128)S(1)}) custom-call(bf16[1024,768]{1,0:T(8,128)(2,1)S(1)} %order_tokens.1.refs_2_.refs_0_.refs_1_.refs_3_, bf16[192,1664]{1,0:T(8,128)(2,1)S(1)} %get-tuple-element.136.refs_1_.refs_10_, ...), custom_call_target="tpu_custom_call" | custom-call | tf_op jit(solution)/shard_map/projection/pallas_call | solution.py:77
  57.3 3.5 %attention_forward.3 = (bf16[1024,384]{1,0:T(8,128)(2,1)S(1)}, bf16[3,2,2,512,512]{4,3,2,1,0:T(8,128)(2,1)S(1)}, f32[1024,384]{1,0:T(8,128)S(1)}) custom-call(s32[2]{0:T(128)S(1)} %bitcast.89, f32[3,2,1024]{2,1,0:T(2,128)S(1)} %reshape.117.refs_1_, bf16[3,3,1024,128]{3,2,1,0:T(8,128)(2,1)S(1)} %get-tuple-element.142.refs_2_.refs_1_), custom_call_target="tpu_custom_call" | custom-call | tf_op jit(solution)/shard_map/attention_forward/pallas_call | solution.py:77
  62.0 3.5 %attention_forward.4 = (bf16[1024,384]{1,0:T(8,128)(2,1)S(1)}, bf16[3,2,2,512,512]{4,3,2,1,0:T(8,128)(2,1)S(1)}, f32[1024,384]{1,0:T(8,128)S(1)}) custom-call(s32[2]{0:T(128)S(1)} %bitcast.90, f32[3,2,1024]{2,1,0:T(2,128)S(1)} %reshape.117.refs_1_, ...), custom_call_target="tpu_custom_call", output_to_operand_aliasing={{0}: (3, {}), {1}: (4, {}), {2}: (5, {})} | custom-call | tf_op jit(solution)/shard_map/attention_forward/pallas_call | solution.py:77
  65.7 3.5 %attention_forward.5 = (bf16[1024,384]{1,0:T(8,128)(2,1)S(1)}, bf16[3,2,2,512,512]{4,3,2,1,0:T(8,128)(2,1)S(1)}, f32[1024,384]{1,0:T(8,128)S(1)}) custom-call(s32[2]{0:T(128)S(1)} %bitcast.91, f32[3,2,1024]{2,1,0:T(2,128)S(1)} %reshape.117.refs_1_, ...), custom_call_target="tpu_custom_call", output_to_operand_aliasing={{0}: (3, {}), {1}: (4, {}), {2}: (5, {})} | custom-call | tf_op jit(solution)/shard_map/attention_forward/pallas_call | solution.py:77
  69.2 7.7 %collective-permute-done.11.refs_6_.refs_0_.refs_2_.refs_10_ = bf16[192,1536]{1,0:T(8,128)(2,1)S(1)} collective-permute-done((bf16[192,1536]{1,0:T(8,128)(2,1)S(1)}, bf16[192,1536]{1,0:T(8,128)(2,1)S(1)}, u32[]{:S(2)}, u32[]{:S(2)}) %collective-permute-start.11) | collective-permute-done | bytes 589856 | tf_op jit(solution)/shard_map/down_across_2/ppermute | solution.py:137
  76.9 1.4 branch.1.refs_2_
  79.4 1.3 collective-permute-start.17
  81.2 1.4 collective-permute-start.19
  82.6 5.6 %collective-permute-done.16.refs_8_.refs_17_ = bf16[96,1536]{1,0:T(8,128)(2,1)S(1)} collective-permute-done((bf16[96,1536]{1,0:T(8,128)(2,1)S(1)}, bf16[96,1536]{1,0:T(8,128)(2,1)S(1)}, u32[]{:S(2)}, u32[]{:S(2)}) %collective-permute-start.16) | collective-permute-done | bytes 294944 | tf_op jit(solution)/shard_map/up_corner_across_1/ppermute | solution.py:137
  89.2 9.9 %hidden_forward.1 = (bf16[1024,768]{1,0:T(8,128)(2,1)S(1)}, bf16[1024,1536]{1,0:T(8,128)(2,1)S(1)}, f32[2,1,1536]{2,1,0:T(1,128)S(1)}, f32[2,1,768]{2,1,0:T(1,128)S(1)}) custom-call(s32[2]{0:T(128)S(1)} %bitcast.92, bf16[1024,768]{1,0:T(8,128)(2,1)S(1)} %order_tokens.1.refs_2_.refs_0_.refs_1_.refs_3_, bf16[1024,768]{1,0:T(8,128)(2,1)S(1)} %branch.1.refs_2_, ...), custom_call_target="tpu_custom_call" | custom-call | flops 2400000000 | bytes 20000000 | tf_op jit(solution)/shard_map/hidden_forward/pallas_call | solution.py:77
  99.9 1.2 collective-permute-done.20.refs_2_
  101.9 1.8 collective-permute-start.22
  103.7 2.6 %collective-permute-start.23 = (f32[1,8,768]{2,1,0:T(8,128)S(1)}, f32[1,8,768]{2,1,0:T(8,128)S(1)}, u32[]{:S(2)}, u32[]{:S(2)}) collective-permute-start(f32[1,8,768]{2,1,0:T(8,128)S(1)} %bitcast.84), channel_id=1, source_target_pairs={{0,24},{2,26},{4,28},{6,30},{8,16},{10,18},{12,20},{14,22},{16,8},... | collective-permute-start | bytes 73736 | tf_op jit(solution)/shard_map/small_sums_across_12/ppermute | solution.py:137
  106.6 2.7 %collective-permute-done.23.refs_3_ = f32[1,8,768]{2,1,0:T(8,128)S(1)} collective-permute-done((f32[1,8,768]{2,1,0:T(8,128)S(1)}, f32[1,8,768]{2,1,0:T(8,128)S(1)}, u32[]{:S(2)}, u32[]{:S(2)}) %collective-permute-start.23) | collective-permute-done | bytes 24608 | tf_op jit(solution)/shard_map/small_sums_across_12/ppermute | solution.py:137
  109.3 1.4 collective-permute-start.24
  111.6 1.3 collective-permute-start.26
  112.9 2.2 collective-permute-done.24.refs_6_.refs_1_
  115.3 1.8 collective-permute-done.26.refs_8_.refs_3_
  117.2 4.2 %rank_backward.1 = (f32[8,768]{1,0:T(8,128)S(1)}, f32[8,1536]{1,0:T(8,128)S(1)}, f32[2,16,128]{2,1,0:T(8,128)S(1)}, bf16[1024,768]{1,0:T(8,128)(2,1)S(1)}) custom-call(s32[2]{0:T(128)S(1)} %bitcast.94, f32[2,16,128]{2,1,0:T(8,128)S(1)} %compare_convert_fusion.refs_6_.refs_1_, f32[2,16,128]{2,1,0:T(8,128)S(1)} %broadcast_in_dim.20.refs_7_.refs_2_, ...), custom_call_target="tpu_custom_call" | custom-call | flops 2400000000 | bytes 20000000 | tf_op jit(solution)/shard_map/rank_backward/pallas_call | solution.py:77
  121.5 3.9 %hidden_in_gradient.1 = (bf16[192,1536]{1,0:T(8,128)(2,1)S(1)}, bf16[192,1536]{1,0:T(8,128)(2,1)S(1)}, bf16[192,1536]{1,0:T(8,128)(2,1)S(1)}, bf16[96,1536]{1,0:T(8,128)(2,1)S(1)}, bf16[96,1536]{1,0:T(8,128)(2,1)S(1)}) custom-call(bf16[1024,768]{1,0:T(8,128)(2,1)S(1)} %get-tuple-element.179.refs_0_, ...), custom_call_target="tpu_custom_call" | custom-call | flops 2400000000 | bytes 15000000 | tf_op jit(solution)/shard_map/hidden_in_gradient/pallas_call | solution.py:77
  125.4 1.2 collective-permute-start.30
  127.4 4.5 %middle_backward.1 = (f32[1024,768]{1,0:T(8,128)S(1)}, bf16[1024,384]{1,0:T(8,128)(2,1)S(1)}, f32[768,384]{1,0:T(8,128)S(1)}) custom-call(s32[2]{0:T(128)S(1)} %bitcast.95, bf16[1024,768]{1,0:T(8,128)(2,1)S(1)} %order_tokens.1.refs_2_.refs_0_.refs_1_.refs_3_, bf16[1024,768]{1,0:T(8,128)(2,1)S(1)} %branch.1.refs_2_, ...), custom_call_target="tpu_custom_call" | custom-call | flops 1200000000 | bytes 15000000 | tf_op jit(solution)/shard_map/middle_backward/pallas_call | solution.py:77
  131.9 3.0 %collective-permute-done.30.refs_2_ = bf16[96,1536]{1,0:T(8,128)(2,1)S(1)} collective-permute-done((bf16[96,1536]{1,0:T(8,128)(2,1)S(1)}, bf16[96,1536]{1,0:T(8,128)(2,1)S(1)}, u32[]{:S(2)}, u32[]{:S(2)}) %collective-permute-start.30) | collective-permute-done | bytes 294944 | tf_op jit(solution)/shard_map/up_gradient_across_1/ppermute | solution.py:137
  137.6 6.1 %attention_backward.3 = (bf16[3,3,1024,128]{3,2,1,0:T(8,128)(2,1)S(1)}, f32[1,8,128]{2,1,0:T(8,128)S(1)}, bf16[192,1152]{1,0:T(8,128)(2,1)S(1)}, bf16[192,1152]{...) custom-call(bf16[3,2,2,512,512]{4,3,2,1,0:T(8,128)(2,1)S(1)} %get-tu, ...), custom_call_target="tpu_custom_call" | custom-call | tf_op jit(solution)/shard_map/attention_backward/pallas_call | solution.py:77
  143.7 6.5 %attention_backward.4 = (bf16[3,3,1024,128]{3,2,1,0:T(8,128)(2,1)S(1)}, f32[1,8,128]{2,1,0:T(8,128)S(1)}, bf16[192,1152]{1,0:T(8,128)(2,1)S(1)}, bf16[192,1152]{...) custom-call(bf16[3,2,2,512,512]{4,3,2,1,0:T(8,128)(2,1)S(1)} %get-tu, ...), custom_call_target="tpu_custom_call", output_to_operand_aliasing={{0}: (7, {}), {2}: (8, {}), {3}: (9, {}), {4}: (10, {}), {5... | custom-call | tf_op jit(solution)/shard_map/attention_backward/pallas_call | solution.py:77
  151.4 1.3 collective-permute-start.29
  153.0 6.3 %attention_backward.5 = (bf16[3,3,1024,128]{3,2,1,0:T(8,128)(2,1)S(1)}, f32[1,8,128]{2,1,0:T(8,128)S(1)}, bf16[192,512]{1,0:T(8,128)(2,1)S(1)}, bf16[192,512]{1,...) custom-call(bf16[3,2,2,512,512]{4,3,2,1,0:T(8,128)(2,1)S(1)} %get-tu, ...), custom_call_target="tpu_custom_call", output_to_operand_aliasing={{0}: (8, {})} | custom-call | tf_op jit(solution)/shard_map/attention_backward/pallas_call | solution.py:77
  162.2 1.3 collective-permute-start.37
  163.6 3.2 %collective-permute-start.39 = (bf16[48,1536]{1,0:T(8,128)(2,1)S(1)}, bf16[48,1536]{1,0:T(8,128)(2,1)S(1)}, u32[]{:S(2)}, u32[]{:S(2)}) collective-permute-start(bf16[48,1536]{1,0:T(8,128)(2,1)S(1)} %get-tuple-element.197), channel_id=1, source_target_pairs={{0,16},{2,18},{4,20},{6,22},{8,24},{10,26},{12,28},{14,30},{16,0},... | collective-permute-start | bytes 442376 | tf_op jit(solution)/shard_map/up_gradient_across_8/ppermute | solution.py:137
  166.8 3.2 %normed_backward.1.refs_7_ = bf16[1024,768]{1,0:T(8,128)(2,1)S(1)} custom-call(bf16[3,3,1024,128]{3,2,1,0:T(8,128)(2,1)S(1)} %get-tuple-element.198.refs_0_, bf16[192,1664]{1,0:T(8,128)(2,1)S(1)} %get-tuple-element.136.refs_1_.refs_10_, bf16[192,1664]{1,0:T(8,128)(2,1)S(1)} %collective-permute-done.3.refs_0_.refs_2_.refs_11_, ...), custom_call_target="tpu_custom_call" | custom-call | flops 1800000000 | bytes 15000000 | tf_op jit(solution)/shard_map/normed_backward/pallas_call | solution.py:77
  170.0 2.3 %collective-permute-done.36.refs_2_ = bf16[96,512]{1,0:T(8,128)(2,1)S(1)} collective-permute-done((bf16[96,512]{1,0:T(8,128)(2,1)S(1)}, bf16[96,512]{1,0:T(8,128)(2,1)S(1)}, u32[]{:S(2)}, u32[]{:S(2)}) %collective-permute-start.36) | collective-permute-done | bytes 98336 | tf_op jit(solution)/shard_map/late_gradient_across_1/ppermute | solution.py:137
  172.5 1.4 collective-permute-start.43
  174.9 1.8 collective-permute-start.40
  176.7 5.2 %token_gradient.1 = (f32[1024,768]{1,0:T(8,128)}, f32[8,128]{1,0:T(8,128)S(1)}) custom-call(f32[1024,768]{1,0:T(8,128)S(1)} %get-tuple-element.204.refs_0_, bf16[1024,768]{1,0:T(8,128)(2,1)S(1)} %get-tuple-element.205.refs_1_, bf16[1024,768]{1,0:T(8,128)(2,1)S(1)} %collective-permute-done.41.refs_2_, ...), custom_call_target="tpu_custom_call" | custom-call | flops 2400000000 | bytes 15000000 | tf_op jit(solution)/shard_map/token_gradient/pallas_call | solution.py:77
  182.3 2.6 %collective-permute-start.42 = (bf16[48,1152]{1,0:T(8,128)(2,1)S(1)}, bf16[48,1152]{1,0:T(8,128)(2,1)S(1)}, u32[]{:S(2)}, u32[]{:S(2)}) collective-permute-start(bf16[48,1152]{1,0:T(8,128)(2,1)S(1)} %get-tuple-element.208), channel_id=1, source_target_pairs={{0,16},{2,18},{4,20},{6,22},{8,24},{10,26},{12,28},{14,30},{16,0},... | collective-permute-start | bytes 331784 | tf_op jit(solution)/shard_map/early_gradient_across_8/ppermute | solution.py:137
  185.4 1.7 collective-permute-start.46
  187.2 2.3 %collective-permute-start.47 = (bf16[48,512]{1,0:T(8,128)(2,1)S(1)}, bf16[48,512]{1,0:T(8,128)(2,1)S(1)}, u32[]{:S(2)}, u32[]{:S(2)}) collective-permute-start(bf16[48,512]{1,0:T(8,128)(2,1)S(1)} %get-tuple-element.213), channel_id=1, source_target_pairs={{0,24},{2,26},{4,28},{6,30},{8,16},{10,18},{12,20},{14,22},{16,8},... | collective-permute-start | bytes 147464 | tf_op jit(solution)/shard_map/late_gradient_across_12/ppermute | solution.py:137
  189.4 4.2 %collective-permute-done.45.refs_7_ = bf16[48,512]{1,0:T(8,128)(2,1)S(1)} collective-permute-done((bf16[48,512]{1,0:T(8,128)(2,1)S(1)}, bf16[48,512]{1,0:T(8,128)(2,1)S(1)}, u32[]{:S(2)}, u32[]{:S(2)}) %collective-permute-start.45) | collective-permute-done | bytes 49184 | tf_op jit(solution)/shard_map/late_gradient_across_8/ppermute | solution.py:137
  193.7 1.4 gradient_totals.1
  199.1 1.9 collective-permute-start.49
  201.9 1.5 collective-permute-start.51
  204.6 2.7 %collective-permute-done.51.refs_3_ = f32[1,24,128]{2,1,0:T(8,128)S(1)} collective-permute-done((f32[1,24,128]{2,1,0:T(8,128)S(1)}, f32[1,24,128]{2,1,0:T(8,128)S(1)}, u32[]{:S(2)}, u32[]{:S(2)}) %collective-permute-start.51) | collective-permute-done | bytes 12320 | tf_op jit(solution)/shard_map/squares_across_12/ppermute | solution.py:137
  207.4 1.3 collective-permute-start.52
  209.5 1.4 collective-permute-start.54
  212.8 1.7 collective-permute-done.54.refs_6_
  215.1 4.7 %update.1 = (f32[1,1]{1,0:T(1,128)}, f32[3,48,384]{2,1,0:T(8,128)}, f32[48,384]{1,0:T(8,128)}, f32[48,1536]{1,0:T(8,128)}, f32[48,1536]{1,0:T(8,128)}, /*index=5...) custom-call(s32[1]{0:T(128)} %bitcast.refs_10_.refs_0_, ...), custom_call_target="tpu_custom_call" | custom-call | bytes 6000000 | tf_op jit(solution)/shard_map/update/pallas_call | solution.py:77
  (155 shorter events, 36.0 us)
Async XLA Ops:
  2.5 13.4 %collective-permute-start = (bf16[48,1664]{1,0:T(8,128)(2,1)}, bf16[48,1664]{1,0:T(8,128)(2,1)S(1)}, u32[]{:S(2)}, u32[]{:S(2)}) collective-permute-start(bf16[48,1664]{1,0:T(8,128)(2,1)} %pack_heads.1.refs_0_), channel_id=1, source_target_pairs={{0,16},{2,18},{4,20},{6,22},{8,24},{10,26},{12,28},{14,30},{16,0},... | collective-permute-start | bytes 479240 | tf_op jit(solution)/shard_map/heads_across_8/ppermute | solution.py:137
  6.5 9.4 %collective-permute-start.1 = (bf16[48,1664]{1,0:T(8,128)(2,1)}, bf16[48,1664]{1,0:T(8,128)(2,1)S(1)}, u32[]{:S(2)}, u32[]{:S(2)}) collective-permute-start(bf16[48,1664]{1,0:T(8,128)(2,1)} %pack_heads.1.refs_0_), channel_id=1, source_target_pairs={{0,8},{2,10},{4,12},{6,14},{8,0},{10,2},{12,4},{14,6},{16,24},{18,... | collective-permute-start | bytes 479240 | tf_op jit(solution)/shard_map/heads_across_4/ppermute | solution.py:137
  8.1 10.8 %collective-permute-start.2 = (bf16[48,1664]{1,0:T(8,128)(2,1)}, bf16[48,1664]{1,0:T(8,128)(2,1)S(1)}, u32[]{:S(2)}, u32[]{:S(2)}) collective-permute-start(bf16[48,1664]{1,0:T(8,128)(2,1)} %pack_heads.1.refs_0_), channel_id=1, source_target_pairs={{0,24},{2,26},{4,28},{6,30},{8,16},{10,18},{12,20},{14,22},{16,8},... | collective-permute-start | bytes 479240 | tf_op jit(solution)/shard_map/heads_across_12/ppermute | solution.py:137
  11.7 16.7 %copy-start.20 = (s32[2,16]{1,0:T(2,128)S(1)}, s32[2,16]{1,0:T(2,128)}, u32[]{:S(2)}) copy-start(s32[2,16]{1,0:T(2,128)} %param.29) | copy-start | bytes 388
  19.9 16.5 %collective-permute-start.3 = (bf16[192,1664]{1,0:T(8,128)(2,1)S(1)}, bf16[192,1664]{1,0:T(8,128)(2,1)S(1)}, u32[]{:S(2)}, u32[]{:S(2)}) collective-permute-start(bf16[192,1664]{1,0:T(8,128)(2,1)S(1)} %get-tuple-element.136.refs_1_.refs_10_), channel_id=1, source_target_pairs={{0,4},{2,6},{4,0},{6,2},{8,12},{10,14},{12,8},{14,10},{16,20},{18,... | collective-permute-start | bytes 1916936 | tf_op jit(solution)/shard_map/heads_across_2/ppermute | solution.py:137
  21.4 15.0 %collective-permute-start.4 = (bf16[192,1664]{1,0:T(8,128)(2,1)S(1)}, bf16[192,1664]{1,0:T(8,128)(2,1)S(1)}, u32[]{:S(2)}, u32[]{:S(2)}) collective-permute-start(bf16[192,1664]{1,0:T(8,128)(2,1)S(1)} %get-tuple-element.136.refs_1_.refs_10_), channel_id=1, source_target_pairs={{0,2},{2,0},{4,6},{6,4},{8,10},{10,8},{12,14},{14,12},{16,18},{18,... | collective-permute-start | bytes 1916936 | tf_op jit(solution)/shard_map/heads_across_1/ppermute | solution.py:137
  23.5 11.7 %collective-permute-start.5 = (bf16[48,1536]{1,0:T(8,128)(2,1)S(1)}, bf16[48,1536]{1,0:T(8,128)(2,1)}, u32[]{:S(2)}, u32[]{:S(2)}) collective-permute-start(bf16[48,1536]{1,0:T(8,128)(2,1)S(1)} %get-tuple-element.137.refs_0_), channel_id=1, source_target_pairs={{0,16},{2,18},{4,20},{6,22},{8,24},{10,26},{12,28},{14,30},{16,0},... | collective-permute-start | bytes 442376 | tf_op jit(solution)/shard_map/up_across_8/ppermute | solution.py:137
  36.1 10.3 %collective-permute-start.9 = (bf16[96,1536]{1,0:T(8,128)(2,1)S(1)}, bf16[96,1536]{1,0:T(8,128)(2,1)S(1)}, u32[]{:S(2)}, u32[]{:S(2)}) collective-permute-start(bf16[96,1536]{1,0:T(8,128)(2,1)S(1)} %join.8.refs_2_.refs_0_), channel_id=1, source_target_pairs={{0,8},{2,10},{4,12},{6,14},{8,0},{10,2},{12,4},{14,6},{16,24},{18,... | collective-permute-start | bytes 884744 | tf_op jit(solution)/shard_map/up_across_4/ppermute | solution.py:137
  36.5 12.0 %collective-permute-start.8 = (bf16[48,1536]{1,0:T(8,128)(2,1)S(1)}, bf16[48,1536]{1,0:T(8,128)(2,1)S(1)}, u32[]{:S(2)}, u32[]{:S(2)}) collective-permute-start(bf16[48,1536]{1,0:T(8,128)(2,1)S(1)} %get-tuple-element.141.refs_0_), channel_id=1, source_target_pairs={{0,16},{2,18},{4,20},{6,22},{8,24},{10,26},{12,28},{14,30},{16,0},... | collective-permute-start | bytes 442376 | tf_op jit(solution)/shard_map/down_across_8/ppermute | solution.py:137
  42.4 8.4 %collective-permute-start.6 = (bf16[96,1664]{1,0:T(8,128)(2,1)S(1)}, bf16[96,1664]{1,0:T(8,128)(2,1)S(1)}, u32[]{:S(2)}, u32[]{:S(2)}) collective-permute-start(bf16[96,1664]{1,0:T(8,128)(2,1)S(1)} %get-tuple-element.139.refs_2_), channel_id=1, source_target_pairs={{0,2},{2,0},{4,6},{6,4},{8,10},{10,8},{12,14},{14,12},{16,18},{18,... | collective-permute-start | bytes 958472 | tf_op jit(solution)/shard_map/heads_corner_across_1/ppermute | solution.py:137
  43.9 9.1 %collective-permute-start.7 = (bf16[96,1664]{1,0:T(8,128)(2,1)S(1)}, bf16[96,1664]{1,0:T(8,128)(2,1)S(1)}, u32[]{:S(2)}, u32[]{:S(2)}) collective-permute-start(bf16[96,1664]{1,0:T(8,128)(2,1)S(1)} %get-tuple-element.140), channel_id=1, source_target_pairs={{0,4},{2,6},{4,0},{6,2},{8,12},{10,14},{12,8},{14,10},{16,20},{18,... | collective-permute-start | bytes 958472 | tf_op jit(solution)/shard_map/heads_corner_across_2/ppermute | solution.py:137
  48.5 12.3 %collective-permute-start.10 = (bf16[96,1536]{1,0:T(8,128)(2,1)S(1)}, bf16[96,1536]{1,0:T(8,128)(2,1)S(1)}, u32[]{:S(2)}, u32[]{:S(2)}) collective-permute-start(bf16[96,1536]{1,0:T(8,128)(2,1)S(1)} %join.10.refs_8_.refs_0_), channel_id=1, source_target_pairs={{0,8},{2,10},{4,12},{6,14},{8,0},{10,2},{12,4},{14,6},{16,24},{18,... | collective-permute-start | bytes 884744 | tf_op jit(solution)/shard_map/down_across_4/ppermute | solution.py:137
  48.6 8.6 %copy-start.14 = (f32[2]{0:T(128)}, f32[2]{0:T(128)S(1)}, u32[]{:S(2)}) copy-start(f32[2]{0:T(128)S(1)} %pad_maximum_fusion.refs_9_.refs_1_) | copy-start | bytes 28
  48.7 16.9 %collective-permute-start.14 = (bf16[192,1536]{1,0:T(8,128)(2,1)S(1)}, bf16[192,1536]{1,0:T(8,128)(2,1)S(1)}, u32[]{:S(2)}, u32[]{:S(2)}) collective-permute-start(bf16[192,1536]{1,0:T(8,128)(2,1)S(1)} %join.9.refs_2_.refs_5_.refs_14_), channel_id=1, source_target_pairs={{0,4},{2,6},{4,0},{6,2},{8,12},{10,14},{12,8},{14,10},{16,20},{18,... | collective-permute-start | bytes 1769480 | tf_op jit(solution)/shard_map/up_across_2/ppermute | solution.py:137
  49.3 16.3 %collective-permute-start.15 = (bf16[192,1536]{1,0:T(8,128)(2,1)S(1)}, bf16[192,1536]{1,0:T(8,128)(2,1)S(1)}, u32[]{:S(2)}, u32[]{:S(2)}) collective-permute-start(bf16[192,1536]{1,0:T(8,128)(2,1)S(1)} %join.9.refs_2_.refs_5_.refs_14_), channel_id=1, source_target_pairs={{0,2},{2,0},{4,6},{6,4},{8,10},{10,8},{12,14},{14,12},{16,18},{18,... | collective-permute-start | bytes 1769480 | tf_op jit(solution)/shard_map/up_across_1/ppermute | solution.py:137
  60.9 16.1 %collective-permute-start.11 = (bf16[192,1536]{1,0:T(8,128)(2,1)S(1)}, bf16[192,1536]{1,0:T(8,128)(2,1)S(1)}, u32[]{:S(2)}, u32[]{:S(2)}) collective-permute-start(bf16[192,1536]{1,0:T(8,128)(2,1)S(1)} %join.11.refs_1_.refs_9_), channel_id=1, source_target_pairs={{0,4},{2,6},{4,0},{6,2},{8,12},{10,14},{12,8},{14,10},{16,20},{18,... | collective-permute-start | bytes 1769480 | tf_op jit(solution)/shard_map/down_across_2/ppermute | solution.py:137
  61.5 15.5 %collective-permute-start.12 = (bf16[192,1536]{1,0:T(8,128)(2,1)S(1)}, bf16[192,1536]{1,0:T(8,128)(2,1)S(1)}, u32[]{:S(2)}, u32[]{:S(2)}) collective-permute-start(bf16[192,1536]{1,0:T(8,128)(2,1)S(1)} %join.11.refs_1_.refs_9_), channel_id=1, source_target_pairs={{0,2},{2,0},{4,6},{6,4},{8,10},{10,8},{12,14},{14,12},{16,18},{18,... | collective-permute-start | bytes 1769480 | tf_op jit(solution)/shard_map/down_across_1/ppermute | solution.py:137
  78.3 10.9 %collective-permute-start.13 = (bf16[1024,768]{1,0:T(8,128)(2,1)S(1)}, bf16[1024,768]{1,0:T(8,128)(2,1)S(1)}, u32[]{:S(2)}, u32[]{:S(2)}) collective-permute-start(bf16[1024,768]{1,0:T(8,128)(2,1)S(1)} %branch.1.refs_2_), channel_id=1, source_target_pairs={{0,1},{1,0},{2,3},{3,2},{4,5},{5,4},{6,7},{7,6},{8,9},{9,8},{10,11... | collective-permute-start | bytes 4718600 | tf_op jit(solution)/shard_map/branch_other_core/ppermute | solution.py:146
  78.4 9.9 %collective-permute-start.16 = (bf16[96,1536]{1,0:T(8,128)(2,1)S(1)}, bf16[96,1536]{1,0:T(8,128)(2,1)S(1)}, u32[]{:S(2)}, u32[]{:S(2)}) collective-permute-start(bf16[96,1536]{1,0:T(8,128)(2,1)S(1)} %get-tuple-element.152), channel_id=1, source_target_pairs={{0,2},{2,0},{4,6},{6,4},{8,10},{10,8},{12,14},{14,12},{16,18},{18,... | collective-permute-start | bytes 884744 | tf_op jit(solution)/shard_map/up_corner_across_1/ppermute | solution.py:137
  79.4 9.9 %collective-permute-start.17 = (bf16[96,1536]{1,0:T(8,128)(2,1)S(1)}, bf16[96,1536]{1,0:T(8,128)(2,1)S(1)}, u32[]{:S(2)}, u32[]{:S(2)}) collective-permute-start(bf16[96,1536]{1,0:T(8,128)(2,1)S(1)} %get-tuple-element.153), channel_id=1, source_target_pairs={{0,4},{2,6},{4,0},{6,2},{8,12},{10,14},{12,8},{14,10},{16,20},{18,... | collective-permute-start | bytes 884744 | tf_op jit(solution)/shard_map/up_corner_across_2/ppermute | solution.py:137
  80.8 18.4 %collective-permute-start.18 = (bf16[96,1536]{1,0:T(8,128)(2,1)S(1)}, bf16[96,1536]{1,0:T(8,128)(2,1)S(1)}, u32[]{:S(2)}, u32[]{:S(2)}) collective-permute-start(bf16[96,1536]{1,0:T(8,128)(2,1)S(1)} %get-tuple-element.155), channel_id=1, source_target_pairs={{0,2},{2,0},{4,6},{6,4},{8,10},{10,8},{12,14},{14,12},{16,18},{18,... | collective-permute-start | bytes 884744 | tf_op jit(solution)/shard_map/down_corner_across_1/ppermute | solution.py:137
  81.2 18.0 %collective-permute-start.19 = (bf16[96,1536]{1,0:T(8,128)(2,1)S(1)}, bf16[96,1536]{1,0:T(8,128)(2,1)S(1)}, u32[]{:S(2)}, u32[]{:S(2)}) collective-permute-start(bf16[96,1536]{1,0:T(8,128)(2,1)S(1)} %get-tuple-element.156), channel_id=1, source_target_pairs={{0,4},{2,6},{4,0},{6,2},{8,12},{10,14},{12,8},{14,10},{16,20},{18,... | collective-permute-start | bytes 884744 | tf_op jit(solution)/shard_map/down_corner_across_2/ppermute | solution.py:137
  99.9 1.2 collective-permute-start.20
  101.9 4.7 %collective-permute-start.21 = (f32[1,8,768]{2,1,0:T(8,128)S(1)}, f32[1,8,768]{2,1,0:T(8,128)S(1)}, u32[]{:S(2)}, u32[]{:S(2)}) collective-permute-start(f32[1,8,768]{2,1,0:T(8,128)S(1)} %bitcast.82), channel_id=1, source_target_pairs={{0,16},{2,18},{4,20},{6,22},{8,24},{10,26},{12,28},{14,30},{16,0},... | collective-permute-start | bytes 73736 | tf_op jit(solution)/shard_map/small_sums_across_8/ppermute | solution.py:137
  101.9 4.7 %collective-permute-start.22 = (f32[1,8,768]{2,1,0:T(8,128)S(1)}, f32[1,8,768]{2,1,0:T(8,128)S(1)}, u32[]{:S(2)}, u32[]{:S(2)}) collective-permute-start(f32[1,8,768]{2,1,0:T(8,128)S(1)} %bitcast.83), channel_id=1, source_target_pairs={{0,8},{2,10},{4,12},{6,14},{8,0},{10,2},{12,4},{14,6},{16,24},{18,... | collective-permute-start | bytes 73736 | tf_op jit(solution)/shard_map/small_sums_across_4/ppermute | solution.py:137
  103.7 5.6 %collective-permute-start.23 = (f32[1,8,768]{2,1,0:T(8,128)S(1)}, f32[1,8,768]{2,1,0:T(8,128)S(1)}, u32[]{:S(2)}, u32[]{:S(2)}) collective-permute-start(f32[1,8,768]{2,1,0:T(8,128)S(1)} %bitcast.84), channel_id=1, source_target_pairs={{0,24},{2,26},{4,28},{6,30},{8,16},{10,18},{12,20},{14,22},{16,8},... | collective-permute-start | bytes 73736 | tf_op jit(solution)/shard_map/small_sums_across_12/ppermute | solution.py:137
  109.3 5.7 %collective-permute-start.24 = (f32[4,8,768]{2,1,0:T(8,128)S(1)}, f32[4,8,768]{2,1,0:T(8,128)S(1)}, u32[]{:S(2)}, u32[]{:S(2)}) collective-permute-start(f32[4,8,768]{2,1,0:T(8,128)S(1)} %join.12.refs_5_.refs_0_), channel_id=1, source_target_pairs={{0,4},{2,6},{4,0},{6,2},{8,12},{10,14},{12,8},{14,10},{16,20},{18,... | collective-permute-start | bytes 294920 | tf_op jit(solution)/shard_map/small_sums_across_2/ppermute | solution.py:137
  110.7 4.6 %collective-permute-start.25 = (f32[4,8,768]{2,1,0:T(8,128)S(1)}, f32[4,8,768]{2,1,0:T(8,128)S(1)}, u32[]{:S(2)}, u32[]{:S(2)}) collective-permute-start(f32[4,8,768]{2,1,0:T(8,128)S(1)} %join.12.refs_5_.refs_0_), channel_id=1, source_target_pairs={{0,2},{2,0},{4,6},{6,4},{8,10},{10,8},{12,14},{14,12},{16,18},{18,... | collective-permute-start | bytes 294920 | tf_op jit(solution)/shard_map/small_sums_across_1/ppermute | solution.py:137
  111.6 5.5 %collective-permute-start.26 = (f32[4,8,768]{2,1,0:T(8,128)S(1)}, f32[4,8,768]{2,1,0:T(8,128)S(1)}, u32[]{:S(2)}, u32[]{:S(2)}) collective-permute-start(f32[4,8,768]{2,1,0:T(8,128)S(1)} %join.12.refs_5_.refs_0_), channel_id=1, source_target_pairs={{0,6},{2,4},{4,2},{6,0},{8,14},{10,12},{12,10},{14,8},{16,22},{18,... | collective-permute-start | bytes 294920 | tf_op jit(solution)/shard_map/small_sums_across_3/ppermute | solution.py:137
  117.2 4.3 %copy-start.16 = (bf16[1024,128]{1,0:T(8,128)(2,1)S(1)}, bf16[1024,128]{1,0:T(8,128)(2,1)}, u32[]{:S(2)}) copy-start(bf16[1024,128]{1,0:T(8,128)(2,1)} %get-tuple-element.291) | copy-start | bytes 786436
  121.4 6.0 %collective-permute-start.27 = (bf16[1024,768]{1,0:T(8,128)(2,1)S(1)}, bf16[1024,768]{1,0:T(8,128)(2,1)S(1)}, u32[]{:S(2)}, u32[]{:S(2)}) collective-permute-start(bf16[1024,768]{1,0:T(8,128)(2,1)S(1)} %get-tuple-element.160.refs_4_), channel_id=1, source_target_pairs={{0,1},{1,0},{2,3},{3,2},{4,5},{5,4},{6,7},{7,6},{8,9},{9,8},{10,11... | collective-permute-start | bytes 4718600 | tf_op jit(solution)/shard_map/second_gradient_other_core/ppermute | solution.py:146
  125.4 9.5 %collective-permute-start.30 = (bf16[96,1536]{1,0:T(8,128)(2,1)S(1)}, bf16[96,1536]{1,0:T(8,128)(2,1)S(1)}, u32[]{:S(2)}, u32[]{:S(2)}) collective-permute-start(bf16[96,1536]{1,0:T(8,128)(2,1)S(1)} %get-tuple-element.184), channel_id=1, source_target_pairs={{0,2},{2,0},{4,6},{6,4},{8,10},{10,8},{12,14},{14,12},{16,18},{18,... | collective-permute-start | bytes 884744 | tf_op jit(solution)/shard_map/up_gradient_across_1/ppermute | solution.py:137
  126.6 9.1 %collective-permute-start.31 = (bf16[96,1536]{1,0:T(8,128)(2,1)S(1)}, bf16[96,1536]{1,0:T(8,128)(2,1)S(1)}, u32[]{:S(2)}, u32[]{:S(2)}) collective-permute-start(bf16[96,1536]{1,0:T(8,128)(2,1)S(1)} %get-tuple-element.185), channel_id=1, source_target_pairs={{0,4},{2,6},{4,0},{6,2},{8,12},{10,14},{12,8},{14,10},{16,20},{18,... | collective-permute-start | bytes 884744 | tf_op jit(solution)/shard_map/up_gradient_across_2/ppermute | solution.py:137
  135.9 16.8 %collective-permute-start.32 = (bf16[192,1536]{1,0:T(8,128)(2,1)S(1)}, bf16[192,1536]{1,0:T(8,128)(2,1)S(1)}, u32[]{:S(2)}, u32[]{:S(2)}) collective-permute-start(bf16[192,1536]{1,0:T(8,128)(2,1)S(1)} %get-tuple-element.186), channel_id=1, source_target_pairs={{0,4},{2,6},{4,0},{6,2},{8,12},{10,14},{12,8},{14,10},{16,20},{18,... | collective-permute-start | bytes 1769480 | tf_op jit(solution)/shard_map/up_gradient_across_2/ppermute | solution.py:137
  136.7 16.0 %collective-permute-start.33 = (bf16[192,1536]{1,0:T(8,128)(2,1)S(1)}, bf16[192,1536]{1,0:T(8,128)(2,1)S(1)}, u32[]{:S(2)}, u32[]{:S(2)}) collective-permute-start(bf16[192,1536]{1,0:T(8,128)(2,1)S(1)} %get-tuple-element.187), channel_id=1, source_target_pairs={{0,2},{2,0},{4,6},{6,4},{8,10},{10,8},{12,14},{14,12},{16,18},{18,... | collective-permute-start | bytes 1769480 | tf_op jit(solution)/shard_map/up_gradient_across_1/ppermute | solution.py:137
  150.2 9.1 %collective-permute-start.28 = (bf16[96,1152]{1,0:T(8,128)(2,1)S(1)}, bf16[96,1152]{1,0:T(8,128)(2,1)S(1)}, u32[]{:S(2)}, u32[]{:S(2)}) collective-permute-start(bf16[96,1152]{1,0:T(8,128)(2,1)S(1)} %get-tuple-element.174), channel_id=1, source_target_pairs={{0,2},{2,0},{4,6},{6,4},{8,10},{10,8},{12,14},{14,12},{16,18},{18,... | collective-permute-start | bytes 663560 | tf_op jit(solution)/shard_map/early_gradient_across_1/ppermute | solution.py:137
  151.4 7.9 %collective-permute-start.29 = (bf16[96,1152]{1,0:T(8,128)(2,1)S(1)}, bf16[96,1152]{1,0:T(8,128)(2,1)S(1)}, u32[]{:S(2)}, u32[]{:S(2)}) collective-permute-start(bf16[96,1152]{1,0:T(8,128)(2,1)S(1)} %get-tuple-element.175), channel_id=1, source_target_pairs={{0,4},{2,6},{4,0},{6,2},{8,12},{10,14},{12,8},{14,10},{16,20},{18,... | collective-permute-start | bytes 663560 | tf_op jit(solution)/shard_map/early_gradient_across_2/ppermute | solution.py:137
  152.9 10.6 %collective-permute-start.38 = (bf16[96,1536]{1,0:T(8,128)(2,1)S(1)}, bf16[96,1536]{1,0:T(8,128)(2,1)S(1)}, u32[]{:S(2)}, u32[]{:S(2)}) collective-permute-start(bf16[96,1536]{1,0:T(8,128)(2,1)S(1)} %get-tuple-element.188.refs_9_), channel_id=1, source_target_pairs={{0,8},{2,10},{4,12},{6,14},{8,0},{10,2},{12,4},{14,6},{16,24},{18,... | collective-permute-start | bytes 884744 | tf_op jit(solution)/shard_map/up_gradient_across_4/ppermute | solution.py:137
  159.4 12.9 %collective-permute-start.34 = (bf16[192,1152]{1,0:T(8,128)(2,1)S(1)}, bf16[192,1152]{1,0:T(8,128)(2,1)S(1)}, u32[]{:S(2)}, u32[]{:S(2)}) collective-permute-start(bf16[192,1152]{1,0:T(8,128)(2,1)S(1)} %get-tuple-element.190.refs_3_), channel_id=1, source_target_pairs={{0,4},{2,6},{4,0},{6,2},{8,12},{10,14},{12,8},{14,10},{16,20},{18,... | collective-permute-start | bytes 1327112 | tf_op jit(solution)/shard_map/early_gradient_across_2/ppermute | solution.py:137
  160.2 12.2 %collective-permute-start.35 = (bf16[192,1152]{1,0:T(8,128)(2,1)S(1)}, bf16[192,1152]{1,0:T(8,128)(2,1)S(1)}, u32[]{:S(2)}, u32[]{:S(2)}) collective-permute-start(bf16[192,1152]{1,0:T(8,128)(2,1)S(1)} %get-tuple-element.191.refs_4_), channel_id=1, source_target_pairs={{0,2},{2,0},{4,6},{6,4},{8,10},{10,8},{12,14},{14,12},{16,18},{18,... | collective-permute-start | bytes 1327112 | tf_op jit(solution)/shard_map/early_gradient_across_1/ppermute | solution.py:137
  161.1 11.2 %collective-permute-start.36 = (bf16[96,512]{1,0:T(8,128)(2,1)S(1)}, bf16[96,512]{1,0:T(8,128)(2,1)S(1)}, u32[]{:S(2)}, u32[]{:S(2)}) collective-permute-start(bf16[96,512]{1,0:T(8,128)(2,1)S(1)} %get-tuple-element.194), channel_id=1, source_target_pairs={{0,2},{2,0},{4,6},{6,4},{8,10},{10,8},{12,14},{14,12},{16,18},{18,... | collective-permute-start | bytes 294920 | tf_op jit(solution)/shard_map/late_gradient_across_1/ppermute | solution.py:137
  162.2 10.1 %collective-permute-start.37 = (bf16[96,512]{1,0:T(8,128)(2,1)S(1)}, bf16[96,512]{1,0:T(8,128)(2,1)S(1)}, u32[]{:S(2)}, u32[]{:S(2)}) collective-permute-start(bf16[96,512]{1,0:T(8,128)(2,1)S(1)} %get-tuple-element.195), channel_id=1, source_target_pairs={{0,4},{2,6},{4,0},{6,2},{8,12},{10,14},{12,8},{14,10},{16,20},{18,... | collective-permute-start | bytes 294920 | tf_op jit(solution)/shard_map/late_gradient_across_2/ppermute | solution.py:137
  163.6 8.7 %collective-permute-start.39 = (bf16[48,1536]{1,0:T(8,128)(2,1)S(1)}, bf16[48,1536]{1,0:T(8,128)(2,1)S(1)}, u32[]{:S(2)}, u32[]{:S(2)}) collective-permute-start(bf16[48,1536]{1,0:T(8,128)(2,1)S(1)} %get-tuple-element.197), channel_id=1, source_target_pairs={{0,16},{2,18},{4,20},{6,22},{8,24},{10,26},{12,28},{14,30},{16,0},... | collective-permute-start | bytes 442376 | tf_op jit(solution)/shard_map/up_gradient_across_8/ppermute | solution.py:137
  172.4 4.3 %collective-permute-start.41 = (bf16[1024,768]{1,0:T(8,128)(2,1)S(1)}, bf16[1024,768]{1,0:T(8,128)(2,1)S(1)}, u32[]{:S(2)}, u32[]{:S(2)}) collective-permute-start(bf16[1024,768]{1,0:T(8,128)(2,1)S(1)} %get-tuple-element.205.refs_1_), channel_id=1, source_target_pairs={{0,1},{1,0},{2,3},{3,2},{4,5},{5,4},{6,7},{7,6},{8,9},{9,8},{10,11... | collective-permute-start | bytes 4718600 | tf_op jit(solution)/shard_map/first_gradient_other_core/ppermute | solution.py:146
  172.5 12.4 %collective-permute-start.43 = (bf16[192,512]{1,0:T(8,128)(2,1)S(1)}, bf16[192,512]{1,0:T(8,128)(2,1)S(1)}, u32[]{:S(2)}, u32[]{:S(2)}) collective-permute-start(bf16[192,512]{1,0:T(8,128)(2,1)S(1)} %get-tuple-element.200.refs_3_), channel_id=1, source_target_pairs={{0,4},{2,6},{4,0},{6,2},{8,12},{10,14},{12,8},{14,10},{16,20},{18,... | collective-permute-start | bytes 589832 | tf_op jit(solution)/shard_map/late_gradient_across_2/ppermute | solution.py:137
  173.9 11.0 %collective-permute-start.44 = (bf16[192,512]{1,0:T(8,128)(2,1)S(1)}, bf16[192,512]{1,0:T(8,128)(2,1)S(1)}, u32[]{:S(2)}, u32[]{:S(2)}) collective-permute-start(bf16[192,512]{1,0:T(8,128)(2,1)S(1)} %get-tuple-element.201.refs_4_), channel_id=1, source_target_pairs={{0,2},{2,0},{4,6},{6,4},{8,10},{10,8},{12,14},{14,12},{16,18},{18,... | collective-permute-start | bytes 589832 | tf_op jit(solution)/shard_map/late_gradient_across_1/ppermute | solution.py:137
  174.9 7.3 %collective-permute-start.40 = (bf16[96,1152]{1,0:T(8,128)(2,1)S(1)}, bf16[96,1152]{1,0:T(8,128)(2,1)S(1)}, u32[]{:S(2)}, u32[]{:S(2)}) collective-permute-start(bf16[96,1152]{1,0:T(8,128)(2,1)S(1)} %get-tuple-element.203.refs_6_), channel_id=1, source_target_pairs={{0,8},{2,10},{4,12},{6,14},{8,0},{10,2},{12,4},{14,6},{16,24},{18,... | collective-permute-start | bytes 663560 | tf_op jit(solution)/shard_map/early_gradient_across_4/ppermute | solution.py:137
  176.7 16.9 %copy-start.10 = (f32[48,3]{0,1:T(4,128)S(1)}, f32[48,3]{0,1:T(4,128)}, u32[]{:S(2)}) copy-start(f32[48,3]{0,1:T(4,128)} %param.36) | copy-start | bytes 1732
  176.7 16.9 %copy-start.12 = (f32[48,2]{0,1:T(2,128)S(1)}, f32[48,2]{0,1:T(2,128)}, u32[]{:S(2)}) copy-start(f32[48,2]{0,1:T(2,128)} %param.37) | copy-start | bytes 1156
  182.0 11.7 %copy-start.1 = (f32[48,1536]{1,0:T(8,128)S(1)}, f32[48,1536]{1,0:T(8,128)}, u32[]{:S(2)}) copy-start(f32[48,1536]{1,0:T(8,128)} %refs_13_.1) | copy-start | bytes 884740
  182.0 11.7 %copy-start.2 = (f32[48,3,384]{2,0,1:T(8,128)S(1)}, f32[48,3,384]{2,0,1:T(8,128)}, u32[]{:S(2)}) copy-start(f32[48,3,384]{2,0,1:T(8,128)} %param.32) | copy-start | bytes 663556
  182.3 11.4 %collective-permute-start.42 = (bf16[48,1152]{1,0:T(8,128)(2,1)S(1)}, bf16[48,1152]{1,0:T(8,128)(2,1)S(1)}, u32[]{:S(2)}, u32[]{:S(2)}) collective-permute-start(bf16[48,1152]{1,0:T(8,128)(2,1)S(1)} %get-tuple-element.208), channel_id=1, source_target_pairs={{0,16},{2,18},{4,20},{6,22},{8,24},{10,26},{12,28},{14,30},{16,0},... | collective-permute-start | bytes 331784 | tf_op jit(solution)/shard_map/early_gradient_across_8/ppermute | solution.py:137
  185.0 8.7 %collective-permute-start.45 = (bf16[48,512]{1,0:T(8,128)(2,1)S(1)}, bf16[48,512]{1,0:T(8,128)(2,1)S(1)}, u32[]{:S(2)}, u32[]{:S(2)}) collective-permute-start(bf16[48,512]{1,0:T(8,128)(2,1)S(1)} %get-tuple-element.211), channel_id=1, source_target_pairs={{0,16},{2,18},{4,20},{6,22},{8,24},{10,26},{12,28},{14,30},{16,0},... | collective-permute-start | bytes 147464 | tf_op jit(solution)/shard_map/late_gradient_across_8/ppermute | solution.py:137
  185.4 8.2 %collective-permute-start.46 = (bf16[48,512]{1,0:T(8,128)(2,1)S(1)}, bf16[48,512]{1,0:T(8,128)(2,1)S(1)}, u32[]{:S(2)}, u32[]{:S(2)}) collective-permute-start(bf16[48,512]{1,0:T(8,128)(2,1)S(1)} %get-tuple-element.212), channel_id=1, source_target_pairs={{0,8},{2,10},{4,12},{6,14},{8,0},{10,2},{12,4},{14,6},{16,24},{18,... | collective-permute-start | bytes 147464 | tf_op jit(solution)/shard_map/late_gradient_across_4/ppermute | solution.py:137
  187.2 6.5 %collective-permute-start.47 = (bf16[48,512]{1,0:T(8,128)(2,1)S(1)}, bf16[48,512]{1,0:T(8,128)(2,1)S(1)}, u32[]{:S(2)}, u32[]{:S(2)}) collective-permute-start(bf16[48,512]{1,0:T(8,128)(2,1)S(1)} %get-tuple-element.213), channel_id=1, source_target_pairs={{0,24},{2,26},{4,28},{6,30},{8,16},{10,18},{12,20},{14,22},{16,8},... | collective-permute-start | bytes 147464 | tf_op jit(solution)/shard_map/late_gradient_across_12/ppermute | solution.py:137
  197.2 17.3 %copy-start.9 = (f32[48,384]{1,0:T(8,128)}, f32[48,384]{1,0:T(8,128)S(1)}, u32[]{:S(2)}) copy-start(f32[48,384]{1,0:T(8,128)S(1)} %get-tuple-element.219.refs_8_) | copy-start | bytes 221188
  197.2 1.2 collective-permute-start.48
  199.1 4.6 %collective-permute-start.49 = (f32[1,24,128]{2,1,0:T(8,128)S(1)}, f32[1,24,128]{2,1,0:T(8,128)S(1)}, u32[]{:S(2)}, u32[]{:S(2)}) collective-permute-start(f32[1,24,128]{2,1,0:T(8,128)S(1)} %bitcast.96), channel_id=1, source_target_pairs={{0,16},{2,18},{4,20},{6,22},{8,24},{10,26},{12,28},{14,30},{16,0},... | collective-permute-start | bytes 36872 | tf_op jit(solution)/shard_map/squares_across_8/ppermute | solution.py:137
  201.0 3.7 %collective-permute-start.50 = (f32[1,24,128]{2,1,0:T(8,128)S(1)}, f32[1,24,128]{2,1,0:T(8,128)S(1)}, u32[]{:S(2)}, u32[]{:S(2)}) collective-permute-start(f32[1,24,128]{2,1,0:T(8,128)S(1)} %bitcast.97), channel_id=1, source_target_pairs={{0,8},{2,10},{4,12},{6,14},{8,0},{10,2},{12,4},{14,6},{16,24},{18,... | collective-permute-start | bytes 36872 | tf_op jit(solution)/shard_map/squares_across_4/ppermute | solution.py:137
  201.9 5.5 %collective-permute-start.51 = (f32[1,24,128]{2,1,0:T(8,128)S(1)}, f32[1,24,128]{2,1,0:T(8,128)S(1)}, u32[]{:S(2)}, u32[]{:S(2)}) collective-permute-start(f32[1,24,128]{2,1,0:T(8,128)S(1)} %bitcast.98), channel_id=1, source_target_pairs={{0,24},{2,26},{4,28},{6,30},{8,16},{10,18},{12,20},{14,22},{16,8},... | collective-permute-start | bytes 36872 | tf_op jit(solution)/shard_map/squares_across_12/ppermute | solution.py:137
  207.4 7.1 %copy-start.8 = (f32[4,24,128]{2,1,0:T(8,128)}, f32[4,24,128]{2,1,0:T(8,128)S(1)}, u32[]{:S(2)}) copy-start(f32[4,24,128]{2,1,0:T(8,128)S(1)} %join.13.refs_3_) | copy-start | bytes 147460
  207.4 4.6 %collective-permute-start.52 = (f32[4,24,128]{2,1,0:T(8,128)S(1)}, f32[4,24,128]{2,1,0:T(8,128)S(1)}, u32[]{:S(2)}, u32[]{:S(2)}) collective-permute-start(f32[4,24,128]{2,1,0:T(8,128)S(1)} %join.13.refs_3_), channel_id=1, source_target_pairs={{0,4},{2,6},{4,0},{6,2},{8,12},{10,14},{12,8},{14,10},{16,20},{18,... | collective-permute-start | bytes 147464 | tf_op jit(solution)/shard_map/squares_across_2/ppermute | solution.py:137
  208.7 4.1 %collective-permute-start.53 = (f32[4,24,128]{2,1,0:T(8,128)S(1)}, f32[4,24,128]{2,1,0:T(8,128)S(1)}, u32[]{:S(2)}, u32[]{:S(2)}) collective-permute-start(f32[4,24,128]{2,1,0:T(8,128)S(1)} %join.13.refs_3_), channel_id=1, source_target_pairs={{0,2},{2,0},{4,6},{6,4},{8,10},{10,8},{12,14},{14,12},{16,18},{18,... | collective-permute-start | bytes 147464 | tf_op jit(solution)/shard_map/squares_across_1/ppermute | solution.py:137
  209.5 5.0 %collective-permute-start.54 = (f32[4,24,128]{2,1,0:T(8,128)S(1)}, f32[4,24,128]{2,1,0:T(8,128)S(1)}, u32[]{:S(2)}, u32[]{:S(2)}) collective-permute-start(f32[4,24,128]{2,1,0:T(8,128)S(1)} %join.13.refs_3_), channel_id=1, source_target_pairs={{0,6},{2,4},{4,2},{6,0},{8,14},{10,12},{12,10},{14,8},{16,22},{18,... | collective-permute-start | bytes 147464 | tf_op jit(solution)/shard_map/squares_across_3/ppermute | solution.py:137
  (12 other events, 16.1 us)
